TPU v7x, 512 devices: a whole 4x4x16 slice. The times are simulated.
512 devices in a mesh: wide: 128 (over x, z, core), narrow: 4 (over y).
Axes of the slice: x: 4, y: 4, z: 16, core: 2. Of those that a mesh axis runs over, the one named last changes fastest.
Arguments:
- restart: float32 [65536, 1024], P('wide', 'narrow'), may hold values from -0.09 to 0.09
- slab_slot: int32 [16384], P('wide'), may hold values from 0 to 16383, as said below
- block_cols: int32 [1024, 16], replicated, may hold values from 0 to 1023, as said below
- filter_cols: int32 [1024, 16], replicated, may hold values from 0 to 1023, as said below
Outputs:
- squared: float32 [65536, 1024], P('wide', 'narrow')
- updated: float32 [65536, 1024], P('wide', 'narrow')
Inputs may be any that keep to these rules, and one draw needn't show every extreme that they name: `slab_slot`: A permutation of all slabs; each aligned block of 128 entries names exactly 128 // 128 slabs of each aligned range of 128 values. `block_cols`: each row i holds 16 distinct block columns c with (c - i) mod 1024 within 8 of 0 either way, i itself among them. `filter_cols`: each row i holds 16 distinct block columns c with (c - i) mod 1024 within 8 of 0 either way, i itself among them.
All inputs are finite; a program needn't handle non-finite values.
Results may differ from a plain program's by a relative error of at most 0.0003.
Values sent between devices are 32-bit elements; how exact they have to be, the bound alone decides.
No kernel may reach another device: no remote copies, remote signals or barrier semaphores. Data moves between devices by JAX's collectives and lax.ppermute only.
A program may use at most 192 MiB of HBM per device.

v0:
```python
import jax
import jax.numpy as jnp
from jax import lax
from jax.sharding import PartitionSpec as P

BLOCK = 64
KNZ = 16
JNZ = 16
SLAB = 4


def with_halo(block, sides, width):
    for axis, dim in sides:
        count = lax.axis_size(axis)
        forward = [(i, i + 1) for i in range(count - 1)]
        forward.append((count - 1, 0))
        backward = [(target, source) for source, target in forward]
        low = lax.ppermute(
            lax.slice_in_dim(block, block.shape[dim] - width, None, axis=dim), axis, forward
        )
        high = lax.ppermute(lax.slice_in_dim(block, 0, width, axis=dim), axis, backward)
        block = jnp.concatenate([low, block, high], axis=dim)
    return block


def multiply(left_rows, left_cols, right_rows, right_cols, out_cols, first_row, total_rows):
    own_rows = left_cols.shape[0]
    width_left = left_cols.shape[1]
    width_right = right_cols.shape[1]
    nearby = (left_cols - first_row + own_rows) % total_rows
    picked = right_cols[nearby]
    matches = picked[:, :, :, None] == out_cols[:, None, None, :]
    found = jnp.any(matches, axis=2)
    slot = jnp.argmax(matches, axis=2)
    right_blocks = right_rows.reshape(3 * own_rows, BLOCK, width_right, BLOCK)
    chosen = right_blocks[nearby[:, :, None], :, slot]
    chosen = jnp.where(found[:, :, :, None, None], chosen, 0.0)
    left_blocks = left_rows.reshape(own_rows, BLOCK, width_left, BLOCK)
    result = jnp.einsum("iakc,ikjcb->iajb", left_blocks, chosen, precision=lax.Precision.HIGHEST)
    return result.reshape(own_rows * BLOCK, -1)


def local(restart, slab_slot, block_cols, filter_cols):
    wide_count = lax.axis_size("wide")
    layer_count = lax.axis_size("narrow")
    wide_index = lax.axis_index("wide")
    layer_index = lax.axis_index("narrow")
    rows_dev = restart.shape[0]
    own_rows = rows_dev // BLOCK
    total_rows = own_rows * wide_count
    first_row = wide_index * own_rows
    pieces = restart.reshape(-1, SLAB, restart.shape[1])
    per_device = pieces.shape[0]
    target = slab_slot // per_device
    position = slab_slot % per_device
    ordering = jnp.argsort(target * per_device + position)
    arrived, arrived_position = (
        lax.all_to_all(pieces[ordering], "wide", split_axis=0, concat_axis=0, tiled=True),
        lax.all_to_all(position[ordering], "wide", split_axis=0, concat_axis=0, tiled=True),
    )
    regrouped = arrived[jnp.argsort(arrived_position)].reshape(rows_dev, restart.shape[1])
    full_own = lax.all_gather(regrouped, "narrow", axis=1, tiled=True)
    beside_all = (first_row - own_rows + jnp.arange(3 * own_rows, dtype=jnp.int32)) % total_rows
    near_cols = block_cols[beside_all]
    near_filter = filter_cols[beside_all]
    own_cols = lax.dynamic_slice_in_dim(block_cols, first_row, own_rows, 0)
    own_filter = lax.dynamic_slice_in_dim(filter_cols, first_row, own_rows, 0)
    part_blocks = KNZ // layer_count
    part_out = JNZ // layer_count
    own_cols_part = lax.dynamic_slice_in_dim(own_cols, layer_index * part_blocks, part_blocks, 1)
    own_filter_part = lax.dynamic_slice_in_dim(own_filter, layer_index * part_out, part_out, 1)
    right_rows = with_halo(full_own, (("wide", 0),), rows_dev)
    square_terms = multiply(
        regrouped, own_cols_part, right_rows, near_cols, own_filter, first_row, total_rows
    )
    squared = lax.psum_scatter(square_terms, "narrow", scatter_dimension=1, tiled=True)
    square_full = lax.all_gather(squared, "narrow", axis=1, tiled=True)
    right_square = with_halo(square_full, (("wide", 0),), rows_dev)
    cubic_terms = multiply(
        regrouped, own_cols_part, right_square, near_filter, own_filter, first_row, total_rows
    )
    cubic = lax.psum_scatter(cubic_terms, "narrow", scatter_dimension=1, tiled=True)
    keep_match = own_cols[:, :, None] == own_filter_part[:, None, :]
    keep_found = jnp.any(keep_match, axis=1)
    keep_slot = jnp.argmax(keep_match, axis=1)
    own_blocks = full_own.reshape(own_rows, BLOCK, KNZ, BLOCK)
    row_pick = jnp.arange(own_rows, dtype=jnp.int32)[:, None]
    kept_blocks = own_blocks[row_pick, :, keep_slot]
    kept_blocks = jnp.where(keep_found[:, :, None, None], kept_blocks, 0.0)
    kept_blocks = jnp.transpose(kept_blocks, (0, 2, 1, 3)).reshape(rows_dev, -1)
    updated = 1.5 * kept_blocks - 0.5 * cubic
    return (squared, updated)


def solution(mesh):
    placed = (P("wide", "narrow"), P("wide"), P(), P())
    return jax.shard_map(
        local,
        mesh=mesh,
        in_specs=placed,
        out_specs=(P("wide", "narrow"), P("wide", "narrow")),
        check_vma=False,
    )
```

profile of v0, /device:TPU:1, one launch (start us, length us, event | category | flops | bytes accessed | tf_op | source)
XLA Modules:
  0.0 445.7 jit_solution(10762147398343984828)
XLA Ops:
  12.4 20.4 %all-to-all-start.1 = ((s32[128,1,1]{2,1,0:T(1,128)}), s32[128,1,1]{2,1,0:T(1,128)S(1)}, u32[]{:S(2)}, u32[]{:S(2)}) async-start(s32[128,1,1]{2,1,0:T(1,128)} %copy.133), calls=%async_computation.1 | async-start | bytes 131072 | tf_op jit(solution)/shard_map/all_to_all | solution.py:59
  35.7 12.1 %all-to-all-done.1 = s32[128,1,1]{2,1,0:T(1,128)S(1)} async-done(((s32[128,1,1]{2,1,0:T(1,128)}), s32[128,1,1]{2,1,0:T(1,128)S(1)}, u32[]{:S(2)}, u32[]{:S(2)}) %all-to-all-start.1) | async-done | bytes 544 | tf_op jit(solution)/shard_map/all_to_all | solution.py:59
  47.8 6.6 %all-to-all-start = ((f32[128,4,256]{2,1,0:T(4,128)}), f32[128,4,256]{2,1,0:T(4,128)S(1)}, u32[]{:S(2)}, u32[]{:S(2)}) async-start(f32[128,4,256]{2,1,0:T(4,128)} %gather_fusion), calls=%async_computation | async-start | bytes 1048576 | tf_op jit(solution)/shard_map/all_to_all | solution.py:58
  56.8 2.5 sort.32
  59.3 28.4 %all-to-all-done = f32[128,4,256]{2,1,0:T(4,128)S(1)} async-done(((f32[128,4,256]{2,1,0:T(4,128)}), f32[128,4,256]{2,1,0:T(4,128)S(1)}, u32[]{:S(2)}, u32[]{:S(2)}) %all-to-all-start) | async-done | bytes 524320 | tf_op jit(solution)/shard_map/all_to_all | solution.py:58
  89.6 30.7 %all-gather.3.cloned.1.call-done = f32[512,1024]{1,0:T(8,128)} async-done(((f32[512,256]{1,0:T(8,128)}), f32[512,1024]{1,0:T(8,128)}) %all-gather.3.cloned.1.call-update) | async-done | bytes 2097168 | tf_op jit(solution)/shard_map/all_gather | solution.py:62
  120.3 2.6 collective-permute-start.1
  122.9 3.1 collective-permute-start
  132.1 16.3 %collective-permute-done.1 = f32[512,1024]{1,0:T(8,128)} collective-permute-done((f32[512,1024]{1,0:T(8,128)}, f32[512,1024]{1,0:T(8,128)}, u32[]{:S(2)}, u32[]{:S(2)}) %collective-permute-start.1) | collective-permute-done | bytes 2097184 | tf_op jit(solution)/shard_map/ppermute | solution.py:21
  149.3 6.6 %pad_maximum_fusion = f32[1536,1024]{1,0:T(8,128)} fusion(f32[512,1024]{1,0:T(8,128)} %collective-permute-done.1, f32[512,1024]{1,0:T(8,128)} %all-gather.3.cloned.1.call-done, f32[512,1024]{1,0:T(8,128)} %collective-permute-done), kind=kLoop, calls=%fused_computation.16 | loop fusion | flops 3145728 | bytes 12582912 | tf_op jit(solution)/shard_map/concatenate | solution.py:22
  155.9 10.6 %reshape.98 = f32[24,64,16,64]{3,2,1,0:T(8,128)} reshape(f32[1536,1024]{1,0:T(8,128)} %pad_maximum_fusion) | data formatting | bytes 12582912 | tf_op jit(solution)/shard_map/reshape | solution.py:35
  166.5 13.9 %copy.138 = f32[24,64,16,64]{3,1,2,0:T(8,128)} copy(f32[24,64,16,64]{3,2,1,0:T(8,128)} %reshape.98) | data formatting | bytes 12582912 | tf_op jit(solution)/shard_map/reshape | solution.py:35
  180.4 14.4 %gather_fusion.5 = f32[512,64,64]{2,1,0:T(8,128)} fusion(f32[24,64,16,64]{3,1,2,0:T(8,128)} %copy.138, s32[512]{0:T(512)S(1)} %reshape.143), kind=kCustom, calls=%fused_computation.5 | custom fusion | bytes 16781312 | tf_op jit(solution)/shard_map/gather | solution.py:36
  194.8 13.6 %fusion.4 = f32[8,64,16,64]{3,1,2,0:T(8,128)S(1)} fusion(f32[8,64,4,64,1]{3,2,1,0,4:T(4,128)S(1)} %bitcast.48, f32[8,4,16,64,64]{4,3,2,1,0:T(8,128)} %bitcast.47, pred[8,4,16]{2,1,0:T(4,128)(4,1)S(1)} %get-tuple-element.21), kind=kOutput, calls=%fused_computation.18 | convolution fusion | flops 1612709888 | bytes 11010560 | tf_op jit(solution)/shard_map/iakc,ikjcb->iajb/dot_general | solution.py:39
  208.4 4.3 copy.141
  212.7 4.9 %reshape.99 = f32[512,1024]{1,0:T(8,128)} reshape(f32[8,64,16,64]{3,2,1,0:T(8,128)} %copy.141) | data formatting | bytes 4194304 | tf_op jit(solution)/shard_map/reshape | solution.py:40
  217.7 39.5 %reduce-scatter.3.cloned.1.call-done = f32[512,256]{1,0:T(8,128)} async-done(((f32[512,1024]{1,0:T(8,128)}), f32[512,256]{1,0:T(8,128)}) %reduce-scatter.3.cloned.1.call-update) | async-done | bytes 524304 | tf_op jit(solution)/shard_map/reduce_scatter | solution.py:76
  257.2 41.1 %all-gather.5.cloned.1.call-done = f32[512,1024]{1,0:T(8,128)} async-done(((f32[512,256]{1,0:T(8,128)}), f32[512,1024]{1,0:T(8,128)}) %all-gather.5.cloned.1.call-update) | async-done | bytes 2097168 | tf_op jit(solution)/shard_map/all_gather | solution.py:77
  298.3 2.8 collective-permute-start.3
  301.1 3.1 collective-permute-start.2
  304.3 22.1 %collective-permute-done.3 = f32[512,1024]{1,0:T(8,128)S(1)} collective-permute-done((f32[512,1024]{1,0:T(8,128)}, f32[512,1024]{1,0:T(8,128)S(1)}, u32[]{:S(2)}, u32[]{:S(2)}) %collective-permute-start.3) | collective-permute-done | bytes 2097184 | tf_op jit(solution)/shard_map/ppermute | solution.py:21
  327.5 5.9 %pad_maximum_fusion.1 = f32[1536,1024]{1,0:T(8,128)} fusion(f32[512,1024]{1,0:T(8,128)S(1)} %collective-permute-done.3, f32[512,1024]{1,0:T(8,128)} %all-gather.5.cloned.1.call-done, f32[512,1024]{1,0:T(8,128)} %collective-permute-done.2), kind=kLoop, calls=%fused_computation.17 | loop fusion | flops 3145728 | bytes 12582912 | tf_op jit(solution)/shard_map/concatenate | solution.py:22
  333.4 10.5 %reshape.101 = f32[24,64,16,64]{3,2,1,0:T(8,128)} reshape(f32[1536,1024]{1,0:T(8,128)} %pad_maximum_fusion.1) | data formatting | bytes 12582912 | tf_op jit(solution)/shard_map/reshape | solution.py:35
  343.9 13.9 %copy.150 = f32[24,64,16,64]{3,1,2,0:T(8,128)} copy(f32[24,64,16,64]{3,2,1,0:T(8,128)} %reshape.101) | data formatting | bytes 12582912 | tf_op jit(solution)/shard_map/reshape | solution.py:35
  357.8 14.4 %gather_fusion.9 = f32[512,64,64]{2,1,0:T(8,128)} fusion(f32[24,64,16,64]{3,1,2,0:T(8,128)} %copy.150, s32[512]{0:T(512)S(1)} %reshape.171), kind=kCustom, calls=%fused_computation.9 | custom fusion | bytes 16781312 | tf_op jit(solution)/shard_map/gather | solution.py:36
  372.2 14.6 %fusion.7 = f32[8,64,16,64]{3,1,2,0:T(8,128)} fusion(f32[8,64,4,64,1]{3,2,1,0,4:T(4,128)S(1)} %bitcast.49, f32[8,4,16,64,64]{4,3,2,1,0:T(8,128)} %bitcast.46, pred[8,4,16]{2,1,0:T(4,128)(4,1)S(1)} %get-tuple-element.20), kind=kOutput, calls=%fused_computation.19 | convolution fusion | flops 1612709888 | bytes 11010560 | tf_op jit(solution)/shard_map/iakc,ikjcb->iajb/dot_general | solution.py:39
  386.8 5.4 %copy.165 = f32[8,64,16,64]{1,0,3,2:T(8,128)} copy(f32[8,64,16,64]{3,1,2,0:T(8,128)} %fusion.7) | data formatting | bytes 4194304 | tf_op jit(solution)/shard_map/reshape | solution.py:40
  392.1 4.9 %reshape.203 = f32[512,1024]{0,1:T(8,128)} reshape(f32[8,64,16,64]{1,0,3,2:T(8,128)} %copy.165) | data formatting | bytes 4194304 | tf_op jit(solution)/shard_map/reshape | solution.py:40
  398.5 2.7 reshape.100
  401.3 5.4 %copy.145 = f32[8,64,16,64]{3,1,2,0:T(8,128)} copy(f32[8,64,16,64]{3,2,1,0:T(8,128)} %reshape.100) | data formatting | bytes 4194304 | tf_op jit(solution)/shard_map/reshape | solution.py:86
  406.7 2.8 gather_fusion.6
  410.3 26.3 %reduce-scatter.5.cloned.1.call-done = f32[512,256]{0,1:T(8,128)} async-done(((f32[512,1024]{0,1:T(8,128)}), f32[512,256]{0,1:T(8,128)}) %reduce-scatter.5.cloned.1.call-update) | async-done | bytes 524304 | tf_op jit(solution)/shard_map/reduce_scatter | solution.py:82
  (66 shorter events, 25.0 us)
Async XLA Ops:
  7.2 118.8 %copy-start.1 = (s32[1024,16]{0,1:T(8,128)S(1)}, s32[1024,16]{0,1:T(8,128)}, u32[]{:S(2)}) copy-start(s32[1024,16]{0,1:T(8,128)} %param.6) | copy-start | bytes 196612
  7.2 119.4 %copy-start.2 = (s32[1024,16]{0,1:T(8,128)S(1)}, s32[1024,16]{0,1:T(8,128)}, u32[]{:S(2)}) copy-start(s32[1024,16]{0,1:T(8,128)} %param.7) | copy-start | bytes 196612
  12.4 35.4 %all-to-all-start.1 = ((s32[128,1,1]{2,1,0:T(1,128)}), s32[128,1,1]{2,1,0:T(1,128)S(1)}, u32[]{:S(2)}, u32[]{:S(2)}) async-start(s32[128,1,1]{2,1,0:T(1,128)} %copy.133), calls=%async_computation.1 | async-start | bytes 131072 | tf_op jit(solution)/shard_map/all_to_all | solution.py:59
  47.8 39.9 %all-to-all-start = ((f32[128,4,256]{2,1,0:T(4,128)}), f32[128,4,256]{2,1,0:T(4,128)S(1)}, u32[]{:S(2)}, u32[]{:S(2)}) async-start(f32[128,4,256]{2,1,0:T(4,128)} %gather_fusion), calls=%async_computation | async-start | bytes 1048576 | tf_op jit(solution)/shard_map/all_to_all | solution.py:58
  54.4 66.0 %all-gather.3.cloned.1.call-start = ((), (), s32[]{:S(2)}) async-start(), calls=%async_computation.4 | async-start | bytes 2621440 | tf_op jit(solution)/shard_map/all_gather | solution.py:62
  89.6 167.6 %reduce-scatter.3.cloned.1.call-start = ((), (), s32[]{:S(2)}) async-start(), calls=%async_computation.5 | async-start | bytes 2621440 | tf_op jit(solution)/shard_map/reduce_scatter | solution.py:76
  120.3 28.1 %collective-permute-start.1 = (f32[512,1024]{1,0:T(8,128)}, f32[512,1024]{1,0:T(8,128)}, u32[]{:S(2)}, u32[]{:S(2)}) collective-permute-start(f32[512,1024]{1,0:T(8,128)} %all-gather.3.cloned.1.call-done), channel_id=1, source_target_pairs={{4,0},{8,4},{12,8},{16,12},{20,16},{24,20},{28,24},{32,28},{36,32}... | collective-permute-start | bytes 6291464 | tf_op jit(solution)/shard_map/ppermute | solution.py:21
  122.9 26.4 %collective-permute-start = (f32[512,1024]{1,0:T(8,128)}, f32[512,1024]{1,0:T(8,128)}, u32[]{:S(2)}, u32[]{:S(2)}) collective-permute-start(f32[512,1024]{1,0:T(8,128)} %all-gather.3.cloned.1.call-done), channel_id=1, source_target_pairs={{0,4},{4,8},{8,12},{12,16},{16,20},{20,24},{24,28},{28,32},{32,36}... | collective-permute-start | bytes 6291464 | tf_op jit(solution)/shard_map/ppermute | solution.py:18
  217.6 80.7 %all-gather.5.cloned.1.call-start = ((), (), s32[]{:S(2)}) async-start(), calls=%async_computation.6 | async-start | bytes 2621440 | tf_op jit(solution)/shard_map/all_gather | solution.py:77
  257.2 179.4 %reduce-scatter.5.cloned.1.call-start = ((), (), s32[]{:S(2)}) async-start(), calls=%async_computation.7 | async-start | bytes 2621440 | tf_op jit(solution)/shard_map/reduce_scatter | solution.py:82
  298.3 28.1 %collective-permute-start.3 = (f32[512,1024]{1,0:T(8,128)}, f32[512,1024]{1,0:T(8,128)S(1)}, u32[]{:S(2)}, u32[]{:S(2)}) collective-permute-start(f32[512,1024]{1,0:T(8,128)} %all-gather.5.cloned.1.call-done), channel_id=1, source_target_pairs={{4,0},{8,4},{12,8},{16,12},{20,16},{24,20},{28,24},{32,28},{36,32}... | collective-permute-start | bytes 6291464 | tf_op jit(solution)/shard_map/ppermute | solution.py:21
  301.1 26.4 %collective-permute-start.2 = (f32[512,1024]{1,0:T(8,128)}, f32[512,1024]{1,0:T(8,128)}, u32[]{:S(2)}, u32[]{:S(2)}) collective-permute-start(f32[512,1024]{1,0:T(8,128)} %all-gather.5.cloned.1.call-done), channel_id=1, source_target_pairs={{0,4},{4,8},{8,12},{12,16},{16,20},{20,24},{24,28},{28,32},{32,36}... | collective-permute-start | bytes 6291464 | tf_op jit(solution)/shard_map/ppermute | solution.py:18
  392.1 6.4 %copy-start = (f32[512,1024]{1,0:T(8,128)S(1)}, f32[512,1024]{1,0:T(8,128)}, u32[]{:S(2)}) copy-start(f32[512,1024]{1,0:T(8,128)} %all-gather.3.cloned.1.call-done) | copy-start | bytes 6291460
Sparse Core Ops, SparseCore 0:
  89.7 30.5 all-gather.2
  217.7 39.3 reduce-scatter.2
  260.0 38.2 all-gather.4
  397.2 39.3 reduce-scatter.4
where the time goes:
time: 454 us; the launch traced here: 446 us
  waiting for transfers between devices  219 us (48%)
  local copies, waits for them, and re-layouts  121 us (27%)
  starting transfers between devices  38.6 us (9%)
  matrix products  28.2 us (6%)
  other arithmetic  25.2 us (6%)
  between operations  14.4 us (3%)
    reshape x4, local copies, waits for them, and re-layouts, multiply(): right_blocks = right_rows.reshape(3 * own_rows, BLOCK, width_right, BLOCK)  48.9 us
    all_gather x1, waiting for transfers between devices, local(): square_full = lax.all_gather(squared, 'narrow', axis=1, tiled=True)  41.1 us
    reduce_scatter x1, waiting for transfers between devices, local(): lax.psum_scatter(square_terms, 'narrow', scatter_dimension=1, tiled=True)  39.5 us
    ppermute x2, waiting for transfers between devices, with_halo(): lax.ppermute(lax.slice_in_dim(block, 0, width, axis=dim), axis, backward)  38.4 us
    all_gather x1, waiting for transfers between devices, local(): full_own = lax.all_gather(regrouped, 'narrow', axis=1, tiled=True)  30.7 us
    gather x2, local copies, waits for them, and re-layouts, multiply(): chosen = right_blocks[nearby[:, :, None], :, slot]  28.8 us
    all_to_all x1, waiting for transfers between devices, local(): lax.all_to_all(pieces[ordering], 'wide', split_axis=0, concat_axis=0, til...  28.4 us
    dot_general x2, matrix products, multiply(): jnp.einsum('iakc,ikjcb->iajb', left_blocks, chosen, precision=lax.Precisi...  28.2 us
  transfers between devices with their start and end apart: 10, of which 10 were waited for; matrix products, arithmetic and copies ran while one was open for 6% of the time, Pallas kernels for 0%

commit v1 on v0

v1 whole, which is shorter than its diff:
```python
import functools

import jax
import jax.numpy as jnp
from jax import lax
from jax.experimental import pallas as pl
from jax.experimental.pallas import tpu as pltpu
from jax.sharding import PartitionSpec as P

BLOCK = 64
KNZ = 16
JNZ = 16
SLAB = 4
N_WIDE = 128
LAYERS = 4
OWN = 8
NBR = 1024
SLABS = 128
ROWS = OWN * BLOCK
WIDTH = 256
CLASS = 6
CLASS_COLS = CLASS * BLOCK
NEAR = 3 * OWN
HALF = 2 * BLOCK

AT_ROW = 0
AT_SLOT = AT_ROW + OWN * KNZ
AT_KEEP = AT_SLOT + OWN * CLASS
AT_ABS = AT_KEEP + OWN * CLASS
AT_REL = AT_ABS + OWN * JNZ
TABLE = AT_REL + OWN * JNZ

VMEM = pl.BlockSpec(memory_space=pltpu.VMEM)
SMEM = pl.BlockSpec(memory_space=pltpu.SMEM)
PARAMS = pltpu.CompilerParams(vmem_limit_bytes=48 * 1024 * 1024)


def cost(flops, bytes_accessed):
    return pl.CostEstimate(flops=flops, bytes_accessed=bytes_accessed, transcendentals=0)


def f32(*shape):
    return jax.ShapeDtypeStruct(shape, jnp.float32)


def pack_kernel(slot_ref, rows_ref, out_ref):
    low = lax.broadcasted_iota(jnp.int32, (8, 128), 0) < SLAB
    for pair in range(SLABS // 2):
        left = rows_ref[8 * pair : 8 * pair + 8, 0:128]
        right = rows_ref[8 * pair : 8 * pair + 8, 128:256]
        first = jnp.where(low, left, pltpu.roll(right, SLAB, 0))
        second = jnp.where(low, pltpu.roll(left, SLAB, 0), right)
        for which, tile in ((0, first), (1, second)):
            slot = slot_ref[2 * pair + which]
            target = slot >> 7
            out_ref[target, 0:8] = tile.reshape(8, 1, 128)
            out_ref[target, 8] = jnp.full((1, 128), (slot & 127).astype(jnp.float32))


def unpack_kernel(position_ref, arrived_ref, rows_ref, tiles):
    for source in range(N_WIDE):
        tiles[position_ref[source]] = arrived_ref[source, 0:8].reshape(8, 128)
    low = lax.broadcasted_iota(jnp.int32, (8, 128), 0) < SLAB
    for pair in range(SLABS // 2):
        first = tiles[2 * pair]
        second = tiles[2 * pair + 1]
        rows_ref[8 * pair : 8 * pair + 8, 0:128] = jnp.where(low, first, pltpu.roll(second, SLAB, 0))
        rows_ref[8 * pair : 8 * pair + 8, 128:256] = jnp.where(low, pltpu.roll(first, SLAB, 0), second)


def pick_pair(source, rows, slot_a, slot_b, none, first_half):
    def one(slot, half):
        there = slot != none
        safe = jnp.where(there, slot, 0)
        block = source[safe >> 1, rows, :]
        turned = pltpu.roll(block, BLOCK, 1)
        same = (safe & 1) == half
        return jnp.where(there, jnp.where(same, block, turned), 0.0)

    return jnp.where(first_half, one(slot_a, 0), one(slot_b, 1))


def class_kernel(table_ref, s0, s1, s2, s3, own_ref, to_right, to_left, chunks):
    for r, shard in enumerate((s0, s1, s2, s3)):
        chunks[2 * r] = shard[:, 0:128]
        chunks[2 * r + 1] = shard[:, 128:256]
    first_half = lax.broadcasted_iota(jnp.int32, (BLOCK, HALF), 1) < BLOCK
    for i in range(OWN):
        rows = slice(i * BLOCK, (i + 1) * BLOCK)
        for q in range(CLASS // 2):
            at = AT_SLOT + i * CLASS + 2 * q
            block = pick_pair(chunks, rows, table_ref[at], table_ref[at + 1], KNZ, first_half)
            own_ref[rows, q * 128 : (q + 1) * 128] = block
            if q > 0:
                to_right[rows, (q - 1) * 128 : q * 128] = block
            if q < 2:
                to_left[rows, q * 128 : (q + 1) * 128] = block


def split(x):
    high = x.astype(jnp.bfloat16)
    return high, (x - high.astype(jnp.float32)).astype(jnp.bfloat16)


def product(table_ref, shards, own_ref, from_left, from_right, right_high, right_low, finish):
    empty = jnp.zeros((ROWS, 128), jnp.bfloat16)
    for source, row, col in ((from_left, 0, 0), (own_ref, ROWS, 0), (from_right, 2 * ROWS, 128)):
        width = source.shape[1]
        high, low = split(source[...])
        right_high[row : row + ROWS, col : col + width] = high
        right_low[row : row + ROWS, col : col + width] = low
    for store in (right_high, right_low):
        store[0:ROWS, WIDTH:CLASS_COLS] = empty
        store[2 * ROWS : 3 * ROWS, 0:128] = empty
    dot = functools.partial(jnp.dot, preferred_element_type=jnp.float32)
    for i in range(OWN):
        rows = slice(i * BLOCK, (i + 1) * BLOCK)
        total = jnp.zeros((BLOCK, CLASS_COLS), jnp.float32)
        for r, shard in enumerate(shards):
            high, low = split(shard[rows, :])
            places = [
                pl.ds(pl.multiple_of(table_ref[AT_ROW + i * KNZ + 4 * r + k] * BLOCK, BLOCK), BLOCK)
                for k in range(KNZ // LAYERS)
            ]
            weight_high = jnp.concatenate([right_high[p, :] for p in places], axis=0)
            weight_low = jnp.concatenate([right_low[p, :] for p in places], axis=0)
            both = dot(jnp.concatenate([high, low], axis=0), weight_high)
            total = total + both[:BLOCK] + both[BLOCK:] + dot(high, weight_low)
        finish(i, rows, total)


def square_kernel(
    table_ref, s0, s1, s2, s3, own_ref, from_left, from_right, square_ref, to_right, to_left, slots_ref, right_high, right_low, chunks
):
    first_half = lax.broadcasted_iota(jnp.int32, (BLOCK, HALF), 1) < BLOCK

    def finish(i, rows, total):
        for q in range(CLASS // 2):
            at = AT_KEEP + i * CLASS + 2 * q
            keep = jnp.where(first_half, table_ref[at], table_ref[at + 1]) != 0
            block = jnp.where(keep, total[:, q * 128 : (q + 1) * 128], 0.0)
            chunks[q, rows, :] = block
            square_ref[rows, q * 128 : (q + 1) * 128] = block
            if q > 0:
                to_right[rows, (q - 1) * 128 : q * 128] = block
            if q < 2:
                to_left[rows, q * 128 : (q + 1) * 128] = block
        for c in range(JNZ // 2):
            at = AT_ABS + i * JNZ + 2 * c
            block = pick_pair(chunks, rows, table_ref[at], table_ref[at + 1], -1, first_half)
            slots_ref[c // 2, rows, (c % 2) * 128 : (c % 2 + 1) * 128] = block

    product(table_ref, (s0, s1, s2, s3), own_ref, from_left, from_right, right_high, right_low, finish)


def cubic_kernel(
    table_ref, s0, s1, s2, s3, own_ref, from_left, from_right, keep_ref, o0, o1, o2, o3, right_high, right_low, chunks
):
    first_half = lax.broadcasted_iota(jnp.int32, (BLOCK, HALF), 1) < BLOCK
    outs = (o0, o1, o2, o3)

    def finish(i, rows, total):
        for q in range(CLASS // 2):
            cols = slice(q * 128, (q + 1) * 128)
            chunks[q, rows, :] = 1.5 * keep_ref[rows, cols] - 0.5 * total[:, cols]
        for c in range(JNZ // 2):
            at = AT_REL + i * JNZ + 2 * c
            block = pick_pair(chunks, rows, table_ref[at], table_ref[at + 1], -1, first_half)
            outs[c // 2][rows, (c % 2) * 128 : (c % 2 + 1) * 128] = block

    product(table_ref, (s0, s1, s2, s3), own_ref, from_left, from_right, right_high, right_low, finish)


RIGHT = [
    pltpu.VMEM((NEAR * BLOCK, CLASS_COLS), jnp.bfloat16),
    pltpu.VMEM((NEAR * BLOCK, CLASS_COLS), jnp.bfloat16),
    pltpu.VMEM((CLASS // 2, ROWS, HALF), jnp.float32),
]


def shift(x, axis, by):
    count = lax.axis_size(axis)
    return lax.ppermute(x, axis, [(i, (i + by) % count) for i in range(count)])


def tables(block_cols, filter_cols, wide_index, layer):
    first_row = wide_index * OWN
    base = first_row - OWN

    def own(cols):
        mine = lax.dynamic_slice_in_dim(cols, first_row, OWN, 0)
        mine = (mine - base) & (NBR - 1)
        turned = lax.dynamic_slice_in_dim(jnp.concatenate([mine, mine], axis=1), layer * (KNZ // LAYERS), KNZ, 1)
        return mine, turned

    _, cols = own(block_cols)
    kept, kept_turned = own(filter_cols)
    places = layer + LAYERS * jnp.arange(CLASS, dtype=jnp.int32)
    slots = jnp.arange(KNZ, dtype=jnp.int32)
    slot = jnp.min(jnp.where(cols[:, None, :] == places[None, :, None], slots, KNZ), axis=2)
    keep = jnp.max((kept[:, None, :] == places[None, :, None]).astype(jnp.int32), axis=2)

    def source(filters):
        return jnp.where((filters - layer) & (LAYERS - 1) == 0, (filters - layer) >> 2, -1)

    return jnp.concatenate([part.reshape(-1) for part in (cols, slot, keep, source(kept), source(kept_turned))])


def local(restart, slab_slot, block_cols, filter_cols):
    wide_index = lax.axis_index("wide")
    layer = lax.axis_index("narrow")
    table = tables(block_cols, filter_cols, wide_index, layer)

    packed = pl.pallas_call(
        pack_kernel,
        out_shape=f32(N_WIDE, 9, 1, 128),
        in_specs=[SMEM, VMEM],
        out_specs=VMEM,
        compiler_params=PARAMS,
        cost_estimate=cost(0, 1 << 20),
        name="pack",
    )(slab_slot, restart)
    arrived = lax.all_to_all(packed, "wide", split_axis=0, concat_axis=0, tiled=True)
    position = arrived[:, 8, 0, 0].astype(jnp.int32)
    mine = pl.pallas_call(
        unpack_kernel,
        out_shape=f32(ROWS, WIDTH),
        in_specs=[SMEM, VMEM],
        out_specs=VMEM,
        scratch_shapes=[pltpu.VMEM((SLABS, 8, 128), jnp.float32)],
        compiler_params=PARAMS,
        cost_estimate=cost(0, 1 << 20),
        name="unpack",
    )(position, arrived)
    shards = (mine, shift(mine, "narrow", -1), shift(mine, "narrow", -2), shift(mine, "narrow", -3))

    half = f32(ROWS, WIDTH)
    whole = f32(ROWS, CLASS_COLS)
    own, to_right, to_left = pl.pallas_call(
        class_kernel,
        out_shape=(whole, half, half),
        in_specs=[SMEM] + [VMEM] * 4,
        out_specs=(VMEM,) * 3,
        scratch_shapes=[pltpu.VMEM((2 * LAYERS, ROWS, HALF), jnp.float32)],
        compiler_params=PARAMS,
        cost_estimate=cost(0, 4 << 20),
        name="columns_of_class",
    )(table, *shards)
    from_left = shift(to_right, "wide", 1)
    from_right = shift(to_left, "wide", -1)

    flops = 2 * 3 * ROWS * KNZ * BLOCK * CLASS_COLS
    square, to_right, to_left, square_slots = pl.pallas_call(
        square_kernel,
        out_shape=(whole, half, half, f32(LAYERS, ROWS, WIDTH)),
        in_specs=[SMEM] + [VMEM] * 7,
        out_specs=(VMEM,) * 4,
        scratch_shapes=RIGHT,
        compiler_params=PARAMS,
        cost_estimate=cost(flops, 8 << 20),
        name="square",
    )(table, *shards, own, from_left, from_right)
    squared = lax.psum_scatter(square_slots, "narrow", scatter_dimension=0)
    from_left = shift(to_right, "wide", 1)
    from_right = shift(to_left, "wide", -1)

    parts = pl.pallas_call(
        cubic_kernel,
        out_shape=(half,) * 4,
        in_specs=[SMEM] + [VMEM] * 8,
        out_specs=(VMEM,) * 4,
        scratch_shapes=RIGHT,
        compiler_params=PARAMS,
        cost_estimate=cost(flops, 8 << 20),
        name="cubic",
    )(table, *shards, square, from_left, from_right, own)
    updated = parts[0] + shift(parts[1], "narrow", 1) + shift(parts[2], "narrow", 2) + shift(parts[3], "narrow", 3)
    return (squared, updated)


def solution(mesh):
    placed = (P("wide", "narrow"), P("wide"), P(), P())
    return jax.shard_map(
        local,
        mesh=mesh,
        in_specs=placed,
        out_specs=(P("wide", "narrow"), P("wide", "narrow")),
        check_vma=False,
    )
```

time: 454 us -> 184 us (0.41)
  the two profiles are of different devices: /device:TPU:1 before, /device:TPU:24 now
where the time goes in v1:
time: 184 us; the launch traced here: 180 us
  waiting for transfers between devices  88.6 us (48%)
  starting transfers between devices  56.1 us (30%)
  between operations  14.2 us (8%)
  Pallas kernels  12.5 us (7%)
  local copies, waits for them, and re-layouts  5.02 us (3%)
  other arithmetic  3.88 us (2%)
    ppermute x10, waiting for transfers between devices, shift(): return lax.ppermute(x, axis, [(i, (i + by) % count) for i in range(count)])  53.6 us
    ppermute x10, starting transfers between devices, shift(): return lax.ppermute(x, axis, [(i, (i + by) % count) for i in range(count)])  36.3 us
    all_to_all x1, waiting for transfers between devices, local(): lax.all_to_all(packed, 'wide', split_axis=0, concat_axis=0, tiled=True)  35 us
    all_to_all x1, starting transfers between devices, local(): lax.all_to_all(packed, 'wide', split_axis=0, concat_axis=0, tiled=True)  19.8 us
    pallas_call x1, Pallas kernels, local(): pl.pallas_call(square_kernel, out_shape=(whole, half, half, f32(LAYERS, R...  4.77 us
    pallas_call x1, Pallas kernels, local(): pl.pallas_call(cubic_kernel, out_shape=(half,) * 4, in_specs=[SMEM] + [VM...  4.02 us
  transfers between devices with their start and end apart: 12, of which 11 were waited for; matrix products, arithmetic and copies ran while one was open for 2% of the time, Pallas kernels for 2%

profile of v1, /device:TPU:24, one launch (start us, length us, event | category | flops | bytes accessed | tf_op | source)
XLA Modules:
  0.0 180.3 jit_solution(18066127547085707129)
XLA Ops:
  7.2 1.0 copy-done.3
  8.9 1.7 pack.1
  10.6 19.8 %all-to-all-start = ((f32[128,9,1,128]{3,2,1,0:T(1,128)}), f32[128,9,1,128]{3,2,1,0:T(1,128)S(1)}, u32[]{:S(2)}, u32[]{:S(2)}) async-start(f32[128,9,1,128]{3,2,1,0:T(1,128)} %pack.1), calls=%async_computation | async-start | bytes 1179648 | tf_op jit(solution)/shard_map/all_to_all | solution.py:223
  30.4 0.8 constant_dynamic-slice_fusion
  31.5 35.0 %all-to-all-done.arrived_ref = f32[128,9,1,128]{3,2,1,0:T(1,128)S(1)} async-done(((f32[128,9,1,128]{3,2,1,0:T(1,128)}), f32[128,9,1,128]{3,2,1,0:T(1,128)S(1)}, u32[]{:S(2)}, u32[]{:S(2)}) %all-to-all-start) | async-done | bytes 589856 | tf_op jit(solution)/shard_map/all_to_all | solution.py:223
  66.5 2.4 %fusion.position_ref = s32[128]{0:T(128)S(1)} fusion(f32[128,9,1,128]{3,2,1,0:T(1,128)S(1)} %all-to-all-done.arrived_ref), kind=kLoop, calls=%fused_computation.2 | loop fusion | flops 128 | bytes 1024 | tf_op jit(solution)/shard_map/convert_element_type | solution.py:224
  68.8 0.8 unpack.1.s0
  69.6 2.1 %collective-permute-start.2 = (f32[512,256]{1,0:T(8,128)S(1)}, f32[512,256]{1,0:T(8,128)S(1)}, u32[]{:S(2)}, u32[]{:S(2)}) collective-permute-start(f32[512,256]{1,0:T(8,128)S(1)} %unpack.1.s0), channel_id=1, source_target_pairs={{0,1},{1,2},{2,3},{3,0},{4,5},{5,6},{6,7},{7,4},{8,9},{9,10},{10,1... | collective-permute-start | bytes 1572872 | tf_op jit(solution)/shard_map/ppermute | solution.py:183
  71.8 4.5 %collective-permute-start.1 = (f32[512,256]{1,0:T(8,128)S(1)}, f32[512,256]{1,0:T(8,128)S(1)}, u32[]{:S(2)}, u32[]{:S(2)}) collective-permute-start(f32[512,256]{1,0:T(8,128)S(1)} %unpack.1.s0), channel_id=1, source_target_pairs={{0,2},{1,3},{2,0},{3,1},{4,6},{5,7},{6,4},{7,5},{8,10},{9,11},{10,... | collective-permute-start | bytes 1572872 | tf_op jit(solution)/shard_map/ppermute | solution.py:183
  76.3 1.9 %collective-permute-start = (f32[512,256]{1,0:T(8,128)S(1)}, f32[512,256]{1,0:T(8,128)S(1)}, u32[]{:S(2)}, u32[]{:S(2)}) collective-permute-start(f32[512,256]{1,0:T(8,128)S(1)} %unpack.1.s0), channel_id=1, source_target_pairs={{0,3},{1,0},{2,1},{3,2},{4,7},{5,4},{6,5},{7,6},{8,11},{9,8},{10,9... | collective-permute-start | bytes 1572872 | tf_op jit(solution)/shard_map/ppermute | solution.py:183
  79.4 6.9 %collective-permute-done.2.s3 = f32[512,256]{1,0:T(8,128)S(1)} collective-permute-done((f32[512,256]{1,0:T(8,128)S(1)}, f32[512,256]{1,0:T(8,128)S(1)}, u32[]{:S(2)}, u32[]{:S(2)}) %collective-permute-start.2) | collective-permute-done | bytes 524320 | tf_op jit(solution)/shard_map/ppermute | solution.py:183
  86.4 3.7 %collective-permute-done.1.s2 = f32[512,256]{1,0:T(8,128)S(1)} collective-permute-done((f32[512,256]{1,0:T(8,128)S(1)}, f32[512,256]{1,0:T(8,128)S(1)}, u32[]{:S(2)}, u32[]{:S(2)}) %collective-permute-start.1) | collective-permute-done | bytes 524320 | tf_op jit(solution)/shard_map/ppermute | solution.py:183
  90.1 9.2 %collective-permute-done.s1 = f32[512,256]{1,0:T(8,128)S(1)} collective-permute-done((f32[512,256]{1,0:T(8,128)S(1)}, f32[512,256]{1,0:T(8,128)S(1)}, u32[]{:S(2)}, u32[]{:S(2)}) %collective-permute-start) | collective-permute-done | bytes 524320 | tf_op jit(solution)/shard_map/ppermute | solution.py:183
  99.2 1.2 columns_of_class.1
  100.4 1.9 %collective-permute-start.3 = (f32[512,256]{1,0:T(8,128)S(1)}, f32[512,256]{1,0:T(8,128)S(1)}, u32[]{:S(2)}, u32[]{:S(2)}) collective-permute-start(f32[512,256]{1,0:T(8,128)S(1)} %get-tuple-element.14), channel_id=1, source_target_pairs={{0,4},{4,8},{8,12},{12,16},{16,20},{20,24},{24,28},{28,32},{32,36}... | collective-permute-start | bytes 1572872 | tf_op jit(solution)/shard_map/ppermute | solution.py:183
  102.3 7.0 %collective-permute-start.4 = (f32[512,256]{1,0:T(8,128)S(1)}, f32[512,256]{1,0:T(8,128)S(1)}, u32[]{:S(2)}, u32[]{:S(2)}) collective-permute-start(f32[512,256]{1,0:T(8,128)S(1)} %get-tuple-element.15), channel_id=1, source_target_pairs={{0,508},{4,0},{8,4},{12,8},{16,12},{20,16},{24,20},{28,24},{32,28}... | collective-permute-start | bytes 1572872 | tf_op jit(solution)/shard_map/ppermute | solution.py:183
  109.3 4.9 %collective-permute-done.3.from_left = f32[512,256]{1,0:T(8,128)S(1)} collective-permute-done((f32[512,256]{1,0:T(8,128)S(1)}, f32[512,256]{1,0:T(8,128)S(1)}, u32[]{:S(2)}, u32[]{:S(2)}) %collective-permute-start.3) | collective-permute-done | bytes 524320 | tf_op jit(solution)/shard_map/ppermute | solution.py:183
  114.2 1.8 collective-permute-done.4.from_right
  116.0 4.8 %square.1 = (f32[512,384]{1,0:T(8,128)S(1)}, f32[512,256]{1,0:T(8,128)S(1)}, f32[512,256]{1,0:T(8,128)S(1)}, f32[4,512,256]{2,1,0:T(8,128)}) custom-call(s32[480]{0:T(512)S(1)} %concatenate.11.table_ref, f32[512,256]{1,0:T(8,128)S(1)} %unpack.1.s0, f32[512,256]{1,0:T(8,128)S(1)} %collective-permute-done.s1, f32[512,256]{1,0:T(8,128)S(1)} %collective-permute-done.1.s2, ...), custom_call_target="tpu_custom_call" | custom-call | flops 1207959552 | bytes 8388608 | tf_op jit(solution)/shard_map/square/pallas_call | solution.py:253
  120.8 0.9 copy-done.1
  121.6 0.8 copy-done.5
  122.5 2.1 %collective-permute-start.5 = (f32[512,256]{1,0:T(8,128)}, f32[512,256]{1,0:T(8,128)S(1)}, u32[]{:S(2)}, u32[]{:S(2)}) collective-permute-start(f32[512,256]{1,0:T(8,128)} %copy-done.5), channel_id=1, source_target_pairs={{0,4},{4,8},{8,12},{12,16},{16,20},{20,24},{24,28},{28,32},{32,36}... | collective-permute-start | bytes 1572872 | tf_op jit(solution)/shard_map/ppermute | solution.py:183
  124.5 7.1 %collective-permute-start.6 = (f32[512,256]{1,0:T(8,128)S(1)}, f32[512,256]{1,0:T(8,128)S(1)}, u32[]{:S(2)}, u32[]{:S(2)}) collective-permute-start(f32[512,256]{1,0:T(8,128)S(1)} %get-tuple-element.19), channel_id=1, source_target_pairs={{0,508},{4,0},{8,4},{12,8},{16,12},{20,16},{24,20},{28,24},{32,28}... | collective-permute-start | bytes 1572872 | tf_op jit(solution)/shard_map/ppermute | solution.py:183
  131.7 5.1 %collective-permute-done.5.from_left = f32[512,256]{1,0:T(8,128)S(1)} collective-permute-done((f32[512,256]{1,0:T(8,128)}, f32[512,256]{1,0:T(8,128)S(1)}, u32[]{:S(2)}, u32[]{:S(2)}) %collective-permute-start.5) | collective-permute-done | bytes 524320 | tf_op jit(solution)/shard_map/ppermute | solution.py:183
  136.8 1.5 collective-permute-done.6.from_right
  138.3 4.0 %cubic.1 = (f32[512,256]{1,0:T(8,128)S(1)}, f32[512,256]{1,0:T(8,128)S(1)}, f32[512,256]{1,0:T(8,128)S(1)}, f32[512,256]{1,0:T(8,128)S(1)}) custom-call(s32[480]{0:T(512)S(1)} %concatenate.11.table_ref, f32[512,256]{1,0:T(8,128)S(1)} %unpack.1.s0, f32[512,256]{1,0:T(8,128)S(1)} %collective-permute-done.s1, f32[512,256]{1,0:T(8,128)S(1)} %collective-permute-done.1.s2, ...), custom_call_target="tpu_custom_call" | custom-call | flops 1207959552 | bytes 8388608 | tf_op jit(solution)/shard_map/cubic/pallas_call | solution.py:267
  142.4 2.5 %collective-permute-start.7 = (f32[512,256]{1,0:T(8,128)S(1)}, f32[512,256]{1,0:T(8,128)S(1)}, u32[]{:S(2)}, u32[]{:S(2)}) collective-permute-start(f32[512,256]{1,0:T(8,128)S(1)} %get-tuple-element.21), channel_id=1, source_target_pairs={{0,1},{1,2},{2,3},{3,0},{4,5},{5,6},{6,7},{7,4},{8,9},{9,10},{10,1... | collective-permute-start | bytes 1572872 | tf_op jit(solution)/shard_map/ppermute | solution.py:183
  144.9 4.4 %collective-permute-start.8 = (f32[512,256]{1,0:T(8,128)S(1)}, f32[512,256]{1,0:T(8,128)S(1)}, u32[]{:S(2)}, u32[]{:S(2)}) collective-permute-start(f32[512,256]{1,0:T(8,128)S(1)} %get-tuple-element.22), channel_id=1, source_target_pairs={{0,2},{1,3},{2,0},{3,1},{4,6},{5,7},{6,4},{7,5},{8,10},{9,11},{10,... | collective-permute-start | bytes 1572872 | tf_op jit(solution)/shard_map/ppermute | solution.py:183
  149.3 2.7 %collective-permute-start.9 = (f32[512,256]{1,0:T(8,128)S(1)}, f32[512,256]{1,0:T(8,128)S(1)}, u32[]{:S(2)}, u32[]{:S(2)}) collective-permute-start(f32[512,256]{1,0:T(8,128)S(1)} %get-tuple-element.23), channel_id=1, source_target_pairs={{0,3},{1,0},{2,1},{3,2},{4,7},{5,4},{6,5},{7,6},{8,11},{9,8},{10,9... | collective-permute-start | bytes 1572872 | tf_op jit(solution)/shard_map/ppermute | solution.py:183
  152.0 11.6 %collective-permute-done.7 = f32[512,256]{1,0:T(8,128)S(1)} collective-permute-done((f32[512,256]{1,0:T(8,128)S(1)}, f32[512,256]{1,0:T(8,128)S(1)}, u32[]{:S(2)}, u32[]{:S(2)}) %collective-permute-start.7) | collective-permute-done | bytes 524320 | tf_op jit(solution)/shard_map/ppermute | solution.py:183
  164.3 8.2 %collective-permute-done.9 = f32[512,256]{1,0:T(8,128)S(1)} collective-permute-done((f32[512,256]{1,0:T(8,128)S(1)}, f32[512,256]{1,0:T(8,128)S(1)}, u32[]{:S(2)}, u32[]{:S(2)}) %collective-permute-start.9) | collective-permute-done | bytes 524320 | tf_op jit(solution)/shard_map/ppermute | solution.py:183
  172.5 0.9 add_add_fusion
  (31 shorter events, 2.9 us)
Async XLA Ops:
  7.2 1.0 copy-start.3
  8.2 0.7 copy-start.4
  10.6 55.9 %all-to-all-start = ((f32[128,9,1,128]{3,2,1,0:T(1,128)}), f32[128,9,1,128]{3,2,1,0:T(1,128)S(1)}, u32[]{:S(2)}, u32[]{:S(2)}) async-start(f32[128,9,1,128]{3,2,1,0:T(1,128)} %pack.1), calls=%async_computation | async-start | bytes 1179648 | tf_op jit(solution)/shard_map/all_to_all | solution.py:223
  30.4 143.1 %reduce-scatter.2.cloned.1.call-start = ((), (), s32[]{:S(2)}) async-start(), calls=%async_computation.2 | async-start | bytes 2621440 | tf_op jit(solution)/shard_map/reduce_scatter | solution.py:263
  69.6 16.8 %collective-permute-start.2 = (f32[512,256]{1,0:T(8,128)S(1)}, f32[512,256]{1,0:T(8,128)S(1)}, u32[]{:S(2)}, u32[]{:S(2)}) collective-permute-start(f32[512,256]{1,0:T(8,128)S(1)} %unpack.1.s0), channel_id=1, source_target_pairs={{0,1},{1,2},{2,3},{3,0},{4,5},{5,6},{6,7},{7,4},{8,9},{9,10},{10,1... | collective-permute-start | bytes 1572872 | tf_op jit(solution)/shard_map/ppermute | solution.py:183
  71.8 18.3 %collective-permute-start.1 = (f32[512,256]{1,0:T(8,128)S(1)}, f32[512,256]{1,0:T(8,128)S(1)}, u32[]{:S(2)}, u32[]{:S(2)}) collective-permute-start(f32[512,256]{1,0:T(8,128)S(1)} %unpack.1.s0), channel_id=1, source_target_pairs={{0,2},{1,3},{2,0},{3,1},{4,6},{5,7},{6,4},{7,5},{8,10},{9,11},{10,... | collective-permute-start | bytes 1572872 | tf_op jit(solution)/shard_map/ppermute | solution.py:183
  76.3 22.9 %collective-permute-start = (f32[512,256]{1,0:T(8,128)S(1)}, f32[512,256]{1,0:T(8,128)S(1)}, u32[]{:S(2)}, u32[]{:S(2)}) collective-permute-start(f32[512,256]{1,0:T(8,128)S(1)} %unpack.1.s0), channel_id=1, source_target_pairs={{0,3},{1,0},{2,1},{3,2},{4,7},{5,4},{6,5},{7,6},{8,11},{9,8},{10,9... | collective-permute-start | bytes 1572872 | tf_op jit(solution)/shard_map/ppermute | solution.py:183
  100.4 20.4 %copy-start = (f32[512,384]{1,0:T(8,128)}, f32[512,384]{1,0:T(8,128)S(1)}, u32[]{:S(2)}) copy-start(f32[512,384]{1,0:T(8,128)S(1)} %get-tuple-element.13.own_ref.keep_ref) | copy-start | bytes 2359300
  100.4 13.8 %collective-permute-start.3 = (f32[512,256]{1,0:T(8,128)S(1)}, f32[512,256]{1,0:T(8,128)S(1)}, u32[]{:S(2)}, u32[]{:S(2)}) collective-permute-start(f32[512,256]{1,0:T(8,128)S(1)} %get-tuple-element.14), channel_id=1, source_target_pairs={{0,4},{4,8},{8,12},{12,16},{16,20},{20,24},{24,28},{28,32},{32,36}... | collective-permute-start | bytes 1572872 | tf_op jit(solution)/shard_map/ppermute | solution.py:183
  102.3 13.6 %collective-permute-start.4 = (f32[512,256]{1,0:T(8,128)S(1)}, f32[512,256]{1,0:T(8,128)S(1)}, u32[]{:S(2)}, u32[]{:S(2)}) collective-permute-start(f32[512,256]{1,0:T(8,128)S(1)} %get-tuple-element.15), channel_id=1, source_target_pairs={{0,508},{4,0},{8,4},{12,8},{16,12},{20,16},{24,20},{28,24},{32,28}... | collective-permute-start | bytes 1572872 | tf_op jit(solution)/shard_map/ppermute | solution.py:183
  120.8 0.9 copy-start.1
  121.6 0.8 copy-start.5
  122.4 15.9 %copy-start.2 = (f32[512,384]{1,0:T(8,128)S(1)}, f32[512,384]{1,0:T(8,128)}, u32[]{:S(2)}) copy-start(f32[512,384]{1,0:T(8,128)} %copy-done.1) | copy-start | bytes 2359300
  122.5 14.3 %collective-permute-start.5 = (f32[512,256]{1,0:T(8,128)}, f32[512,256]{1,0:T(8,128)S(1)}, u32[]{:S(2)}, u32[]{:S(2)}) collective-permute-start(f32[512,256]{1,0:T(8,128)} %copy-done.5), channel_id=1, source_target_pairs={{0,4},{4,8},{8,12},{12,16},{16,20},{20,24},{24,28},{28,32},{32,36}... | collective-permute-start | bytes 1572872 | tf_op jit(solution)/shard_map/ppermute | solution.py:183
  124.5 13.8 %collective-permute-start.6 = (f32[512,256]{1,0:T(8,128)S(1)}, f32[512,256]{1,0:T(8,128)S(1)}, u32[]{:S(2)}, u32[]{:S(2)}) collective-permute-start(f32[512,256]{1,0:T(8,128)S(1)} %get-tuple-element.19), channel_id=1, source_target_pairs={{0,508},{4,0},{8,4},{12,8},{16,12},{20,16},{24,20},{28,24},{32,28}... | collective-permute-start | bytes 1572872 | tf_op jit(solution)/shard_map/ppermute | solution.py:183
  142.4 21.2 %collective-permute-start.7 = (f32[512,256]{1,0:T(8,128)S(1)}, f32[512,256]{1,0:T(8,128)S(1)}, u32[]{:S(2)}, u32[]{:S(2)}) collective-permute-start(f32[512,256]{1,0:T(8,128)S(1)} %get-tuple-element.21), channel_id=1, source_target_pairs={{0,1},{1,2},{2,3},{3,0},{4,5},{5,6},{6,7},{7,4},{8,9},{9,10},{10,1... | collective-permute-start | bytes 1572872 | tf_op jit(solution)/shard_map/ppermute | solution.py:183
  144.9 19.4 %collective-permute-start.8 = (f32[512,256]{1,0:T(8,128)S(1)}, f32[512,256]{1,0:T(8,128)S(1)}, u32[]{:S(2)}, u32[]{:S(2)}) collective-permute-start(f32[512,256]{1,0:T(8,128)S(1)} %get-tuple-element.22), channel_id=1, source_target_pairs={{0,2},{1,3},{2,0},{3,1},{4,6},{5,7},{6,4},{7,5},{8,10},{9,11},{10,... | collective-permute-start | bytes 1572872 | tf_op jit(solution)/shard_map/ppermute | solution.py:183
  149.3 23.2 %collective-permute-start.9 = (f32[512,256]{1,0:T(8,128)S(1)}, f32[512,256]{1,0:T(8,128)S(1)}, u32[]{:S(2)}, u32[]{:S(2)}) collective-permute-start(f32[512,256]{1,0:T(8,128)S(1)} %get-tuple-element.23), channel_id=1, source_target_pairs={{0,3},{1,0},{2,1},{3,2},{4,7},{5,4},{6,5},{7,6},{8,11},{9,8},{10,9... | collective-permute-start | bytes 1572872 | tf_op jit(solution)/shard_map/ppermute | solution.py:183
Sparse Core Ops, SparseCore 0:
  122.6 35.4 reduce-scatter.1

commit v2 on v1

--- a/solution.py
+++ b/solution.py
@@ -32,7 +32,7 @@
 
 VMEM = pl.BlockSpec(memory_space=pltpu.VMEM)
 SMEM = pl.BlockSpec(memory_space=pltpu.SMEM)
-PARAMS = pltpu.CompilerParams(vmem_limit_bytes=48 * 1024 * 1024)
+PARAMS = pltpu.CompilerParams(vmem_limit_bytes=24 * 1024 * 1024)
 
 
 def cost(flops, bytes_accessed):
@@ -130,9 +130,10 @@
 
 
 def square_kernel(
-    table_ref, s0, s1, s2, s3, own_ref, from_left, from_right, square_ref, to_right, to_left, slots_ref, right_high, right_low, chunks
+    table_ref, s0, s1, s2, s3, own_ref, from_left, from_right, square_ref, to_right, to_left, o0, o1, o2, o3, right_high, right_low, chunks
 ):
     first_half = lax.broadcasted_iota(jnp.int32, (BLOCK, HALF), 1) < BLOCK
+    outs = (o0, o1, o2, o3)
 
     def finish(i, rows, total):
         for q in range(CLASS // 2):
@@ -146,9 +147,9 @@
             if q < 2:
                 to_left[rows, q * 128 : (q + 1) * 128] = block
         for c in range(JNZ // 2):
-            at = AT_ABS + i * JNZ + 2 * c
+            at = AT_REL + i * JNZ + 2 * c
             block = pick_pair(chunks, rows, table_ref[at], table_ref[at + 1], -1, first_half)
-            slots_ref[c // 2, rows, (c % 2) * 128 : (c % 2 + 1) * 128] = block
+            outs[c // 2][rows, (c % 2) * 128 : (c % 2 + 1) * 128] = block
 
     product(table_ref, (s0, s1, s2, s3), own_ref, from_left, from_right, right_high, right_low, finish)
 
@@ -181,6 +182,11 @@
 def shift(x, axis, by):
     count = lax.axis_size(axis)
     return lax.ppermute(x, axis, [(i, (i + by) % count) for i in range(count)])
+
+
+def gather_slots(parts):
+    first, second, third = (shift(parts[r], "narrow", r) for r in range(1, LAYERS))
+    return parts[0] + first + second + third
 
 
 def tables(block_cols, filter_cols, wide_index, layer):
@@ -250,20 +256,20 @@
     from_right = shift(to_left, "wide", -1)
 
     flops = 2 * 3 * ROWS * KNZ * BLOCK * CLASS_COLS
-    square, to_right, to_left, square_slots = pl.pallas_call(
+    square, to_right, to_left, *slots = pl.pallas_call(
         square_kernel,
-        out_shape=(whole, half, half, f32(LAYERS, ROWS, WIDTH)),
+        out_shape=(whole,) + (half,) * 6,
         in_specs=[SMEM] + [VMEM] * 7,
-        out_specs=(VMEM,) * 4,
+        out_specs=(VMEM,) * 7,
         scratch_shapes=RIGHT,
         compiler_params=PARAMS,
         cost_estimate=cost(flops, 8 << 20),
         name="square",
     )(table, *shards, own, from_left, from_right)
-    squared = lax.psum_scatter(square_slots, "narrow", scatter_dimension=0)
     from_left = shift(to_right, "wide", 1)
     from_right = shift(to_left, "wide", -1)
 
+    squared = gather_slots(slots)
     parts = pl.pallas_call(
         cubic_kernel,
         out_shape=(half,) * 4,
@@ -274,7 +280,7 @@
         cost_estimate=cost(flops, 8 << 20),
         name="cubic",
     )(table, *shards, square, from_left, from_right, own)
-    updated = parts[0] + shift(parts[1], "narrow", 1) + shift(parts[2], "narrow", 2) + shift(parts[3], "narrow", 3)
+    updated = gather_slots(parts)
     return (squared, updated)
 
 

time: 184 us -> 173 us (0.940); the launches traced: 180 us -> 171 us
  between operations: 14.2 us -> 0.85 us
  starting transfers between devices: 56.1 us -> 65.6 us
  waiting for transfers between devices: 88.6 us -> 86.1 us
  Pallas kernels: 12.5 us -> 10.6 us
    ppermute x10 -> x13, starting transfers between devices: 36.3 us -> 45.9 us  [shift(): return lax.ppermute(x, axis, [(i, (i + by) % count) for i in range(count)])]
    ppermute x10 -> x13, waiting for transfers between devices: 53.6 us -> 51.1 us  [shift(): return lax.ppermute(x, axis, [(i, (i + by) % count) for i in range(count)])]
  transfers between devices with their start and end apart: 12 -> 14, of which waited for: 11 -> 10; matrix products, arithmetic and copies ran while one was open for 2% -> 2% of each run, Pallas kernels for 2% -> 2%
where the time goes in v2:
time: 173 us; the launch traced here: 171 us
  waiting for transfers between devices  86.1 us (50%)
  starting transfers between devices  65.6 us (38%)
  Pallas kernels  10.6 us (6%)
  other arithmetic  4.81 us (3%)
  local copies, waits for them, and re-layouts  3.34 us (2%)
    ppermute x13, waiting for transfers between devices, shift(): return lax.ppermute(x, axis, [(i, (i + by) % count) for i in range(count)])  51.1 us
    ppermute x13, starting transfers between devices, shift(): return lax.ppermute(x, axis, [(i, (i + by) % count) for i in range(count)])  45.9 us
    all_to_all x1, waiting for transfers between devices, local(): lax.all_to_all(packed, 'wide', split_axis=0, concat_axis=0, tiled=True)  35 us
    all_to_all x1, starting transfers between devices, local(): lax.all_to_all(packed, 'wide', split_axis=0, concat_axis=0, tiled=True)  19.8 us
  transfers between devices with their start and end apart: 14, of which 10 were waited for; matrix products, arithmetic and copies ran while one was open for 2% of the time, Pallas kernels for 2%

profile of v2, /device:TPU:24, one launch (start us, length us, event | category | flops | bytes accessed | tf_op | source)
XLA Modules:
  0.0 171.3 jit_solution(15530566600278985220)
XLA Ops:
  0.6 1.0 copy-done
  2.3 1.7 %pack.1 = f32[128,9,1,128]{3,2,1,0:T(1,128)} custom-call(s32[128]{0:T(128)S(1)} %copy-done.1, f32[512,256]{1,0:T(8,128)S(1)} %copy-done), custom_call_target="tpu_custom_call" | custom-call | bytes 1048576 | tf_op jit(solution)/shard_map/pack/pallas_call | solution.py:220
  4.1 19.8 %all-to-all-start = ((f32[128,9,1,128]{3,2,1,0:T(1,128)}), f32[128,9,1,128]{3,2,1,0:T(1,128)S(1)}, u32[]{:S(2)}, u32[]{:S(2)}) async-start(f32[128,9,1,128]{3,2,1,0:T(1,128)} %pack.1), calls=%async_computation | async-start | bytes 1179648 | tf_op jit(solution)/shard_map/all_to_all | solution.py:229
  24.9 35.0 %all-to-all-done.arrived_ref = f32[128,9,1,128]{3,2,1,0:T(1,128)S(1)} async-done(((f32[128,9,1,128]{3,2,1,0:T(1,128)}), f32[128,9,1,128]{3,2,1,0:T(1,128)S(1)}, u32[]{:S(2)}, u32[]{:S(2)}) %all-to-all-start) | async-done | bytes 589856 | tf_op jit(solution)/shard_map/all_to_all | solution.py:229
  59.9 2.4 %fusion.position_ref = s32[128]{0:T(128)S(1)} fusion(f32[128,9,1,128]{3,2,1,0:T(1,128)S(1)} %all-to-all-done.arrived_ref), kind=kLoop, calls=%fused_computation.3 | loop fusion | flops 128 | bytes 1024 | tf_op jit(solution)/shard_map/convert_element_type | solution.py:230
  63.1 2.1 %collective-permute-start.2 = (f32[512,256]{1,0:T(8,128)S(1)}, f32[512,256]{1,0:T(8,128)S(1)}, u32[]{:S(2)}, u32[]{:S(2)}) collective-permute-start(f32[512,256]{1,0:T(8,128)S(1)} %unpack.1.s0), channel_id=1, source_target_pairs={{0,1},{1,2},{2,3},{3,0},{4,5},{5,6},{6,7},{7,4},{8,9},{9,10},{10,1... | collective-permute-start | bytes 1572872 | tf_op jit(solution)/shard_map/ppermute | solution.py:184
  65.2 4.5 %collective-permute-start.1 = (f32[512,256]{1,0:T(8,128)S(1)}, f32[512,256]{1,0:T(8,128)S(1)}, u32[]{:S(2)}, u32[]{:S(2)}) collective-permute-start(f32[512,256]{1,0:T(8,128)S(1)} %unpack.1.s0), channel_id=1, source_target_pairs={{0,2},{1,3},{2,0},{3,1},{4,6},{5,7},{6,4},{7,5},{8,10},{9,11},{10,... | collective-permute-start | bytes 1572872 | tf_op jit(solution)/shard_map/ppermute | solution.py:184
  69.7 1.9 %collective-permute-start = (f32[512,256]{1,0:T(8,128)S(1)}, f32[512,256]{1,0:T(8,128)S(1)}, u32[]{:S(2)}, u32[]{:S(2)}) collective-permute-start(f32[512,256]{1,0:T(8,128)S(1)} %unpack.1.s0), channel_id=1, source_target_pairs={{0,3},{1,0},{2,1},{3,2},{4,7},{5,4},{6,5},{7,6},{8,11},{9,8},{10,9... | collective-permute-start | bytes 1572872 | tf_op jit(solution)/shard_map/ppermute | solution.py:184
  72.9 6.9 %collective-permute-done.2.s3 = f32[512,256]{1,0:T(8,128)S(1)} collective-permute-done((f32[512,256]{1,0:T(8,128)S(1)}, f32[512,256]{1,0:T(8,128)S(1)}, u32[]{:S(2)}, u32[]{:S(2)}) %collective-permute-start.2) | collective-permute-done | bytes 524320 | tf_op jit(solution)/shard_map/ppermute | solution.py:184
  79.8 3.7 %collective-permute-done.1.s2 = f32[512,256]{1,0:T(8,128)S(1)} collective-permute-done((f32[512,256]{1,0:T(8,128)S(1)}, f32[512,256]{1,0:T(8,128)S(1)}, u32[]{:S(2)}, u32[]{:S(2)}) %collective-permute-start.1) | collective-permute-done | bytes 524320 | tf_op jit(solution)/shard_map/ppermute | solution.py:184
  83.5 9.2 %collective-permute-done.s1 = f32[512,256]{1,0:T(8,128)S(1)} collective-permute-done((f32[512,256]{1,0:T(8,128)S(1)}, f32[512,256]{1,0:T(8,128)S(1)}, u32[]{:S(2)}, u32[]{:S(2)}) %collective-permute-start) | collective-permute-done | bytes 524320 | tf_op jit(solution)/shard_map/ppermute | solution.py:184
  92.7 1.2 columns_of_class.1
  93.9 1.9 %collective-permute-start.3 = (f32[512,256]{1,0:T(8,128)S(1)}, f32[512,256]{1,0:T(8,128)S(1)}, u32[]{:S(2)}, u32[]{:S(2)}) collective-permute-start(f32[512,256]{1,0:T(8,128)S(1)} %get-tuple-element.17), channel_id=1, source_target_pairs={{0,4},{4,8},{8,12},{12,16},{16,20},{20,24},{24,28},{28,32},{32,36}... | collective-permute-start | bytes 1572872 | tf_op jit(solution)/shard_map/ppermute | solution.py:184
  95.8 7.0 %collective-permute-start.4 = (f32[512,256]{1,0:T(8,128)S(1)}, f32[512,256]{1,0:T(8,128)S(1)}, u32[]{:S(2)}, u32[]{:S(2)}) collective-permute-start(f32[512,256]{1,0:T(8,128)S(1)} %get-tuple-element.18), channel_id=1, source_target_pairs={{0,508},{4,0},{8,4},{12,8},{16,12},{20,16},{24,20},{28,24},{32,28}... | collective-permute-start | bytes 1572872 | tf_op jit(solution)/shard_map/ppermute | solution.py:184
  102.8 4.9 %collective-permute-done.3.from_left = f32[512,256]{1,0:T(8,128)S(1)} collective-permute-done((f32[512,256]{1,0:T(8,128)S(1)}, f32[512,256]{1,0:T(8,128)S(1)}, u32[]{:S(2)}, u32[]{:S(2)}) %collective-permute-start.3) | collective-permute-done | bytes 524320 | tf_op jit(solution)/shard_map/ppermute | solution.py:184
  107.7 1.8 %collective-permute-done.4.from_right = f32[512,256]{1,0:T(8,128)S(1)} collective-permute-done((f32[512,256]{1,0:T(8,128)S(1)}, f32[512,256]{1,0:T(8,128)S(1)}, u32[]{:S(2)}, u32[]{:S(2)}) %collective-permute-start.4) | collective-permute-done | bytes 524320 | tf_op jit(solution)/shard_map/ppermute | solution.py:184
  109.4 3.4 %square.1 = (f32[512,384]{1,0:T(8,128)S(1)}, f32[512,256]{1,0:T(8,128)S(1)}, f32[512,256]{1,0:T(8,128)S(1)}, f32[512,256]{1,0:T(8,128)S(1)}, f32[512,256]{1,0:T(...) custom-call(s32[480]{0:T(512)S(1)} %concatenate.11.table_ref, f32[512,256]{1,0:T(8,128)S(1)} %unpack.1.s0, ...), custom_call_target="tpu_custom_call" | custom-call | flops 1207959552 | bytes 8388608 | tf_op jit(solution)/shard_map/square/pallas_call | solution.py:259
  112.9 1.9 %collective-permute-start.8 = (f32[512,256]{1,0:T(8,128)S(1)}, f32[512,256]{1,0:T(8,128)S(1)}, u32[]{:S(2)}, u32[]{:S(2)}) collective-permute-start(f32[512,256]{1,0:T(8,128)S(1)} %get-tuple-element.24), channel_id=1, source_target_pairs={{0,4},{4,8},{8,12},{12,16},{16,20},{20,24},{24,28},{28,32},{32,36}... | collective-permute-start | bytes 1572872 | tf_op jit(solution)/shard_map/ppermute | solution.py:184
  114.8 7.1 %collective-permute-start.9 = (f32[512,256]{1,0:T(8,128)S(1)}, f32[512,256]{1,0:T(8,128)S(1)}, u32[]{:S(2)}, u32[]{:S(2)}) collective-permute-start(f32[512,256]{1,0:T(8,128)S(1)} %get-tuple-element.25), channel_id=1, source_target_pairs={{0,508},{4,0},{8,4},{12,8},{16,12},{20,16},{24,20},{28,24},{32,28}... | collective-permute-start | bytes 1572872 | tf_op jit(solution)/shard_map/ppermute | solution.py:184
  122.0 2.5 %collective-permute-start.5 = (f32[512,256]{1,0:T(8,128)S(1)}, f32[512,256]{1,0:T(8,128)S(1)}, u32[]{:S(2)}, u32[]{:S(2)}) collective-permute-start(f32[512,256]{1,0:T(8,128)S(1)} %get-tuple-element.20), channel_id=1, source_target_pairs={{0,1},{1,2},{2,3},{3,0},{4,5},{5,6},{6,7},{7,4},{8,9},{9,10},{10,1... | collective-permute-start | bytes 1572872 | tf_op jit(solution)/shard_map/ppermute | solution.py:184
  124.5 4.4 %collective-permute-start.6 = (f32[512,256]{1,0:T(8,128)S(1)}, f32[512,256]{1,0:T(8,128)S(1)}, u32[]{:S(2)}, u32[]{:S(2)}) collective-permute-start(f32[512,256]{1,0:T(8,128)S(1)} %get-tuple-element.21), channel_id=1, source_target_pairs={{0,2},{1,3},{2,0},{3,1},{4,6},{5,7},{6,4},{7,5},{8,10},{9,11},{10,... | collective-permute-start | bytes 1572872 | tf_op jit(solution)/shard_map/ppermute | solution.py:184
  128.9 2.9 %collective-permute-start.7 = (f32[512,256]{1,0:T(8,128)S(1)}, f32[512,256]{1,0:T(8,128)S(1)}, u32[]{:S(2)}, u32[]{:S(2)}) collective-permute-start(f32[512,256]{1,0:T(8,128)S(1)} %get-tuple-element.22), channel_id=1, source_target_pairs={{0,3},{1,0},{2,1},{3,2},{4,7},{5,4},{6,5},{7,6},{8,11},{9,8},{10,9... | collective-permute-start | bytes 1572872 | tf_op jit(solution)/shard_map/ppermute | solution.py:184
  131.8 3.5 %cubic.1 = (f32[512,256]{1,0:T(8,128)S(1)}, f32[512,256]{1,0:T(8,128)S(1)}, f32[512,256]{1,0:T(8,128)S(1)}, f32[512,256]{1,0:T(8,128)S(1)}) custom-call(s32[480]{0:T(512)S(1)} %concatenate.11.table_ref, f32[512,256]{1,0:T(8,128)S(1)} %unpack.1.s0, f32[512,256]{1,0:T(8,128)S(1)} %collective-permute-done.s1, f32[512,256]{1,0:T(8,128)S(1)} %collective-permute-done.1.s2, ...), custom_call_target="tpu_custom_call" | custom-call | flops 1207959552 | bytes 8388608 | tf_op jit(solution)/shard_map/cubic/pallas_call | solution.py:273
  135.3 4.3 %collective-permute-start.10 = (f32[512,256]{1,0:T(8,128)S(1)}, f32[512,256]{1,0:T(8,128)S(1)}, u32[]{:S(2)}, u32[]{:S(2)}) collective-permute-start(f32[512,256]{1,0:T(8,128)S(1)} %get-tuple-element.27), channel_id=1, source_target_pairs={{0,1},{1,2},{2,3},{3,0},{4,5},{5,6},{6,7},{7,4},{8,9},{9,10},{10,1... | collective-permute-start | bytes 1572872 | tf_op jit(solution)/shard_map/ppermute | solution.py:184
  139.6 1.9 %collective-permute-start.11 = (f32[512,256]{1,0:T(8,128)S(1)}, f32[512,256]{1,0:T(8,128)S(1)}, u32[]{:S(2)}, u32[]{:S(2)}) collective-permute-start(f32[512,256]{1,0:T(8,128)S(1)} %get-tuple-element.28), channel_id=1, source_target_pairs={{0,2},{1,3},{2,0},{3,1},{4,6},{5,7},{6,4},{7,5},{8,10},{9,11},{10,... | collective-permute-start | bytes 1572872 | tf_op jit(solution)/shard_map/ppermute | solution.py:184
  141.6 3.3 %collective-permute-start.12 = (f32[512,256]{1,0:T(8,128)S(1)}, f32[512,256]{1,0:T(8,128)S(1)}, u32[]{:S(2)}, u32[]{:S(2)}) collective-permute-start(f32[512,256]{1,0:T(8,128)S(1)} %get-tuple-element.29), channel_id=1, source_target_pairs={{0,3},{1,0},{2,1},{3,2},{4,7},{5,4},{6,5},{7,6},{8,11},{9,8},{10,9... | collective-permute-start | bytes 1572872 | tf_op jit(solution)/shard_map/ppermute | solution.py:184
  144.9 13.3 %collective-permute-done.7 = f32[512,256]{1,0:T(8,128)S(1)} collective-permute-done((f32[512,256]{1,0:T(8,128)S(1)}, f32[512,256]{1,0:T(8,128)S(1)}, u32[]{:S(2)}, u32[]{:S(2)}) %collective-permute-start.7) | collective-permute-done | bytes 524320 | tf_op jit(solution)/shard_map/ppermute | solution.py:184
  158.2 0.9 add_add_fusion.1
  159.1 2.0 %collective-permute-done.10 = f32[512,256]{1,0:T(8,128)S(1)} collective-permute-done((f32[512,256]{1,0:T(8,128)S(1)}, f32[512,256]{1,0:T(8,128)S(1)}, u32[]{:S(2)}, u32[]{:S(2)}) %collective-permute-start.10) | collective-permute-done | bytes 524320 | tf_op jit(solution)/shard_map/ppermute | solution.py:184
  161.1 3.8 %collective-permute-done.11 = f32[512,256]{1,0:T(8,128)S(1)} collective-permute-done((f32[512,256]{1,0:T(8,128)S(1)}, f32[512,256]{1,0:T(8,128)S(1)}, u32[]{:S(2)}, u32[]{:S(2)}) %collective-permute-start.11) | collective-permute-done | bytes 524320 | tf_op jit(solution)/shard_map/ppermute | solution.py:184
  164.9 5.5 %collective-permute-done.12 = f32[512,256]{1,0:T(8,128)S(1)} collective-permute-done((f32[512,256]{1,0:T(8,128)S(1)}, f32[512,256]{1,0:T(8,128)S(1)}, u32[]{:S(2)}, u32[]{:S(2)}) %collective-permute-start.12) | collective-permute-done | bytes 524320 | tf_op jit(solution)/shard_map/ppermute | solution.py:184
  170.4 0.9 add_add_fusion
  (27 shorter events, 3.7 us)
Async XLA Ops:
  0.6 1.0 copy-start
  1.7 0.7 copy-start.1
  4.1 55.9 %all-to-all-start = ((f32[128,9,1,128]{3,2,1,0:T(1,128)}), f32[128,9,1,128]{3,2,1,0:T(1,128)S(1)}, u32[]{:S(2)}, u32[]{:S(2)}) async-start(f32[128,9,1,128]{3,2,1,0:T(1,128)} %pack.1), calls=%async_computation | async-start | bytes 1179648 | tf_op jit(solution)/shard_map/all_to_all | solution.py:229
  63.1 16.8 %collective-permute-start.2 = (f32[512,256]{1,0:T(8,128)S(1)}, f32[512,256]{1,0:T(8,128)S(1)}, u32[]{:S(2)}, u32[]{:S(2)}) collective-permute-start(f32[512,256]{1,0:T(8,128)S(1)} %unpack.1.s0), channel_id=1, source_target_pairs={{0,1},{1,2},{2,3},{3,0},{4,5},{5,6},{6,7},{7,4},{8,9},{9,10},{10,1... | collective-permute-start | bytes 1572872 | tf_op jit(solution)/shard_map/ppermute | solution.py:184
  65.2 18.3 %collective-permute-start.1 = (f32[512,256]{1,0:T(8,128)S(1)}, f32[512,256]{1,0:T(8,128)S(1)}, u32[]{:S(2)}, u32[]{:S(2)}) collective-permute-start(f32[512,256]{1,0:T(8,128)S(1)} %unpack.1.s0), channel_id=1, source_target_pairs={{0,2},{1,3},{2,0},{3,1},{4,6},{5,7},{6,4},{7,5},{8,10},{9,11},{10,... | collective-permute-start | bytes 1572872 | tf_op jit(solution)/shard_map/ppermute | solution.py:184
  69.7 22.9 %collective-permute-start = (f32[512,256]{1,0:T(8,128)S(1)}, f32[512,256]{1,0:T(8,128)S(1)}, u32[]{:S(2)}, u32[]{:S(2)}) collective-permute-start(f32[512,256]{1,0:T(8,128)S(1)} %unpack.1.s0), channel_id=1, source_target_pairs={{0,3},{1,0},{2,1},{3,2},{4,7},{5,4},{6,5},{7,6},{8,11},{9,8},{10,9... | collective-permute-start | bytes 1572872 | tf_op jit(solution)/shard_map/ppermute | solution.py:184
  93.9 13.8 %collective-permute-start.3 = (f32[512,256]{1,0:T(8,128)S(1)}, f32[512,256]{1,0:T(8,128)S(1)}, u32[]{:S(2)}, u32[]{:S(2)}) collective-permute-start(f32[512,256]{1,0:T(8,128)S(1)} %get-tuple-element.17), channel_id=1, source_target_pairs={{0,4},{4,8},{8,12},{12,16},{16,20},{20,24},{24,28},{28,32},{32,36}... | collective-permute-start | bytes 1572872 | tf_op jit(solution)/shard_map/ppermute | solution.py:184
  95.8 13.6 %collective-permute-start.4 = (f32[512,256]{1,0:T(8,128)S(1)}, f32[512,256]{1,0:T(8,128)S(1)}, u32[]{:S(2)}, u32[]{:S(2)}) collective-permute-start(f32[512,256]{1,0:T(8,128)S(1)} %get-tuple-element.18), channel_id=1, source_target_pairs={{0,508},{4,0},{8,4},{12,8},{16,12},{20,16},{24,20},{28,24},{32,28}... | collective-permute-start | bytes 1572872 | tf_op jit(solution)/shard_map/ppermute | solution.py:184
  112.9 18.9 %collective-permute-start.8 = (f32[512,256]{1,0:T(8,128)S(1)}, f32[512,256]{1,0:T(8,128)S(1)}, u32[]{:S(2)}, u32[]{:S(2)}) collective-permute-start(f32[512,256]{1,0:T(8,128)S(1)} %get-tuple-element.24), channel_id=1, source_target_pairs={{0,4},{4,8},{8,12},{12,16},{16,20},{20,24},{24,28},{28,32},{32,36}... | collective-permute-start | bytes 1572872 | tf_op jit(solution)/shard_map/ppermute | solution.py:184
  114.8 17.0 %collective-permute-start.9 = (f32[512,256]{1,0:T(8,128)S(1)}, f32[512,256]{1,0:T(8,128)S(1)}, u32[]{:S(2)}, u32[]{:S(2)}) collective-permute-start(f32[512,256]{1,0:T(8,128)S(1)} %get-tuple-element.25), channel_id=1, source_target_pairs={{0,508},{4,0},{8,4},{12,8},{16,12},{20,16},{24,20},{28,24},{32,28}... | collective-permute-start | bytes 1572872 | tf_op jit(solution)/shard_map/ppermute | solution.py:184
  122.0 19.6 %collective-permute-start.5 = (f32[512,256]{1,0:T(8,128)S(1)}, f32[512,256]{1,0:T(8,128)S(1)}, u32[]{:S(2)}, u32[]{:S(2)}) collective-permute-start(f32[512,256]{1,0:T(8,128)S(1)} %get-tuple-element.20), channel_id=1, source_target_pairs={{0,1},{1,2},{2,3},{3,0},{4,5},{5,6},{6,7},{7,4},{8,9},{9,10},{10,1... | collective-permute-start | bytes 1572872 | tf_op jit(solution)/shard_map/ppermute | solution.py:184
  124.5 20.4 %collective-permute-start.6 = (f32[512,256]{1,0:T(8,128)S(1)}, f32[512,256]{1,0:T(8,128)S(1)}, u32[]{:S(2)}, u32[]{:S(2)}) collective-permute-start(f32[512,256]{1,0:T(8,128)S(1)} %get-tuple-element.21), channel_id=1, source_target_pairs={{0,2},{1,3},{2,0},{3,1},{4,6},{5,7},{6,4},{7,5},{8,10},{9,11},{10,... | collective-permute-start | bytes 1572872 | tf_op jit(solution)/shard_map/ppermute | solution.py:184
  128.9 29.3 %collective-permute-start.7 = (f32[512,256]{1,0:T(8,128)S(1)}, f32[512,256]{1,0:T(8,128)S(1)}, u32[]{:S(2)}, u32[]{:S(2)}) collective-permute-start(f32[512,256]{1,0:T(8,128)S(1)} %get-tuple-element.22), channel_id=1, source_target_pairs={{0,3},{1,0},{2,1},{3,2},{4,7},{5,4},{6,5},{7,6},{8,11},{9,8},{10,9... | collective-permute-start | bytes 1572872 | tf_op jit(solution)/shard_map/ppermute | solution.py:184
  135.3 25.7 %collective-permute-start.10 = (f32[512,256]{1,0:T(8,128)S(1)}, f32[512,256]{1,0:T(8,128)S(1)}, u32[]{:S(2)}, u32[]{:S(2)}) collective-permute-start(f32[512,256]{1,0:T(8,128)S(1)} %get-tuple-element.27), channel_id=1, source_target_pairs={{0,1},{1,2},{2,3},{3,0},{4,5},{5,6},{6,7},{7,4},{8,9},{9,10},{10,1... | collective-permute-start | bytes 1572872 | tf_op jit(solution)/shard_map/ppermute | solution.py:184
  139.6 25.2 %collective-permute-start.11 = (f32[512,256]{1,0:T(8,128)S(1)}, f32[512,256]{1,0:T(8,128)S(1)}, u32[]{:S(2)}, u32[]{:S(2)}) collective-permute-start(f32[512,256]{1,0:T(8,128)S(1)} %get-tuple-element.28), channel_id=1, source_target_pairs={{0,2},{1,3},{2,0},{3,1},{4,6},{5,7},{6,4},{7,5},{8,10},{9,11},{10,... | collective-permute-start | bytes 1572872 | tf_op jit(solution)/shard_map/ppermute | solution.py:184
  141.6 28.8 %collective-permute-start.12 = (f32[512,256]{1,0:T(8,128)S(1)}, f32[512,256]{1,0:T(8,128)S(1)}, u32[]{:S(2)}, u32[]{:S(2)}) collective-permute-start(f32[512,256]{1,0:T(8,128)S(1)} %get-tuple-element.29), channel_id=1, source_target_pairs={{0,3},{1,0},{2,1},{3,2},{4,7},{5,4},{6,5},{7,6},{8,11},{9,8},{10,9... | collective-permute-start | bytes 1572872 | tf_op jit(solution)/shard_map/ppermute | solution.py:184

commit v3 on v2

v3 whole, which is shorter than its diff:
```python
import functools

import jax
import jax.numpy as jnp
from jax import lax
from jax.experimental import pallas as pl
from jax.experimental.pallas import tpu as pltpu
from jax.sharding import PartitionSpec as P

BLOCK = 64
KNZ = 16
JNZ = 16
SLAB = 4
N_WIDE = 128
LAYERS = 4
OWN = 8
NBR = 1024
SLABS = 128
ROWS = OWN * BLOCK
WIDTH = 256
CLASS = 6
CLASS_COLS = CLASS * BLOCK
NEAR = 3 * OWN
HALF = 2 * BLOCK
KEPT = JNZ // LAYERS
MOST = OWN * KEPT
FIRST = 18
LATE = MOST - FIRST

AT_ROW = 0
AT_SLOT = AT_ROW + OWN * KNZ
AT_KEEP = AT_SLOT + OWN * CLASS
AT_SEND = AT_KEEP + OWN * CLASS
AT_PLACE = AT_SEND + LAYERS * OWN * KEPT
AT_LATE = AT_PLACE + OWN * KEPT

VMEM = pl.BlockSpec(memory_space=pltpu.VMEM)
SMEM = pl.BlockSpec(memory_space=pltpu.SMEM)
PARAMS = pltpu.CompilerParams(vmem_limit_bytes=24 * 1024 * 1024)


def cost(flops, bytes_accessed):
    return pl.CostEstimate(flops=flops, bytes_accessed=bytes_accessed, transcendentals=0)


def f32(*shape):
    return jax.ShapeDtypeStruct(shape, jnp.float32)


def pack_kernel(slot_ref, rows_ref, out_ref):
    low = lax.broadcasted_iota(jnp.int32, (8, 128), 0) < SLAB
    for pair in range(SLABS // 2):
        left = rows_ref[8 * pair : 8 * pair + 8, 0:128]
        right = rows_ref[8 * pair : 8 * pair + 8, 128:256]
        first = jnp.where(low, left, pltpu.roll(right, SLAB, 0))
        second = jnp.where(low, pltpu.roll(left, SLAB, 0), right)
        for which, tile in ((0, first), (1, second)):
            slot = slot_ref[2 * pair + which]
            target = slot >> 7
            out_ref[target, 0:8] = tile.reshape(8, 1, 128)
            out_ref[target, 8] = jnp.full((1, 128), (slot & 127).astype(jnp.float32))


def unpack_kernel(arrived_ref, rows_ref, tiles, places, *halves):
    for source in range(N_WIDE):
        tiles[8 * source : 8 * source + 8, :] = arrived_ref[source, 0:8].reshape(8, 128)
        places[source : source + 1, :] = arrived_ref[source, 8]
    order = lax.broadcasted_iota(jnp.int32, (SLABS, N_WIDE), 0).astype(jnp.float32)
    chosen = (jnp.transpose(places[...]) == order).astype(jnp.bfloat16)
    for row in range(8):
        rest = tiles[pl.ds(row, N_WIDE, stride=8), :]
        found = jnp.zeros((SLABS, 128), jnp.float32)
        for _ in range(3):
            part = rest.astype(jnp.bfloat16)
            rest = rest - part.astype(jnp.float32)
            found = found + jnp.dot(chosen, part, preferred_element_type=jnp.float32)
        half = row // SLAB
        halves[half][pl.ds(row % SLAB, SLABS, stride=SLAB), :] = found
    for half in range(2):
        rows_ref[:, half * 128 : (half + 1) * 128] = halves[half][...]


def pick(source, chunk, row, half, there, wanted, other=0.0):
    block = source[chunk, pl.ds(pl.multiple_of(row, BLOCK), BLOCK), :]
    return jnp.where(there, jnp.where(half == wanted, block, pltpu.roll(block, BLOCK, 1)), other)


def first_lanes():
    return lax.broadcasted_iota(jnp.int32, (BLOCK, HALF), 1) < BLOCK


def pack_blocks(table_ref, source, out_ref, at):
    first_half = first_lanes()

    def one(entry, wanted):
        there = entry >= 0
        place = entry & (OWN - 1)
        row = (jnp.maximum(entry, 0) >> 3) * BLOCK
        return pick(source, jnp.where(there, place >> 1, 0), row, place & 1, there, wanted)

    for pair in range(out_ref.shape[0] // BLOCK):
        block = jnp.where(first_half, one(table_ref[at + 2 * pair], 0), one(table_ref[at + 2 * pair + 1], 1))
        out_ref[pair * BLOCK : (pair + 1) * BLOCK, :] = block


def place_blocks(table_ref, source, out_ref, at, before=None):
    first_half = first_lanes()
    for i in range(OWN):
        rows = slice(i * BLOCK, (i + 1) * BLOCK)
        for c in range(KEPT // 2):
            cols = slice(c * HALF, (c + 1) * HALF)
            other = 0.0 if before is None else before[rows, cols]

            def one(entry, wanted):
                safe = jnp.maximum(entry, 0)
                return pick(source, 0, (safe >> 1) * BLOCK, safe & 1, entry >= 0, wanted, other)

            slot = at + i * KEPT + 2 * c
            out_ref[rows, cols] = jnp.where(first_half, one(table_ref[slot], 0), one(table_ref[slot + 1], 1))


def stack_blocks(parts, stacked):
    row = 0
    for part in parts:
        stacked[0, row : row + part.shape[0], :] = part[...]
        row += part.shape[0]


def place_kernel(table_ref, p0, p1, p2, p3, out_ref, stacked):
    stack_blocks((p0, p1, p2, p3), stacked)
    place_blocks(table_ref, stacked, out_ref, AT_PLACE)


def late_pack_kernel(table_ref, source_ref, o1, o2, o3, chunks):
    for q in range(CLASS // 2):
        chunks[q] = source_ref[:, q * HALF : (q + 1) * HALF]
    for r, out_ref in enumerate((o1, o2, o3)):
        pack_blocks(table_ref, chunks, out_ref, AT_SEND + (r + 1) * MOST + FIRST)


def late_place_kernel(table_ref, before_ref, p1, p2, p3, out_ref, stacked):
    stack_blocks((p1, p2, p3), stacked)
    place_blocks(table_ref, stacked, out_ref, AT_LATE, before_ref)


def class_kernel(table_ref, s0, s1, s2, s3, own_ref, to_right, to_left, chunks):
    for r, shard in enumerate((s0, s1, s2, s3)):
        chunks[2 * r] = shard[:, 0:128]
        chunks[2 * r + 1] = shard[:, 128:256]
    first_half = first_lanes()
    for i in range(OWN):
        rows = slice(i * BLOCK, (i + 1) * BLOCK)

        def one(slot, wanted):
            there = slot != KNZ
            safe = jnp.where(there, slot, 0)
            return pick(chunks, safe >> 1, i * BLOCK, safe & 1, there, wanted)

        for q in range(CLASS // 2):
            at = AT_SLOT + i * CLASS + 2 * q
            block = jnp.where(first_half, one(table_ref[at], 0), one(table_ref[at + 1], 1))
            own_ref[rows, q * 128 : (q + 1) * 128] = block
            if q > 0:
                to_right[rows, (q - 1) * 128 : q * 128] = block
            if q < 2:
                to_left[rows, q * 128 : (q + 1) * 128] = block


def split(x):
    high = x.astype(jnp.bfloat16)
    return high, (x - high.astype(jnp.float32)).astype(jnp.bfloat16)


def product(table_ref, shards, own_ref, from_left, from_right, right_high, right_low, finish):
    empty = jnp.zeros((ROWS, 128), jnp.bfloat16)
    for source, row, col in ((from_left, 0, 0), (own_ref, ROWS, 0), (from_right, 2 * ROWS, 128)):
        width = source.shape[1]
        high, low = split(source[...])
        right_high[row : row + ROWS, col : col + width] = high
        right_low[row : row + ROWS, col : col + width] = low
    for store in (right_high, right_low):
        store[0:ROWS, WIDTH:CLASS_COLS] = empty
        store[2 * ROWS : 3 * ROWS, 0:128] = empty
    dot = functools.partial(jnp.dot, preferred_element_type=jnp.float32)
    for i in range(OWN):
        rows = slice(i * BLOCK, (i + 1) * BLOCK)
        total = jnp.zeros((BLOCK, CLASS_COLS), jnp.float32)
        for r, shard in enumerate(shards):
            high, low = split(shard[rows, :])
            places = [
                pl.ds(pl.multiple_of(table_ref[AT_ROW + i * KNZ + 4 * r + k] * BLOCK, BLOCK), BLOCK)
                for k in range(KNZ // LAYERS)
            ]
            weight_high = jnp.concatenate([right_high[p, :] for p in places], axis=0)
            weight_low = jnp.concatenate([right_low[p, :] for p in places], axis=0)
            both = dot(jnp.concatenate([high, low], axis=0), weight_high)
            total = total + both[:BLOCK] + both[BLOCK:] + dot(high, weight_low)
        finish(i, rows, total)


def square_kernel(
    table_ref, s0, s1, s2, s3, own_ref, from_left, from_right, square_ref, to_right, to_left, o0, o1, o2, o3, right_high, right_low, chunks
):
    first_half = first_lanes()

    def finish(i, rows, total):
        for q in range(CLASS // 2):
            at = AT_KEEP + i * CLASS + 2 * q
            keep = jnp.where(first_half, table_ref[at], table_ref[at + 1]) != 0
            block = jnp.where(keep, total[:, q * 128 : (q + 1) * 128], 0.0)
            chunks[q, rows, :] = block
            square_ref[rows, q * 128 : (q + 1) * 128] = block
            if q > 0:
                to_right[rows, (q - 1) * 128 : q * 128] = block
            if q < 2:
                to_left[rows, q * 128 : (q + 1) * 128] = block

    product(table_ref, (s0, s1, s2, s3), own_ref, from_left, from_right, right_high, right_low, finish)
    for r, out_ref in enumerate((o0, o1, o2, o3)):
        pack_blocks(table_ref, chunks, out_ref, AT_SEND + r * MOST)


def cubic_kernel(
    table_ref, s0, s1, s2, s3, own_ref, from_left, from_right, keep_ref, step_ref, o0, o1, o2, o3, right_high, right_low, chunks
):

    def finish(i, rows, total):
        for q in range(CLASS // 2):
            cols = slice(q * 128, (q + 1) * 128)
            block = 1.5 * keep_ref[rows, cols] - 0.5 * total[:, cols]
            chunks[q, rows, :] = block
            step_ref[rows, cols] = block

    product(table_ref, (s0, s1, s2, s3), own_ref, from_left, from_right, right_high, right_low, finish)
    for r, out_ref in enumerate((o0, o1, o2, o3)):
        pack_blocks(table_ref, chunks, out_ref, AT_SEND + r * MOST)


RIGHT = [
    pltpu.VMEM((NEAR * BLOCK, CLASS_COLS), jnp.bfloat16),
    pltpu.VMEM((NEAR * BLOCK, CLASS_COLS), jnp.bfloat16),
    pltpu.VMEM((CLASS // 2, ROWS, HALF), jnp.float32),
]


def shift(x, axis, by):
    count = lax.axis_size(axis)
    return lax.ppermute(x, axis, [(i, (i + by) % count) for i in range(count)])


def call(kernel, name, outs, *operands, scratch=(), size=1 << 20, flops=0, scalars=1):
    single = not isinstance(outs, tuple)
    return pl.pallas_call(
        kernel,
        out_shape=outs,
        in_specs=[SMEM] * scalars + [VMEM] * (len(operands) - scalars),
        out_specs=VMEM if single else (VMEM,) * len(outs),
        scratch_shapes=list(scratch),
        compiler_params=PARAMS,
        cost_estimate=cost(flops, size),
        name=name,
    )(*operands)


def blocks(count):
    return f32(count // 2 * BLOCK, HALF)


def send_parts(parts):
    return tuple(shift(part, "narrow", r + 1) for r, part in enumerate(parts))


def place(table, own, parts):
    stacked = pltpu.VMEM((1, (MOST + 3 * FIRST) // 2 * BLOCK, HALF), jnp.float32)
    return call(place_kernel, "place_blocks", f32(ROWS, WIDTH), table, own, *parts, scratch=(stacked,))


def place_late(table, before, source):
    chunks = pltpu.VMEM((CLASS // 2, ROWS, HALF), jnp.float32)
    parts = call(late_pack_kernel, "late_blocks", (blocks(LATE),) * 3, table, source, scratch=(chunks,))
    stacked = pltpu.VMEM((1, 3 * LATE // 2 * BLOCK, HALF), jnp.float32)
    return call(late_place_kernel, "place_late_blocks", f32(ROWS, WIDTH), table, before, *send_parts(parts), scratch=(stacked,))


def any_late(filter_cols):
    ones = jnp.left_shift(1, 8 * (filter_cols & (LAYERS - 1)))
    counts = jnp.sum(ones.reshape(N_WIDE, OWN, LAYERS, KEPT), axis=(1, 3))
    layers = jnp.arange(LAYERS, dtype=jnp.int32)
    each = (counts[:, :, None] >> (8 * layers)) & 255
    return jnp.max(jnp.where(layers[:, None] == layers, 0, each)) > FIRST


def tables(block_cols, filter_cols, wide_index, layer):
    first_row = wide_index * OWN
    base = first_row - OWN

    def own(cols):
        mine = lax.dynamic_slice_in_dim(cols, first_row, OWN, 0)
        mine = (mine - base) & (NBR - 1)
        turned = lax.dynamic_slice_in_dim(jnp.concatenate([mine, mine], axis=1), layer * (KNZ // LAYERS), KNZ, 1)
        return mine, turned

    _, cols = own(block_cols)
    kept, kept_turned = own(filter_cols)
    places = layer + LAYERS * jnp.arange(CLASS, dtype=jnp.int32)
    slots = jnp.arange(KNZ, dtype=jnp.int32)
    slot = jnp.min(jnp.where(cols[:, None, :] == places[None, :, None], slots, KNZ), axis=2)
    keep = jnp.max((kept[:, None, :] == places[None, :, None]).astype(jnp.int32), axis=2)

    wanted = kept_turned.reshape(OWN, LAYERS, KEPT).transpose(1, 0, 2).reshape(LAYERS, MOST)
    here = (wanted & (LAYERS - 1)) == layer
    order = jnp.arange(MOST, dtype=jnp.int32)
    earlier = order[None, :] < order[:, None]
    rank = jnp.sum((here[:, None, :] & earlier).astype(jnp.int32), axis=2)
    code = (order >> 2) * OWN + ((wanted - layer) >> 2)
    chosen = here[:, None, :] & (rank[:, None, :] == order[None, :, None])
    send = jnp.max(jnp.where(chosen, code[:, None, :], -1), axis=2)
    group = wanted[0] & (LAYERS - 1)
    source = (layer - group) & (LAYERS - 1)
    place = jnp.sum(((group[None, :] == group[:, None]) & earlier).astype(jnp.int32), axis=1)
    mine = source == 0
    first = jnp.where(mine, place, MOST + FIRST * (source - 1) + place)
    late = jnp.logical_not(mine) & (place >= FIRST)
    first = jnp.where(late, -1, first)
    late = jnp.where(late, LATE * (source - 1) + place - FIRST, -1)
    return jnp.concatenate([part.reshape(-1) for part in (cols, slot, keep, send, first, late)])


def local(restart, slab_slot, block_cols, filter_cols):
    wide_index = lax.axis_index("wide")
    layer = lax.axis_index("narrow")
    table, late = lax.optimization_barrier((tables(block_cols, filter_cols, wide_index, layer), any_late(filter_cols)))

    packed = call(pack_kernel, "pack", f32(N_WIDE, 9, 1, 128), slab_slot, restart)
    arrived = lax.all_to_all(packed, "wide", split_axis=0, concat_axis=0, tiled=True)
    scratch = (pltpu.VMEM((8 * N_WIDE, 128), jnp.float32), pltpu.VMEM((N_WIDE, 128), jnp.float32)) + (pltpu.VMEM((ROWS, 128), jnp.float32),) * 2
    mine = call(unpack_kernel, "unpack", f32(ROWS, WIDTH), arrived, scratch=scratch, scalars=0)
    shards = (mine, shift(mine, "narrow", -1), shift(mine, "narrow", -2), shift(mine, "narrow", -3))

    half = f32(ROWS, WIDTH)
    whole = f32(ROWS, CLASS_COLS)
    sent = (blocks(MOST), blocks(FIRST), blocks(FIRST), blocks(FIRST))
    flops = 2 * 3 * ROWS * KNZ * BLOCK * CLASS_COLS
    chunks = pltpu.VMEM((2 * LAYERS, ROWS, HALF), jnp.float32)
    own, to_right, to_left = call(class_kernel, "columns_of_class", (whole, half, half), table, *shards, scratch=(chunks,), size=4 << 20)
    from_left = shift(to_right, "wide", 1)
    from_right = shift(to_left, "wide", -1)

    square, to_right, to_left, *parts = call(
        square_kernel, "square", (whole, half, half) + sent, table, *shards, own, from_left, from_right,
        scratch=RIGHT, size=8 << 20, flops=flops,
    )
    from_left = shift(to_right, "wide", 1)
    from_right = shift(to_left, "wide", -1)
    squared = place(table, parts[0], send_parts(parts[1:]))

    step, *parts = call(
        cubic_kernel, "cubic", (whole,) + sent, table, *shards, square, from_left, from_right, own,
        scratch=RIGHT, size=8 << 20, flops=flops,
    )
    updated = place(table, parts[0], send_parts(parts[1:]))

    def with_late(state):
        _, squared, updated = state
        return jnp.zeros((), bool), place_late(table, squared, square), place_late(table, updated, step)

    return lax.while_loop(lambda state: state[0], with_late, (late, squared, updated))[1:]


def solution(mesh):
    placed = (P("wide", "narrow"), P("wide"), P(), P())
    return jax.shard_map(
        local,
        mesh=mesh,
        in_specs=placed,
        out_specs=(P("wide", "narrow"), P("wide", "narrow")),
        check_vma=False,
    )
```

time: 173 us -> 154 us (0.89)
  waiting for transfers between devices: 86.1 us -> 64.7 us
  Pallas kernels: 10.6 us -> 15.1 us
  other arithmetic: 4.81 us -> 1.93 us
    ppermute x13, waiting for transfers between devices: 51.1 us -> 32.5 us  [shift(): return lax.ppermute(x, axis, [(i, (i + by) % count) for i in range(count)])]
    pallas_call x5 -> x7, Pallas kernels: 10.6 us -> 15.1 us  [call(): pl.pallas_call(kernel, out_shape=outs, in_specs=[SMEM] * scalars + [VMEM]...]
    all_to_all x1, waiting for transfers between devices: 35 us -> 32.2 us  [local(): lax.all_to_all(packed, 'wide', split_axis=0, concat_axis=0, tiled=True)]
    convert_element_type x1 -> x0, other arithmetic: 2.35 us -> none  [local(): position = arrived[:, 8, 0, 0].astype(jnp.int32)]
    add x2 -> x1, other arithmetic: 1.86 us -> 0.01 us  [tables(): code = (order >> 2) * OWN + (wanted - layer >> 2)]
  transfers between devices with their start and end apart: 14 -> 14, of which waited for: 10 -> 9; matrix products, arithmetic and copies ran while one was open for 2% -> 3% of each run, Pallas kernels for 2% -> 4%
where the time goes in v3:
time: 154 us; the launch traced here: 153 us
  starting transfers between devices  65.6 us (43%)
  waiting for transfers between devices  64.7 us (42%)
  Pallas kernels  15.1 us (10%)
  local copies, waits for them, and re-layouts  4.53 us (3%)
  other arithmetic  1.93 us (1%)
  between operations  1.58 us (1%)
    ppermute x13, starting transfers between devices, shift(): return lax.ppermute(x, axis, [(i, (i + by) % count) for i in range(count)])  45.7 us
    ppermute x13, waiting for transfers between devices, shift(): return lax.ppermute(x, axis, [(i, (i + by) % count) for i in range(count)])  32.5 us
    all_to_all x1, waiting for transfers between devices, local(): lax.all_to_all(packed, 'wide', split_axis=0, concat_axis=0, tiled=True)  32.2 us
    all_to_all x1, starting transfers between devices, local(): lax.all_to_all(packed, 'wide', split_axis=0, concat_axis=0, tiled=True)  19.9 us
    pallas_call x7, Pallas kernels, call(): pl.pallas_call(kernel, out_shape=outs, in_specs=[SMEM] * scalars + [VMEM]...  15.1 us
  transfers between devices with their start and end apart: 14, of which 9 were waited for; matrix products, arithmetic and copies ran while one was open for 3% of the time, Pallas kernels for 4%

profile of v3, /device:TPU:24, one launch (start us, length us, event | category | flops | bytes accessed | tf_op | source)
XLA Modules:
  0.0 153.5 jit_solution(13495556461287252524)
XLA Ops:
  0.6 1.0 copy-done
  2.3 1.7 %pack.1 = f32[128,9,1,128]{3,2,1,0:T(1,128)} custom-call(s32[128]{0:T(128)S(1)} %copy-done.1, f32[512,256]{1,0:T(8,128)S(1)} %copy-done), custom_call_target="tpu_custom_call" | custom-call | bytes 1048576 | tf_op jit(solution)/shard_map/pack/pallas_call | solution.py:253
  4.1 19.9 %all-to-all-start = ((f32[128,9,1,128]{3,2,1,0:T(1,128)}), f32[128,9,1,128]{3,2,1,0:T(1,128)S(1)}, u32[]{:S(2)}, u32[]{:S(2)}) async-start(f32[128,9,1,128]{3,2,1,0:T(1,128)} %pack.1), calls=%async_computation | async-start | bytes 1179648 | tf_op jit(solution)/shard_map/all_to_all | solution.py:335
  24.0 0.8 constant_dynamic-slice_fusion.1
  27.9 32.2 %all-to-all-done.arrived_ref = f32[128,9,1,128]{3,2,1,0:T(1,128)S(1)} async-done(((f32[128,9,1,128]{3,2,1,0:T(1,128)}), f32[128,9,1,128]{3,2,1,0:T(1,128)S(1)}, u32[]{:S(2)}, u32[]{:S(2)}) %all-to-all-start) | async-done | bytes 589856 | tf_op jit(solution)/shard_map/all_to_all | solution.py:335
  60.1 0.7 unpack.1.s0
  60.7 2.1 %collective-permute-start.8 = (f32[512,256]{1,0:T(8,128)S(1)}, f32[512,256]{1,0:T(8,128)S(1)}, u32[]{:S(2)}, u32[]{:S(2)}) collective-permute-start(f32[512,256]{1,0:T(8,128)S(1)} %unpack.1.s0), channel_id=1, source_target_pairs={{0,1},{1,2},{2,3},{3,0},{4,5},{5,6},{6,7},{7,4},{8,9},{9,10},{10,1... | collective-permute-start | bytes 1572872 | tf_op jit(solution)/shard_map/ppermute | solution.py:248
  62.9 4.5 %collective-permute-start.7 = (f32[512,256]{1,0:T(8,128)S(1)}, f32[512,256]{1,0:T(8,128)S(1)}, u32[]{:S(2)}, u32[]{:S(2)}) collective-permute-start(f32[512,256]{1,0:T(8,128)S(1)} %unpack.1.s0), channel_id=1, source_target_pairs={{0,2},{1,3},{2,0},{3,1},{4,6},{5,7},{6,4},{7,5},{8,10},{9,11},{10,... | collective-permute-start | bytes 1572872 | tf_op jit(solution)/shard_map/ppermute | solution.py:248
  67.4 1.9 %collective-permute-start.6 = (f32[512,256]{1,0:T(8,128)S(1)}, f32[512,256]{1,0:T(8,128)S(1)}, u32[]{:S(2)}, u32[]{:S(2)}) collective-permute-start(f32[512,256]{1,0:T(8,128)S(1)} %unpack.1.s0), channel_id=1, source_target_pairs={{0,3},{1,0},{2,1},{3,2},{4,7},{5,4},{6,5},{7,6},{8,11},{9,8},{10,9... | collective-permute-start | bytes 1572872 | tf_op jit(solution)/shard_map/ppermute | solution.py:248
  69.3 0.7 select_reduce_fusion.2
  71.0 6.5 %collective-permute-done.8.s3 = f32[512,256]{1,0:T(8,128)S(1)} collective-permute-done((f32[512,256]{1,0:T(8,128)S(1)}, f32[512,256]{1,0:T(8,128)S(1)}, u32[]{:S(2)}, u32[]{:S(2)}) %collective-permute-start.8) | collective-permute-done | bytes 524320 | tf_op jit(solution)/shard_map/ppermute | solution.py:248
  77.5 3.7 %collective-permute-done.7.s2 = f32[512,256]{1,0:T(8,128)S(1)} collective-permute-done((f32[512,256]{1,0:T(8,128)S(1)}, f32[512,256]{1,0:T(8,128)S(1)}, u32[]{:S(2)}, u32[]{:S(2)}) %collective-permute-start.7) | collective-permute-done | bytes 524320 | tf_op jit(solution)/shard_map/ppermute | solution.py:248
  81.2 9.1 %collective-permute-done.6.s1 = f32[512,256]{1,0:T(8,128)S(1)} collective-permute-done((f32[512,256]{1,0:T(8,128)S(1)}, f32[512,256]{1,0:T(8,128)S(1)}, u32[]{:S(2)}, u32[]{:S(2)}) %collective-permute-start.6) | collective-permute-done | bytes 524320 | tf_op jit(solution)/shard_map/ppermute | solution.py:248
  90.3 1.2 columns_of_class.1
  91.5 1.9 %collective-permute-start.9 = (f32[512,256]{1,0:T(8,128)S(1)}, f32[512,256]{1,0:T(8,128)S(1)}, u32[]{:S(2)}, u32[]{:S(2)}) collective-permute-start(f32[512,256]{1,0:T(8,128)S(1)} %get-tuple-element.60), channel_id=1, source_target_pairs={{0,4},{4,8},{8,12},{12,16},{16,20},{20,24},{24,28},{28,32},{32,36}... | collective-permute-start | bytes 1572872 | tf_op jit(solution)/shard_map/ppermute | solution.py:248
  93.4 7.0 %collective-permute-start.10 = (f32[512,256]{1,0:T(8,128)S(1)}, f32[512,256]{1,0:T(8,128)S(1)}, u32[]{:S(2)}, u32[]{:S(2)}) collective-permute-start(f32[512,256]{1,0:T(8,128)S(1)} %get-tuple-element.61), channel_id=1, source_target_pairs={{0,508},{4,0},{8,4},{12,8},{16,12},{20,16},{24,20},{28,24},{32,28}... | collective-permute-start | bytes 1572872 | tf_op jit(solution)/shard_map/ppermute | solution.py:248
  100.4 4.9 %collective-permute-done.9.from_left = f32[512,256]{1,0:T(8,128)S(1)} collective-permute-done((f32[512,256]{1,0:T(8,128)S(1)}, f32[512,256]{1,0:T(8,128)S(1)}, u32[]{:S(2)}, u32[]{:S(2)}) %collective-permute-start.9) | collective-permute-done | bytes 524320 | tf_op jit(solution)/shard_map/ppermute | solution.py:248
  105.3 1.8 %collective-permute-done.10.from_right = f32[512,256]{1,0:T(8,128)S(1)} collective-permute-done((f32[512,256]{1,0:T(8,128)S(1)}, f32[512,256]{1,0:T(8,128)S(1)}, u32[]{:S(2)}, u32[]{:S(2)}) %collective-permute-start.10) | collective-permute-done | bytes 524320 | tf_op jit(solution)/shard_map/ppermute | solution.py:248
  107.1 4.0 %square.1 = (f32[512,384]{1,0:T(8,128)S(1)}, f32[512,256]{1,0:T(8,128)S(1)}, f32[512,256]{1,0:T(8,128)S(1)}, f32[1024,128]{1,0:T(8,128)S(1)}, f32[576,128]{1,0:T...) custom-call(s32[416]{0:T(512)S(1)} %concatenate.11.table_ref, f32[512,256]{1,0:T(8,128)S(1)} %unpack.1.s0, ...), custom_call_target="tpu_custom_call" | custom-call | flops 1207959552 | bytes 8388608 | tf_op jit(solution)/shard_map/square/pallas_call | solution.py:253
  111.1 1.9 %collective-permute-start.14 = (f32[512,256]{1,0:T(8,128)S(1)}, f32[512,256]{1,0:T(8,128)S(1)}, u32[]{:S(2)}, u32[]{:S(2)}) collective-permute-start(f32[512,256]{1,0:T(8,128)S(1)} %get-tuple-element.67), channel_id=1, source_target_pairs={{0,4},{4,8},{8,12},{12,16},{16,20},{20,24},{24,28},{28,32},{32,36}... | collective-permute-start | bytes 1572872 | tf_op jit(solution)/shard_map/ppermute | solution.py:248
  113.0 7.1 %collective-permute-start.15 = (f32[512,256]{1,0:T(8,128)S(1)}, f32[512,256]{1,0:T(8,128)S(1)}, u32[]{:S(2)}, u32[]{:S(2)}) collective-permute-start(f32[512,256]{1,0:T(8,128)S(1)} %get-tuple-element.68), channel_id=1, source_target_pairs={{0,508},{4,0},{8,4},{12,8},{16,12},{20,16},{24,20},{28,24},{32,28}... | collective-permute-start | bytes 1572872 | tf_op jit(solution)/shard_map/ppermute | solution.py:248
  120.2 2.5 %collective-permute-start.11 = (f32[576,128]{1,0:T(8,128)S(1)}, f32[576,128]{1,0:T(8,128)S(1)}, u32[]{:S(2)}, u32[]{:S(2)}) collective-permute-start(f32[576,128]{1,0:T(8,128)S(1)} %get-tuple-element.63), channel_id=1, source_target_pairs={{0,1},{1,2},{2,3},{3,0},{4,5},{5,6},{6,7},{7,4},{8,9},{9,10},{10,1... | collective-permute-start | bytes 884744 | tf_op jit(solution)/shard_map/ppermute | solution.py:248
  122.7 4.4 %collective-permute-start.12 = (f32[576,128]{1,0:T(8,128)S(1)}, f32[576,128]{1,0:T(8,128)S(1)}, u32[]{:S(2)}, u32[]{:S(2)}) collective-permute-start(f32[576,128]{1,0:T(8,128)S(1)} %get-tuple-element.64), channel_id=1, source_target_pairs={{0,2},{1,3},{2,0},{3,1},{4,6},{5,7},{6,4},{7,5},{8,10},{9,11},{10,... | collective-permute-start | bytes 884744 | tf_op jit(solution)/shard_map/ppermute | solution.py:248
  127.1 2.9 %collective-permute-start.13 = (f32[576,128]{1,0:T(8,128)S(1)}, f32[576,128]{1,0:T(8,128)S(1)}, u32[]{:S(2)}, u32[]{:S(2)}) collective-permute-start(f32[576,128]{1,0:T(8,128)S(1)} %get-tuple-element.65), channel_id=1, source_target_pairs={{0,3},{1,0},{2,1},{3,2},{4,7},{5,4},{6,5},{7,6},{8,11},{9,8},{10,9... | collective-permute-start | bytes 884744 | tf_op jit(solution)/shard_map/ppermute | solution.py:248
  130.0 4.0 %cubic.1 = (f32[512,384]{1,0:T(8,128)S(1)}, f32[1024,128]{1,0:T(8,128)S(1)}, f32[576,128]{1,0:T(8,128)S(1)}, f32[576,128]{1,0:T(8,128)S(1)}, f32[576,128]{1,0:T(8,128)S(1)}) custom-call(s32[416]{0:T(512)S(1)} %concatenate.11.table_ref, f32[512,256]{1,0:T(8,128)S(1)} %unpack.1.s0, f32[512,256]{1,0:T(8,128)S(1)} %collective-permute-done.6.s1, ...), custom_call_target="tpu_custom_call" | custom-call | flops 1207959552 | bytes 8388608 | tf_op jit(solution)/shard_map/cubic/pallas_call | solution.py:253
  134.1 4.3 %collective-permute-start.16 = (f32[576,128]{1,0:T(8,128)S(1)}, f32[576,128]{1,0:T(8,128)S(1)}, u32[]{:S(2)}, u32[]{:S(2)}) collective-permute-start(f32[576,128]{1,0:T(8,128)S(1)} %get-tuple-element.70), channel_id=1, source_target_pairs={{0,1},{1,2},{2,3},{3,0},{4,5},{5,6},{6,7},{7,4},{8,9},{9,10},{10,1... | collective-permute-start | bytes 884744 | tf_op jit(solution)/shard_map/ppermute | solution.py:248
  138.4 1.9 %collective-permute-start.17 = (f32[576,128]{1,0:T(8,128)S(1)}, f32[576,128]{1,0:T(8,128)S(1)}, u32[]{:S(2)}, u32[]{:S(2)}) collective-permute-start(f32[576,128]{1,0:T(8,128)S(1)} %get-tuple-element.71), channel_id=1, source_target_pairs={{0,2},{1,3},{2,0},{3,1},{4,6},{5,7},{6,4},{7,5},{8,10},{9,11},{10,... | collective-permute-start | bytes 884744 | tf_op jit(solution)/shard_map/ppermute | solution.py:248
  140.3 3.1 %collective-permute-start.18 = (f32[576,128]{1,0:T(8,128)S(1)}, f32[576,128]{1,0:T(8,128)S(1)}, u32[]{:S(2)}, u32[]{:S(2)}) collective-permute-start(f32[576,128]{1,0:T(8,128)S(1)} %get-tuple-element.72), channel_id=1, source_target_pairs={{0,3},{1,0},{2,1},{3,2},{4,7},{5,4},{6,5},{7,6},{8,11},{9,8},{10,9... | collective-permute-start | bytes 884744 | tf_op jit(solution)/shard_map/ppermute | solution.py:248
  143.5 1.8 %place_blocks.2 = f32[512,256]{1,0:T(8,128)} custom-call(s32[416]{0:T(512)S(1)} %concatenate.11.table_ref, f32[1024,128]{1,0:T(8,128)S(1)} %get-tuple-element.62.p0, f32[576,128]{1,0:T(8,128)S(1)} %collective-permute-done.11.p1, f32[576,128]{1,0:T(8,128)S(1)} %collective-permute-done.12.p2, f32[576,128]{1,0:T(8,128)S(1)} %collective-permute-done.13.p3), custom_call_target="tpu_custom_call" | custom-call | bytes 1048576 | tf_op jit(solution)/shard_map/place_blocks/pallas_call | solution.py:253
  145.8 2.8 %collective-permute-done.17.p2 = f32[576,128]{1,0:T(8,128)S(1)} collective-permute-done((f32[576,128]{1,0:T(8,128)S(1)}, f32[576,128]{1,0:T(8,128)S(1)}, u32[]{:S(2)}, u32[]{:S(2)}) %collective-permute-start.17) | collective-permute-done | bytes 294944 | tf_op jit(solution)/shard_map/ppermute | solution.py:248
  148.6 3.1 %collective-permute-done.18.p3 = f32[576,128]{1,0:T(8,128)S(1)} collective-permute-done((f32[576,128]{1,0:T(8,128)S(1)}, f32[576,128]{1,0:T(8,128)S(1)}, u32[]{:S(2)}, u32[]{:S(2)}) %collective-permute-start.18) | collective-permute-done | bytes 294944 | tf_op jit(solution)/shard_map/ppermute | solution.py:248
  151.7 1.8 %place_blocks.3 = f32[512,256]{1,0:T(8,128)} custom-call(s32[416]{0:T(512)S(1)} %concatenate.11.table_ref, f32[1024,128]{1,0:T(8,128)S(1)} %get-tuple-element.69.p0, f32[576,128]{1,0:T(8,128)S(1)} %collective-permute-done.16.p1, f32[576,128]{1,0:T(8,128)S(1)} %collective-permute-done.17.p2, f32[576,128]{1,0:T(8,128)S(1)} %collective-permute-done.18.p3), custom_call_target="tpu_custom_call" | custom-call | bytes 1048576 | tf_op jit(solution)/shard_map/place_blocks/pallas_call | solution.py:253
  (51 shorter events, 4.5 us)
Async XLA Ops:
  0.6 1.0 copy-start
  1.7 0.7 copy-start.1
  4.1 19.9 %copy-start.5 = (s32[1024,16]{0,1:T(8,128)S(1)}, s32[1024,16]{0,1:T(8,128)}, u32[]{:S(2)}) copy-start(s32[1024,16]{0,1:T(8,128)} %param.9) | copy-start | bytes 196612
  4.1 56.0 %all-to-all-start = ((f32[128,9,1,128]{3,2,1,0:T(1,128)}), f32[128,9,1,128]{3,2,1,0:T(1,128)S(1)}, u32[]{:S(2)}, u32[]{:S(2)}) async-start(f32[128,9,1,128]{3,2,1,0:T(1,128)} %pack.1), calls=%async_computation | async-start | bytes 1179648 | tf_op jit(solution)/shard_map/all_to_all | solution.py:335
  60.7 16.8 %collective-permute-start.8 = (f32[512,256]{1,0:T(8,128)S(1)}, f32[512,256]{1,0:T(8,128)S(1)}, u32[]{:S(2)}, u32[]{:S(2)}) collective-permute-start(f32[512,256]{1,0:T(8,128)S(1)} %unpack.1.s0), channel_id=1, source_target_pairs={{0,1},{1,2},{2,3},{3,0},{4,5},{5,6},{6,7},{7,4},{8,9},{9,10},{10,1... | collective-permute-start | bytes 1572872 | tf_op jit(solution)/shard_map/ppermute | solution.py:248
  62.9 18.3 %collective-permute-start.7 = (f32[512,256]{1,0:T(8,128)S(1)}, f32[512,256]{1,0:T(8,128)S(1)}, u32[]{:S(2)}, u32[]{:S(2)}) collective-permute-start(f32[512,256]{1,0:T(8,128)S(1)} %unpack.1.s0), channel_id=1, source_target_pairs={{0,2},{1,3},{2,0},{3,1},{4,6},{5,7},{6,4},{7,5},{8,10},{9,11},{10,... | collective-permute-start | bytes 1572872 | tf_op jit(solution)/shard_map/ppermute | solution.py:248
  67.4 23.0 %collective-permute-start.6 = (f32[512,256]{1,0:T(8,128)S(1)}, f32[512,256]{1,0:T(8,128)S(1)}, u32[]{:S(2)}, u32[]{:S(2)}) collective-permute-start(f32[512,256]{1,0:T(8,128)S(1)} %unpack.1.s0), channel_id=1, source_target_pairs={{0,3},{1,0},{2,1},{3,2},{4,7},{5,4},{6,5},{7,6},{8,11},{9,8},{10,9... | collective-permute-start | bytes 1572872 | tf_op jit(solution)/shard_map/ppermute | solution.py:248
  91.5 13.8 %collective-permute-start.9 = (f32[512,256]{1,0:T(8,128)S(1)}, f32[512,256]{1,0:T(8,128)S(1)}, u32[]{:S(2)}, u32[]{:S(2)}) collective-permute-start(f32[512,256]{1,0:T(8,128)S(1)} %get-tuple-element.60), channel_id=1, source_target_pairs={{0,4},{4,8},{8,12},{12,16},{16,20},{20,24},{24,28},{28,32},{32,36}... | collective-permute-start | bytes 1572872 | tf_op jit(solution)/shard_map/ppermute | solution.py:248
  93.4 13.6 %collective-permute-start.10 = (f32[512,256]{1,0:T(8,128)S(1)}, f32[512,256]{1,0:T(8,128)S(1)}, u32[]{:S(2)}, u32[]{:S(2)}) collective-permute-start(f32[512,256]{1,0:T(8,128)S(1)} %get-tuple-element.61), channel_id=1, source_target_pairs={{0,508},{4,0},{8,4},{12,8},{16,12},{20,16},{24,20},{28,24},{32,28}... | collective-permute-start | bytes 1572872 | tf_op jit(solution)/shard_map/ppermute | solution.py:248
  111.1 18.9 %collective-permute-start.14 = (f32[512,256]{1,0:T(8,128)S(1)}, f32[512,256]{1,0:T(8,128)S(1)}, u32[]{:S(2)}, u32[]{:S(2)}) collective-permute-start(f32[512,256]{1,0:T(8,128)S(1)} %get-tuple-element.67), channel_id=1, source_target_pairs={{0,4},{4,8},{8,12},{12,16},{16,20},{20,24},{24,28},{28,32},{32,36}... | collective-permute-start | bytes 1572872 | tf_op jit(solution)/shard_map/ppermute | solution.py:248
  113.0 17.0 %collective-permute-start.15 = (f32[512,256]{1,0:T(8,128)S(1)}, f32[512,256]{1,0:T(8,128)S(1)}, u32[]{:S(2)}, u32[]{:S(2)}) collective-permute-start(f32[512,256]{1,0:T(8,128)S(1)} %get-tuple-element.68), channel_id=1, source_target_pairs={{0,508},{4,0},{8,4},{12,8},{16,12},{20,16},{24,20},{28,24},{32,28}... | collective-permute-start | bytes 1572872 | tf_op jit(solution)/shard_map/ppermute | solution.py:248
  120.2 20.2 %collective-permute-start.11 = (f32[576,128]{1,0:T(8,128)S(1)}, f32[576,128]{1,0:T(8,128)S(1)}, u32[]{:S(2)}, u32[]{:S(2)}) collective-permute-start(f32[576,128]{1,0:T(8,128)S(1)} %get-tuple-element.63), channel_id=1, source_target_pairs={{0,1},{1,2},{2,3},{3,0},{4,5},{5,6},{6,7},{7,4},{8,9},{9,10},{10,1... | collective-permute-start | bytes 884744 | tf_op jit(solution)/shard_map/ppermute | solution.py:248
  122.7 20.8 %collective-permute-start.12 = (f32[576,128]{1,0:T(8,128)S(1)}, f32[576,128]{1,0:T(8,128)S(1)}, u32[]{:S(2)}, u32[]{:S(2)}) collective-permute-start(f32[576,128]{1,0:T(8,128)S(1)} %get-tuple-element.64), channel_id=1, source_target_pairs={{0,2},{1,3},{2,0},{3,1},{4,6},{5,7},{6,4},{7,5},{8,10},{9,11},{10,... | collective-permute-start | bytes 884744 | tf_op jit(solution)/shard_map/ppermute | solution.py:248
  127.1 16.4 %collective-permute-start.13 = (f32[576,128]{1,0:T(8,128)S(1)}, f32[576,128]{1,0:T(8,128)S(1)}, u32[]{:S(2)}, u32[]{:S(2)}) collective-permute-start(f32[576,128]{1,0:T(8,128)S(1)} %get-tuple-element.65), channel_id=1, source_target_pairs={{0,3},{1,0},{2,1},{3,2},{4,7},{5,4},{6,5},{7,6},{8,11},{9,8},{10,9... | collective-permute-start | bytes 884744 | tf_op jit(solution)/shard_map/ppermute | solution.py:248
  134.1 11.7 %collective-permute-start.16 = (f32[576,128]{1,0:T(8,128)S(1)}, f32[576,128]{1,0:T(8,128)S(1)}, u32[]{:S(2)}, u32[]{:S(2)}) collective-permute-start(f32[576,128]{1,0:T(8,128)S(1)} %get-tuple-element.70), channel_id=1, source_target_pairs={{0,1},{1,2},{2,3},{3,0},{4,5},{5,6},{6,7},{7,4},{8,9},{9,10},{10,1... | collective-permute-start | bytes 884744 | tf_op jit(solution)/shard_map/ppermute | solution.py:248
  138.4 10.2 %collective-permute-start.17 = (f32[576,128]{1,0:T(8,128)S(1)}, f32[576,128]{1,0:T(8,128)S(1)}, u32[]{:S(2)}, u32[]{:S(2)}) collective-permute-start(f32[576,128]{1,0:T(8,128)S(1)} %get-tuple-element.71), channel_id=1, source_target_pairs={{0,2},{1,3},{2,0},{3,1},{4,6},{5,7},{6,4},{7,5},{8,10},{9,11},{10,... | collective-permute-start | bytes 884744 | tf_op jit(solution)/shard_map/ppermute | solution.py:248
  140.3 11.3 %collective-permute-start.18 = (f32[576,128]{1,0:T(8,128)S(1)}, f32[576,128]{1,0:T(8,128)S(1)}, u32[]{:S(2)}, u32[]{:S(2)}) collective-permute-start(f32[576,128]{1,0:T(8,128)S(1)} %get-tuple-element.72), channel_id=1, source_target_pairs={{0,3},{1,0},{2,1},{3,2},{4,7},{5,4},{6,5},{7,6},{8,11},{9,8},{10,9... | collective-permute-start | bytes 884744 | tf_op jit(solution)/shard_map/ppermute | solution.py:248

commit v4 on v3

--- a/solution.py
+++ b/solution.py
@@ -33,6 +33,7 @@
 AT_SEND = AT_KEEP + OWN * CLASS
 AT_PLACE = AT_SEND + LAYERS * OWN * KEPT
 AT_LATE = AT_PLACE + OWN * KEPT
+AT_ODD = AT_LATE + OWN * KEPT
 
 VMEM = pl.BlockSpec(memory_space=pltpu.VMEM)
 SMEM = pl.BlockSpec(memory_space=pltpu.SMEM)
@@ -143,7 +144,15 @@
     place_blocks(table_ref, stacked, out_ref, AT_LATE, before_ref)
 
 
-def class_kernel(table_ref, s0, s1, s2, s3, own_ref, to_right, to_left, chunks):
+def write_halos(table_ref, source, cross_ref, inner_ref):
+    odd = table_ref[AT_ODD]
+    for q in range(2):
+        cols = slice(q * HALF, (q + 1) * HALF)
+        cross_ref[:, cols] = source[odd + q]
+        inner_ref[:, cols] = source[1 - odd + q]
+
+
+def class_kernel(table_ref, s0, s1, s2, s3, own_ref, cross_ref, inner_ref, chunks, mine):
     for r, shard in enumerate((s0, s1, s2, s3)):
         chunks[2 * r] = shard[:, 0:128]
         chunks[2 * r + 1] = shard[:, 128:256]
@@ -160,10 +169,8 @@
             at = AT_SLOT + i * CLASS + 2 * q
             block = jnp.where(first_half, one(table_ref[at], 0), one(table_ref[at + 1], 1))
             own_ref[rows, q * 128 : (q + 1) * 128] = block
-            if q > 0:
-                to_right[rows, (q - 1) * 128 : q * 128] = block
-            if q < 2:
-                to_left[rows, q * 128 : (q + 1) * 128] = block
+            mine[q, rows, :] = block
+    write_halos(table_ref, mine, cross_ref, inner_ref)
 
 
 def split(x):
@@ -171,13 +178,21 @@
     return high, (x - high.astype(jnp.float32)).astype(jnp.bfloat16)
 
 
-def product(table_ref, shards, own_ref, from_left, from_right, right_high, right_low, finish):
+def product(table_ref, shards, own_ref, cross, inner, right_high, right_low, finish):
     empty = jnp.zeros((ROWS, 128), jnp.bfloat16)
-    for source, row, col in ((from_left, 0, 0), (own_ref, ROWS, 0), (from_right, 2 * ROWS, 128)):
-        width = source.shape[1]
-        high, low = split(source[...])
-        right_high[row : row + ROWS, col : col + width] = high
-        right_low[row : row + ROWS, col : col + width] = low
+    odd = table_ref[AT_ODD]
+    for source, side in ((cross, odd), (own_ref, None), (inner, 1 - odd)):
+        for q in range(source.shape[1] // HALF):
+            high, low = split(source[:, q * HALF : (q + 1) * HALF])
+            if side is None:
+                place = (slice(ROWS, 2 * ROWS), slice(q * HALF, (q + 1) * HALF))
+            else:
+                place = (
+                    pl.ds(pl.multiple_of(side * 2 * ROWS, 2 * ROWS), ROWS),
+                    pl.ds(pl.multiple_of((side + q) * HALF, HALF), HALF),
+                )
+            right_high[place] = high
+            right_low[place] = low
     for store in (right_high, right_low):
         store[0:ROWS, WIDTH:CLASS_COLS] = empty
         store[2 * ROWS : 3 * ROWS, 0:128] = empty
@@ -199,7 +214,7 @@
 
 
 def square_kernel(
-    table_ref, s0, s1, s2, s3, own_ref, from_left, from_right, square_ref, to_right, to_left, o0, o1, o2, o3, right_high, right_low, chunks
+    table_ref, s0, s1, s2, s3, own_ref, cross, inner, square_ref, to_cross, to_inner, o0, o1, o2, o3, right_high, right_low, chunks
 ):
     first_half = first_lanes()
 
@@ -210,18 +225,15 @@
             block = jnp.where(keep, total[:, q * 128 : (q + 1) * 128], 0.0)
             chunks[q, rows, :] = block
             square_ref[rows, q * 128 : (q + 1) * 128] = block
-            if q > 0:
-                to_right[rows, (q - 1) * 128 : q * 128] = block
-            if q < 2:
-                to_left[rows, q * 128 : (q + 1) * 128] = block
-
-    product(table_ref, (s0, s1, s2, s3), own_ref, from_left, from_right, right_high, right_low, finish)
+
+    product(table_ref, (s0, s1, s2, s3), own_ref, cross, inner, right_high, right_low, finish)
+    write_halos(table_ref, chunks, to_cross, to_inner)
     for r, out_ref in enumerate((o0, o1, o2, o3)):
         pack_blocks(table_ref, chunks, out_ref, AT_SEND + r * MOST)
 
 
 def cubic_kernel(
-    table_ref, s0, s1, s2, s3, own_ref, from_left, from_right, keep_ref, step_ref, o0, o1, o2, o3, right_high, right_low, chunks
+    table_ref, s0, s1, s2, s3, own_ref, cross, inner, keep_ref, step_ref, o0, o1, o2, o3, right_high, right_low, chunks
 ):
 
     def finish(i, rows, total):
@@ -231,7 +243,7 @@
             chunks[q, rows, :] = block
             step_ref[rows, cols] = block
 
-    product(table_ref, (s0, s1, s2, s3), own_ref, from_left, from_right, right_high, right_low, finish)
+    product(table_ref, (s0, s1, s2, s3), own_ref, cross, inner, right_high, right_low, finish)
     for r, out_ref in enumerate((o0, o1, o2, o3)):
         pack_blocks(table_ref, chunks, out_ref, AT_SEND + r * MOST)
 
@@ -288,6 +300,12 @@
     layers = jnp.arange(LAYERS, dtype=jnp.int32)
     each = (counts[:, :, None] >> (8 * layers)) & 255
     return jnp.max(jnp.where(layers[:, None] == layers, 0, each)) > FIRST
+
+
+def halos(cross, inner):
+    count = lax.axis_size("wide")
+    over = [(i, (i + 1) % count if i % 2 else (i - 1) % count) for i in range(count)]
+    return lax.ppermute(cross, "wide", over), lax.ppermute(inner, "wide", [(i, i ^ 1) for i in range(count)])
 
 
 def tables(block_cols, filter_cols, wide_index, layer):
@@ -323,7 +341,7 @@
     late = jnp.logical_not(mine) & (place >= FIRST)
     first = jnp.where(late, -1, first)
     late = jnp.where(late, LATE * (source - 1) + place - FIRST, -1)
-    return jnp.concatenate([part.reshape(-1) for part in (cols, slot, keep, send, first, late)])
+    return jnp.concatenate([jnp.reshape(part, -1) for part in (cols, slot, keep, send, first, late, wide_index & 1)])
 
 
 def local(restart, slab_slot, block_cols, filter_cols):
@@ -342,20 +360,20 @@
     sent = (blocks(MOST), blocks(FIRST), blocks(FIRST), blocks(FIRST))
     flops = 2 * 3 * ROWS * KNZ * BLOCK * CLASS_COLS
     chunks = pltpu.VMEM((2 * LAYERS, ROWS, HALF), jnp.float32)
-    own, to_right, to_left = call(class_kernel, "columns_of_class", (whole, half, half), table, *shards, scratch=(chunks,), size=4 << 20)
-    from_left = shift(to_right, "wide", 1)
-    from_right = shift(to_left, "wide", -1)
-
-    square, to_right, to_left, *parts = call(
-        square_kernel, "square", (whole, half, half) + sent, table, *shards, own, from_left, from_right,
+    own, cross, inner = call(
+        class_kernel, "columns_of_class", (whole, half, half), table, *shards, scratch=(chunks, RIGHT[2]), size=4 << 20
+    )
+    cross, inner = halos(cross, inner)
+
+    square, cross_next, inner_next, *parts = call(
+        square_kernel, "square", (whole, half, half) + sent, table, *shards, own, cross, inner,
         scratch=RIGHT, size=8 << 20, flops=flops,
     )
-    from_left = shift(to_right, "wide", 1)
-    from_right = shift(to_left, "wide", -1)
+    cross, inner = halos(cross_next, inner_next)
     squared = place(table, parts[0], send_parts(parts[1:]))
 
     step, *parts = call(
-        cubic_kernel, "cubic", (whole,) + sent, table, *shards, square, from_left, from_right, own,
+        cubic_kernel, "cubic", (whole,) + sent, table, *shards, square, cross, inner, own,
         scratch=RIGHT, size=8 << 20, flops=flops,
     )
     updated = place(table, parts[0], send_parts(parts[1:]))

time: 154 us -> 152 us (0.987)
  starting transfers between devices: 65.6 us -> 57.1 us
  waiting for transfers between devices: 64.7 us -> 70.9 us
    ppermute x13 -> x9, starting transfers between devices: 45.7 us -> 27.9 us  [shift(): return lax.ppermute(x, axis, [(i, (i + by) % count) for i in range(count)])]
    ppermute x0 -> x4, starting transfers between devices: none -> 9.28 us  [the longest x2 5.09 us: halos(): lax.ppermute(inner, 'wide', [(i, i ^ 1) for i in range(count)])]
    ppermute x0 -> x4, waiting for transfers between devices: none -> 8.55 us  [the longest x2 8.54 us: halos(): lax.ppermute(cross, 'wide', over)]
    ppermute x13 -> x9, waiting for transfers between devices: 32.5 us -> 30.1 us  [shift(): return lax.ppermute(x, axis, [(i, (i + by) % count) for i in range(count)])]
  transfers between devices with their start and end apart: 14 -> 14, of which waited for: 9 -> 8; matrix products, arithmetic and copies ran while one was open for 3% -> 3% of each run, Pallas kernels for 4% -> 4%
where the time goes in v4:
time: 152 us; the launch traced here: 151 us
  waiting for transfers between devices  70.9 us (47%)
  starting transfers between devices  57.1 us (38%)
  Pallas kernels  15.3 us (10%)
  local copies, waits for them, and re-layouts  4.53 us (3%)
  other arithmetic  1.93 us (1%)
  between operations  1.58 us (1%)
    all_to_all x1, waiting for transfers between devices, local(): lax.all_to_all(packed, 'wide', split_axis=0, concat_axis=0, tiled=True)  32.2 us
    ppermute x9, waiting for transfers between devices, shift(): return lax.ppermute(x, axis, [(i, (i + by) % count) for i in range(count)])  30.1 us
    ppermute x9, starting transfers between devices, shift(): return lax.ppermute(x, axis, [(i, (i + by) % count) for i in range(count)])  27.9 us
    all_to_all x1, starting transfers between devices, local(): lax.all_to_all(packed, 'wide', split_axis=0, concat_axis=0, tiled=True)  19.9 us
    pallas_call x7, Pallas kernels, call(): pl.pallas_call(kernel, out_shape=outs, in_specs=[SMEM] * scalars + [VMEM]...  15.3 us
    ppermute x2, waiting for transfers between devices, halos(): lax.ppermute(cross, 'wide', over)  8.54 us
    ppermute x2, starting transfers between devices, halos(): lax.ppermute(inner, 'wide', [(i, i ^ 1) for i in range(count)])  5.09 us
    ppermute x2, starting transfers between devices, halos(): lax.ppermute(cross, 'wide', over)  4.19 us
  transfers between devices with their start and end apart: 14, of which 8 were waited for; matrix products, arithmetic and copies ran while one was open for 3% of the time, Pallas kernels for 4%

profile of v4, /device:TPU:24, one launch (start us, length us, event | category | flops | bytes accessed | tf_op | source)
XLA Modules:
  0.0 151.4 jit_solution(4111700071001802278)
XLA Ops:
  0.6 1.0 copy-done
  2.3 1.7 %pack.1 = f32[128,9,1,128]{3,2,1,0:T(1,128)} custom-call(s32[128]{0:T(128)S(1)} %copy-done.1, f32[512,256]{1,0:T(8,128)S(1)} %copy-done), custom_call_target="tpu_custom_call" | custom-call | bytes 1048576 | tf_op jit(solution)/shard_map/pack/pallas_call | solution.py:265
  4.1 19.9 %all-to-all-start = ((f32[128,9,1,128]{3,2,1,0:T(1,128)}), f32[128,9,1,128]{3,2,1,0:T(1,128)S(1)}, u32[]{:S(2)}, u32[]{:S(2)}) async-start(f32[128,9,1,128]{3,2,1,0:T(1,128)} %pack.1), calls=%async_computation | async-start | bytes 1179648 | tf_op jit(solution)/shard_map/all_to_all | solution.py:353
  24.0 0.8 constant_dynamic-slice_fusion.1
  27.9 32.2 %all-to-all-done.arrived_ref = f32[128,9,1,128]{3,2,1,0:T(1,128)S(1)} async-done(((f32[128,9,1,128]{3,2,1,0:T(1,128)}), f32[128,9,1,128]{3,2,1,0:T(1,128)S(1)}, u32[]{:S(2)}, u32[]{:S(2)}) %all-to-all-start) | async-done | bytes 589856 | tf_op jit(solution)/shard_map/all_to_all | solution.py:353
  60.1 0.7 unpack.1.s0
  60.7 2.1 %collective-permute-start.8 = (f32[512,256]{1,0:T(8,128)S(1)}, f32[512,256]{1,0:T(8,128)S(1)}, u32[]{:S(2)}, u32[]{:S(2)}) collective-permute-start(f32[512,256]{1,0:T(8,128)S(1)} %unpack.1.s0), channel_id=1, source_target_pairs={{0,1},{1,2},{2,3},{3,0},{4,5},{5,6},{6,7},{7,4},{8,9},{9,10},{10,1... | collective-permute-start | bytes 1572872 | tf_op jit(solution)/shard_map/ppermute | solution.py:260
  62.9 4.5 %collective-permute-start.7 = (f32[512,256]{1,0:T(8,128)S(1)}, f32[512,256]{1,0:T(8,128)S(1)}, u32[]{:S(2)}, u32[]{:S(2)}) collective-permute-start(f32[512,256]{1,0:T(8,128)S(1)} %unpack.1.s0), channel_id=1, source_target_pairs={{0,2},{1,3},{2,0},{3,1},{4,6},{5,7},{6,4},{7,5},{8,10},{9,11},{10,... | collective-permute-start | bytes 1572872 | tf_op jit(solution)/shard_map/ppermute | solution.py:260
  67.4 1.9 %collective-permute-start.6 = (f32[512,256]{1,0:T(8,128)S(1)}, f32[512,256]{1,0:T(8,128)S(1)}, u32[]{:S(2)}, u32[]{:S(2)}) collective-permute-start(f32[512,256]{1,0:T(8,128)S(1)} %unpack.1.s0), channel_id=1, source_target_pairs={{0,3},{1,0},{2,1},{3,2},{4,7},{5,4},{6,5},{7,6},{8,11},{9,8},{10,9... | collective-permute-start | bytes 1572872 | tf_op jit(solution)/shard_map/ppermute | solution.py:260
  69.3 0.7 select_reduce_fusion.2
  71.0 6.5 %collective-permute-done.8.s3 = f32[512,256]{1,0:T(8,128)S(1)} collective-permute-done((f32[512,256]{1,0:T(8,128)S(1)}, f32[512,256]{1,0:T(8,128)S(1)}, u32[]{:S(2)}, u32[]{:S(2)}) %collective-permute-start.8) | collective-permute-done | bytes 524320 | tf_op jit(solution)/shard_map/ppermute | solution.py:260
  77.5 3.7 %collective-permute-done.7.s2 = f32[512,256]{1,0:T(8,128)S(1)} collective-permute-done((f32[512,256]{1,0:T(8,128)S(1)}, f32[512,256]{1,0:T(8,128)S(1)}, u32[]{:S(2)}, u32[]{:S(2)}) %collective-permute-start.7) | collective-permute-done | bytes 524320 | tf_op jit(solution)/shard_map/ppermute | solution.py:260
  81.2 9.1 %collective-permute-done.6.s1 = f32[512,256]{1,0:T(8,128)S(1)} collective-permute-done((f32[512,256]{1,0:T(8,128)S(1)}, f32[512,256]{1,0:T(8,128)S(1)}, u32[]{:S(2)}, u32[]{:S(2)}) %collective-permute-start.6) | collective-permute-done | bytes 524320 | tf_op jit(solution)/shard_map/ppermute | solution.py:260
  90.3 1.2 columns_of_class.1
  91.6 2.1 %collective-permute-start.9 = (f32[512,256]{1,0:T(8,128)S(1)}, f32[512,256]{1,0:T(8,128)S(1)}, u32[]{:S(2)}, u32[]{:S(2)}) collective-permute-start(f32[512,256]{1,0:T(8,128)S(1)} %get-tuple-element.60), channel_id=1, source_target_pairs={{0,508},{4,8},{8,4},{12,16},{16,12},{20,24},{24,20},{28,32},{32,28... | collective-permute-start | bytes 1572872 | tf_op jit(solution)/shard_map/ppermute | solution.py:308
  93.7 3.2 %collective-permute-start.10 = (f32[512,256]{1,0:T(8,128)S(1)}, f32[512,256]{1,0:T(8,128)S(1)}, u32[]{:S(2)}, u32[]{:S(2)}) collective-permute-start(f32[512,256]{1,0:T(8,128)S(1)} %get-tuple-element.61), channel_id=1, source_target_pairs={{0,4},{4,0},{8,12},{12,8},{16,20},{20,16},{24,28},{28,24},{32,36},... | collective-permute-start | bytes 1572872 | tf_op jit(solution)/shard_map/ppermute | solution.py:308
  96.9 8.5 %collective-permute-done.9.cross = f32[512,256]{1,0:T(8,128)S(1)} collective-permute-done((f32[512,256]{1,0:T(8,128)S(1)}, f32[512,256]{1,0:T(8,128)S(1)}, u32[]{:S(2)}, u32[]{:S(2)}) %collective-permute-start.9) | collective-permute-done | bytes 524320 | tf_op jit(solution)/shard_map/ppermute | solution.py:308
  105.4 4.1 %square.1 = (f32[512,384]{1,0:T(8,128)S(1)}, f32[512,256]{1,0:T(8,128)S(1)}, f32[512,256]{1,0:T(8,128)S(1)}, f32[1024,128]{1,0:T(8,128)S(1)}, f32[576,128]{1,0:T...) custom-call(s32[417]{0:T(512)S(1)} %concatenate.11.table_ref, f32[512,256]{1,0:T(8,128)S(1)} %unpack.1.s0, ...), custom_call_target="tpu_custom_call" | custom-call | flops 1207959552 | bytes 8388608 | tf_op jit(solution)/shard_map/square/pallas_call | solution.py:265
  109.5 2.1 %collective-permute-start.14 = (f32[512,256]{1,0:T(8,128)S(1)}, f32[512,256]{1,0:T(8,128)S(1)}, u32[]{:S(2)}, u32[]{:S(2)}) collective-permute-start(f32[512,256]{1,0:T(8,128)S(1)} %get-tuple-element.67), channel_id=1, source_target_pairs={{0,508},{4,8},{8,4},{12,16},{16,12},{20,24},{24,20},{28,32},{32,28... | collective-permute-start | bytes 1572872 | tf_op jit(solution)/shard_map/ppermute | solution.py:308
  111.6 1.9 %collective-permute-start.15 = (f32[512,256]{1,0:T(8,128)S(1)}, f32[512,256]{1,0:T(8,128)S(1)}, u32[]{:S(2)}, u32[]{:S(2)}) collective-permute-start(f32[512,256]{1,0:T(8,128)S(1)} %get-tuple-element.68), channel_id=1, source_target_pairs={{0,4},{4,0},{8,12},{12,8},{16,20},{20,16},{24,28},{28,24},{32,36},... | collective-permute-start | bytes 1572872 | tf_op jit(solution)/shard_map/ppermute | solution.py:308
  113.5 2.3 %collective-permute-start.11 = (f32[576,128]{1,0:T(8,128)S(1)}, f32[576,128]{1,0:T(8,128)S(1)}, u32[]{:S(2)}, u32[]{:S(2)}) collective-permute-start(f32[576,128]{1,0:T(8,128)S(1)} %get-tuple-element.63), channel_id=1, source_target_pairs={{0,1},{1,2},{2,3},{3,0},{4,5},{5,6},{6,7},{7,4},{8,9},{9,10},{10,1... | collective-permute-start | bytes 884744 | tf_op jit(solution)/shard_map/ppermute | solution.py:260
  115.9 4.4 %collective-permute-start.12 = (f32[576,128]{1,0:T(8,128)S(1)}, f32[576,128]{1,0:T(8,128)S(1)}, u32[]{:S(2)}, u32[]{:S(2)}) collective-permute-start(f32[576,128]{1,0:T(8,128)S(1)} %get-tuple-element.64), channel_id=1, source_target_pairs={{0,2},{1,3},{2,0},{3,1},{4,6},{5,7},{6,4},{7,5},{8,10},{9,11},{10,... | collective-permute-start | bytes 884744 | tf_op jit(solution)/shard_map/ppermute | solution.py:260
  120.3 3.1 %collective-permute-start.13 = (f32[576,128]{1,0:T(8,128)S(1)}, f32[576,128]{1,0:T(8,128)S(1)}, u32[]{:S(2)}, u32[]{:S(2)}) collective-permute-start(f32[576,128]{1,0:T(8,128)S(1)} %get-tuple-element.65), channel_id=1, source_target_pairs={{0,3},{1,0},{2,1},{3,2},{4,7},{5,4},{6,5},{7,6},{8,11},{9,8},{10,9... | collective-permute-start | bytes 884744 | tf_op jit(solution)/shard_map/ppermute | solution.py:260
  123.4 4.0 %cubic.1 = (f32[512,384]{1,0:T(8,128)S(1)}, f32[1024,128]{1,0:T(8,128)S(1)}, f32[576,128]{1,0:T(8,128)S(1)}, f32[576,128]{1,0:T(8,128)S(1)}, f32[576,128]{1,0:T(8,128)S(1)}) custom-call(s32[417]{0:T(512)S(1)} %concatenate.11.table_ref, f32[512,256]{1,0:T(8,128)S(1)} %unpack.1.s0, f32[512,256]{1,0:T(8,128)S(1)} %collective-permute-done.6.s1, ...), custom_call_target="tpu_custom_call" | custom-call | flops 1207959552 | bytes 8388608 | tf_op jit(solution)/shard_map/cubic/pallas_call | solution.py:265
  127.5 4.1 %collective-permute-start.16 = (f32[576,128]{1,0:T(8,128)S(1)}, f32[576,128]{1,0:T(8,128)S(1)}, u32[]{:S(2)}, u32[]{:S(2)}) collective-permute-start(f32[576,128]{1,0:T(8,128)S(1)} %get-tuple-element.70), channel_id=1, source_target_pairs={{0,1},{1,2},{2,3},{3,0},{4,5},{5,6},{6,7},{7,4},{8,9},{9,10},{10,1... | collective-permute-start | bytes 884744 | tf_op jit(solution)/shard_map/ppermute | solution.py:260
  131.6 2.7 %collective-permute-start.17 = (f32[576,128]{1,0:T(8,128)S(1)}, f32[576,128]{1,0:T(8,128)S(1)}, u32[]{:S(2)}, u32[]{:S(2)}) collective-permute-start(f32[576,128]{1,0:T(8,128)S(1)} %get-tuple-element.71), channel_id=1, source_target_pairs={{0,2},{1,3},{2,0},{3,1},{4,6},{5,7},{6,4},{7,5},{8,10},{9,11},{10,... | collective-permute-start | bytes 884744 | tf_op jit(solution)/shard_map/ppermute | solution.py:260
  134.3 2.7 %collective-permute-start.18 = (f32[576,128]{1,0:T(8,128)S(1)}, f32[576,128]{1,0:T(8,128)S(1)}, u32[]{:S(2)}, u32[]{:S(2)}) collective-permute-start(f32[576,128]{1,0:T(8,128)S(1)} %get-tuple-element.72), channel_id=1, source_target_pairs={{0,3},{1,0},{2,1},{3,2},{4,7},{5,4},{6,5},{7,6},{8,11},{9,8},{10,9... | collective-permute-start | bytes 884744 | tf_op jit(solution)/shard_map/ppermute | solution.py:260
  137.1 1.8 %place_blocks.2 = f32[512,256]{1,0:T(8,128)} custom-call(s32[417]{0:T(512)S(1)} %concatenate.11.table_ref, f32[1024,128]{1,0:T(8,128)S(1)} %get-tuple-element.62.p0, f32[576,128]{1,0:T(8,128)S(1)} %collective-permute-done.11.p1, f32[576,128]{1,0:T(8,128)S(1)} %collective-permute-done.12.p2, f32[576,128]{1,0:T(8,128)S(1)} %collective-permute-done.13.p3), custom_call_target="tpu_custom_call" | custom-call | bytes 1048576 | tf_op jit(solution)/shard_map/place_blocks/pallas_call | solution.py:265
  138.9 5.2 %collective-permute-done.16.p1 = f32[576,128]{1,0:T(8,128)S(1)} collective-permute-done((f32[576,128]{1,0:T(8,128)S(1)}, f32[576,128]{1,0:T(8,128)S(1)}, u32[]{:S(2)}, u32[]{:S(2)}) %collective-permute-start.16) | collective-permute-done | bytes 294944 | tf_op jit(solution)/shard_map/ppermute | solution.py:260
  144.0 1.0 collective-permute-done.17.p2
  145.0 4.6 %collective-permute-done.18.p3 = f32[576,128]{1,0:T(8,128)S(1)} collective-permute-done((f32[576,128]{1,0:T(8,128)S(1)}, f32[576,128]{1,0:T(8,128)S(1)}, u32[]{:S(2)}, u32[]{:S(2)}) %collective-permute-start.18) | collective-permute-done | bytes 294944 | tf_op jit(solution)/shard_map/ppermute | solution.py:260
  149.6 1.8 %place_blocks.3 = f32[512,256]{1,0:T(8,128)} custom-call(s32[417]{0:T(512)S(1)} %concatenate.11.table_ref, f32[1024,128]{1,0:T(8,128)S(1)} %get-tuple-element.69.p0, f32[576,128]{1,0:T(8,128)S(1)} %collective-permute-done.16.p1, f32[576,128]{1,0:T(8,128)S(1)} %collective-permute-done.17.p2, f32[576,128]{1,0:T(8,128)S(1)} %collective-permute-done.18.p3), custom_call_target="tpu_custom_call" | custom-call | bytes 1048576 | tf_op jit(solution)/shard_map/place_blocks/pallas_call | solution.py:265
  (51 shorter events, 4.0 us)
Async XLA Ops:
  0.6 1.0 copy-start
  1.7 0.7 copy-start.1
  4.1 19.9 %copy-start.5 = (s32[1024,16]{0,1:T(8,128)S(1)}, s32[1024,16]{0,1:T(8,128)}, u32[]{:S(2)}) copy-start(s32[1024,16]{0,1:T(8,128)} %param.9) | copy-start | bytes 196612
  4.1 56.0 %all-to-all-start = ((f32[128,9,1,128]{3,2,1,0:T(1,128)}), f32[128,9,1,128]{3,2,1,0:T(1,128)S(1)}, u32[]{:S(2)}, u32[]{:S(2)}) async-start(f32[128,9,1,128]{3,2,1,0:T(1,128)} %pack.1), calls=%async_computation | async-start | bytes 1179648 | tf_op jit(solution)/shard_map/all_to_all | solution.py:353
  60.7 16.8 %collective-permute-start.8 = (f32[512,256]{1,0:T(8,128)S(1)}, f32[512,256]{1,0:T(8,128)S(1)}, u32[]{:S(2)}, u32[]{:S(2)}) collective-permute-start(f32[512,256]{1,0:T(8,128)S(1)} %unpack.1.s0), channel_id=1, source_target_pairs={{0,1},{1,2},{2,3},{3,0},{4,5},{5,6},{6,7},{7,4},{8,9},{9,10},{10,1... | collective-permute-start | bytes 1572872 | tf_op jit(solution)/shard_map/ppermute | solution.py:260
  62.9 18.3 %collective-permute-start.7 = (f32[512,256]{1,0:T(8,128)S(1)}, f32[512,256]{1,0:T(8,128)S(1)}, u32[]{:S(2)}, u32[]{:S(2)}) collective-permute-start(f32[512,256]{1,0:T(8,128)S(1)} %unpack.1.s0), channel_id=1, source_target_pairs={{0,2},{1,3},{2,0},{3,1},{4,6},{5,7},{6,4},{7,5},{8,10},{9,11},{10,... | collective-permute-start | bytes 1572872 | tf_op jit(solution)/shard_map/ppermute | solution.py:260
  67.4 23.0 %collective-permute-start.6 = (f32[512,256]{1,0:T(8,128)S(1)}, f32[512,256]{1,0:T(8,128)S(1)}, u32[]{:S(2)}, u32[]{:S(2)}) collective-permute-start(f32[512,256]{1,0:T(8,128)S(1)} %unpack.1.s0), channel_id=1, source_target_pairs={{0,3},{1,0},{2,1},{3,2},{4,7},{5,4},{6,5},{7,6},{8,11},{9,8},{10,9... | collective-permute-start | bytes 1572872 | tf_op jit(solution)/shard_map/ppermute | solution.py:260
  91.6 13.8 %collective-permute-start.9 = (f32[512,256]{1,0:T(8,128)S(1)}, f32[512,256]{1,0:T(8,128)S(1)}, u32[]{:S(2)}, u32[]{:S(2)}) collective-permute-start(f32[512,256]{1,0:T(8,128)S(1)} %get-tuple-element.60), channel_id=1, source_target_pairs={{0,508},{4,8},{8,4},{12,16},{16,12},{20,24},{24,20},{28,32},{32,28... | collective-permute-start | bytes 1572872 | tf_op jit(solution)/shard_map/ppermute | solution.py:308
  93.7 11.7 %collective-permute-start.10 = (f32[512,256]{1,0:T(8,128)S(1)}, f32[512,256]{1,0:T(8,128)S(1)}, u32[]{:S(2)}, u32[]{:S(2)}) collective-permute-start(f32[512,256]{1,0:T(8,128)S(1)} %get-tuple-element.61), channel_id=1, source_target_pairs={{0,4},{4,0},{8,12},{12,8},{16,20},{20,16},{24,28},{28,24},{32,36},... | collective-permute-start | bytes 1572872 | tf_op jit(solution)/shard_map/ppermute | solution.py:308
  109.5 13.9 %collective-permute-start.14 = (f32[512,256]{1,0:T(8,128)S(1)}, f32[512,256]{1,0:T(8,128)S(1)}, u32[]{:S(2)}, u32[]{:S(2)}) collective-permute-start(f32[512,256]{1,0:T(8,128)S(1)} %get-tuple-element.67), channel_id=1, source_target_pairs={{0,508},{4,8},{8,4},{12,16},{16,12},{20,24},{24,20},{28,32},{32,28... | collective-permute-start | bytes 1572872 | tf_op jit(solution)/shard_map/ppermute | solution.py:308
  111.6 11.8 %collective-permute-start.15 = (f32[512,256]{1,0:T(8,128)S(1)}, f32[512,256]{1,0:T(8,128)S(1)}, u32[]{:S(2)}, u32[]{:S(2)}) collective-permute-start(f32[512,256]{1,0:T(8,128)S(1)} %get-tuple-element.68), channel_id=1, source_target_pairs={{0,4},{4,0},{8,12},{12,8},{16,20},{20,16},{24,28},{28,24},{32,36},... | collective-permute-start | bytes 1572872 | tf_op jit(solution)/shard_map/ppermute | solution.py:308
  113.5 20.8 %collective-permute-start.11 = (f32[576,128]{1,0:T(8,128)S(1)}, f32[576,128]{1,0:T(8,128)S(1)}, u32[]{:S(2)}, u32[]{:S(2)}) collective-permute-start(f32[576,128]{1,0:T(8,128)S(1)} %get-tuple-element.63), channel_id=1, source_target_pairs={{0,1},{1,2},{2,3},{3,0},{4,5},{5,6},{6,7},{7,4},{8,9},{9,10},{10,1... | collective-permute-start | bytes 884744 | tf_op jit(solution)/shard_map/ppermute | solution.py:260
  115.9 21.2 %collective-permute-start.12 = (f32[576,128]{1,0:T(8,128)S(1)}, f32[576,128]{1,0:T(8,128)S(1)}, u32[]{:S(2)}, u32[]{:S(2)}) collective-permute-start(f32[576,128]{1,0:T(8,128)S(1)} %get-tuple-element.64), channel_id=1, source_target_pairs={{0,2},{1,3},{2,0},{3,1},{4,6},{5,7},{6,4},{7,5},{8,10},{9,11},{10,... | collective-permute-start | bytes 884744 | tf_op jit(solution)/shard_map/ppermute | solution.py:260
  120.3 16.8 %collective-permute-start.13 = (f32[576,128]{1,0:T(8,128)S(1)}, f32[576,128]{1,0:T(8,128)S(1)}, u32[]{:S(2)}, u32[]{:S(2)}) collective-permute-start(f32[576,128]{1,0:T(8,128)S(1)} %get-tuple-element.65), channel_id=1, source_target_pairs={{0,3},{1,0},{2,1},{3,2},{4,7},{5,4},{6,5},{7,6},{8,11},{9,8},{10,9... | collective-permute-start | bytes 884744 | tf_op jit(solution)/shard_map/ppermute | solution.py:260
  127.5 16.6 %collective-permute-start.16 = (f32[576,128]{1,0:T(8,128)S(1)}, f32[576,128]{1,0:T(8,128)S(1)}, u32[]{:S(2)}, u32[]{:S(2)}) collective-permute-start(f32[576,128]{1,0:T(8,128)S(1)} %get-tuple-element.70), channel_id=1, source_target_pairs={{0,1},{1,2},{2,3},{3,0},{4,5},{5,6},{6,7},{7,4},{8,9},{9,10},{10,1... | collective-permute-start | bytes 884744 | tf_op jit(solution)/shard_map/ppermute | solution.py:260
  131.6 13.4 %collective-permute-start.17 = (f32[576,128]{1,0:T(8,128)S(1)}, f32[576,128]{1,0:T(8,128)S(1)}, u32[]{:S(2)}, u32[]{:S(2)}) collective-permute-start(f32[576,128]{1,0:T(8,128)S(1)} %get-tuple-element.71), channel_id=1, source_target_pairs={{0,2},{1,3},{2,0},{3,1},{4,6},{5,7},{6,4},{7,5},{8,10},{9,11},{10,... | collective-permute-start | bytes 884744 | tf_op jit(solution)/shard_map/ppermute | solution.py:260
  134.3 15.3 %collective-permute-start.18 = (f32[576,128]{1,0:T(8,128)S(1)}, f32[576,128]{1,0:T(8,128)S(1)}, u32[]{:S(2)}, u32[]{:S(2)}) collective-permute-start(f32[576,128]{1,0:T(8,128)S(1)} %get-tuple-element.72), channel_id=1, source_target_pairs={{0,3},{1,0},{2,1},{3,2},{4,7},{5,4},{6,5},{7,6},{8,11},{9,8},{10,9... | collective-permute-start | bytes 884744 | tf_op jit(solution)/shard_map/ppermute | solution.py:260

commit v5 on v4

--- a/solution.py
+++ b/solution.py
@@ -24,7 +24,7 @@
 HALF = 2 * BLOCK
 KEPT = JNZ // LAYERS
 MOST = OWN * KEPT
-FIRST = 18
+FIRST = 16
 LATE = MOST - FIRST
 
 AT_ROW = 0
@@ -294,12 +294,18 @@
     return call(late_place_kernel, "place_late_blocks", f32(ROWS, WIDTH), table, before, *send_parts(parts), scratch=(stacked,))
 
 
-def any_late(filter_cols):
-    ones = jnp.left_shift(1, 8 * (filter_cols & (LAYERS - 1)))
-    counts = jnp.sum(ones.reshape(N_WIDE, OWN, LAYERS, KEPT), axis=(1, 3))
-    layers = jnp.arange(LAYERS, dtype=jnp.int32)
-    each = (counts[:, :, None] >> (8 * layers)) & 255
-    return jnp.max(jnp.where(layers[:, None] == layers, 0, each)) > FIRST
+def class_of(cols, groups, turn):
+    return (cols + turn * groups) & (LAYERS - 1)
+
+
+def choose_turn(filter_cols):
+    turns = jnp.arange(LAYERS, dtype=jnp.int32)
+    ones = jnp.left_shift(1, 8 * class_of(filter_cols, filter_cols >> 2, turns[:, None, None]))
+    counts = jnp.sum(ones.reshape(LAYERS, N_WIDE, OWN, LAYERS, KEPT), axis=(2, 4))
+    each = (counts[..., None] >> (8 * turns)) & 255
+    most = jnp.max(jnp.where(turns[:, None] == turns, 0, each), axis=(1, 2, 3))
+    least = jnp.min(most)
+    return jnp.min(jnp.where(most == least, turns, LAYERS - 1)), least > FIRST
 
 
 def halos(cross, inner):
@@ -308,7 +314,7 @@
     return lax.ppermute(cross, "wide", over), lax.ppermute(inner, "wide", [(i, i ^ 1) for i in range(count)])
 
 
-def tables(block_cols, filter_cols, wide_index, layer):
+def tables(block_cols, filter_cols, wide_index, layer, turn):
     first_row = wide_index * OWN
     base = first_row - OWN
 
@@ -320,20 +326,28 @@
 
     _, cols = own(block_cols)
     kept, kept_turned = own(filter_cols)
-    places = layer + LAYERS * jnp.arange(CLASS, dtype=jnp.int32)
+    places = jnp.arange(CLASS, dtype=jnp.int32)
+
+    def classes(mine):
+        return class_of(mine, (base >> 2) + (mine >> 2), turn)
+
+    def at_place(mine):
+        return jnp.where(classes(mine) == layer, mine >> 2, CLASS)
+
     slots = jnp.arange(KNZ, dtype=jnp.int32)
-    slot = jnp.min(jnp.where(cols[:, None, :] == places[None, :, None], slots, KNZ), axis=2)
-    keep = jnp.max((kept[:, None, :] == places[None, :, None]).astype(jnp.int32), axis=2)
+    slot = jnp.min(jnp.where(at_place(cols)[:, None, :] == places[None, :, None], slots, KNZ), axis=2)
+    keep = jnp.max((at_place(kept)[:, None, :] == places[None, :, None]).astype(jnp.int32), axis=2)
 
     wanted = kept_turned.reshape(OWN, LAYERS, KEPT).transpose(1, 0, 2).reshape(LAYERS, MOST)
-    here = (wanted & (LAYERS - 1)) == layer
+    groups = classes(wanted)
+    here = groups == layer
     order = jnp.arange(MOST, dtype=jnp.int32)
     earlier = order[None, :] < order[:, None]
     rank = jnp.sum((here[:, None, :] & earlier).astype(jnp.int32), axis=2)
-    code = (order >> 2) * OWN + ((wanted - layer) >> 2)
+    code = (order >> 2) * OWN + (wanted >> 2)
     chosen = here[:, None, :] & (rank[:, None, :] == order[None, :, None])
     send = jnp.max(jnp.where(chosen, code[:, None, :], -1), axis=2)
-    group = wanted[0] & (LAYERS - 1)
+    group = groups[0]
     source = (layer - group) & (LAYERS - 1)
     place = jnp.sum(((group[None, :] == group[:, None]) & earlier).astype(jnp.int32), axis=1)
     mine = source == 0
@@ -347,7 +361,8 @@
 def local(restart, slab_slot, block_cols, filter_cols):
     wide_index = lax.axis_index("wide")
     layer = lax.axis_index("narrow")
-    table, late = lax.optimization_barrier((tables(block_cols, filter_cols, wide_index, layer), any_late(filter_cols)))
+    turn, late = choose_turn(filter_cols)
+    table, late = lax.optimization_barrier((tables(block_cols, filter_cols, wide_index, layer, turn), late))
 
     packed = call(pack_kernel, "pack", f32(N_WIDE, 9, 1, 128), slab_slot, restart)
     arrived = lax.all_to_all(packed, "wide", split_axis=0, concat_axis=0, tiled=True)

time: 152 us -> 152 us (level)
  waiting for transfers between devices: 70.9 us -> 67.4 us
  other arithmetic: 1.93 us -> 4.65 us
    all_to_all x1, waiting for transfers between devices: 32.2 us -> 28 us  [local(): lax.all_to_all(packed, 'wide', split_axis=0, concat_axis=0, tiled=True)]
    reduce_min x0 -> x3, other arithmetic: none -> 2.1 us  [the longest x1 1.28 us: choose_turn(): return (jnp.min(jnp.where(most == least, turns, LAYERS - 1)), least > FIRST)]
  transfers between devices with their start and end apart: 14 -> 14, of which waited for: 8 -> 8; matrix products, arithmetic and copies ran while one was open for 3% -> 5% of each run, Pallas kernels for 4% -> 3%
where the time goes in v5:
time: 152 us; the launch traced here: 151 us
  waiting for transfers between devices  67.4 us (44%)
  starting transfers between devices  57.2 us (38%)
  Pallas kernels  14.4 us (9%)
  local copies, waits for them, and re-layouts  5.49 us (4%)
  other arithmetic  4.65 us (3%)
  between operations  1.61 us (1%)
    ppermute x9, waiting for transfers between devices, shift(): return lax.ppermute(x, axis, [(i, (i + by) % count) for i in range(count)])  30.9 us
    all_to_all x1, waiting for transfers between devices, local(): lax.all_to_all(packed, 'wide', split_axis=0, concat_axis=0, tiled=True)  28 us
    ppermute x9, starting transfers between devices, shift(): return lax.ppermute(x, axis, [(i, (i + by) % count) for i in range(count)])  28 us
    all_to_all x1, starting transfers between devices, local(): lax.all_to_all(packed, 'wide', split_axis=0, concat_axis=0, tiled=True)  19.9 us
    pallas_call x7, Pallas kernels, call(): pl.pallas_call(kernel, out_shape=outs, in_specs=[SMEM] * scalars + [VMEM]...  14.4 us
    ppermute x2, waiting for transfers between devices, halos(): lax.ppermute(cross, 'wide', over)  8.54 us
    ppermute x2, starting transfers between devices, halos(): lax.ppermute(inner, 'wide', [(i, i ^ 1) for i in range(count)])  5.09 us
    ppermute x2, starting transfers between devices, halos(): lax.ppermute(cross, 'wide', over)  4.2 us
  transfers between devices with their start and end apart: 14, of which 8 were waited for; matrix products, arithmetic and copies ran while one was open for 5% of the time, Pallas kernels for 3%

profile of v5, /device:TPU:24, one launch (start us, length us, event | category | flops | bytes accessed | tf_op | source)
XLA Modules:
  0.0 150.7 jit_solution(13732882653569064092)
XLA Ops:
  0.7 1.1 copy-done.1
  2.4 1.7 %pack.1 = f32[128,9,1,128]{3,2,1,0:T(1,128)} custom-call(s32[128]{0:T(128)S(1)} %copy-done.2, f32[512,256]{1,0:T(8,128)S(1)} %copy-done.1), custom_call_target="tpu_custom_call" | custom-call | bytes 1048576 | tf_op jit(solution)/shard_map/pack/pallas_call | solution.py:265
  4.1 19.9 %all-to-all-start = ((f32[128,9,1,128]{3,2,1,0:T(1,128)}), f32[128,9,1,128]{3,2,1,0:T(1,128)S(1)}, u32[]{:S(2)}, u32[]{:S(2)}) async-start(f32[128,9,1,128]{3,2,1,0:T(1,128)} %pack.1), calls=%async_computation | async-start | bytes 1179648 | tf_op jit(solution)/shard_map/all_to_all | solution.py:368
  27.9 1.3 fusion.4
  29.2 0.7 fusion.1
  32.1 28.0 %all-to-all-done.arrived_ref = f32[128,9,1,128]{3,2,1,0:T(1,128)S(1)} async-done(((f32[128,9,1,128]{3,2,1,0:T(1,128)}), f32[128,9,1,128]{3,2,1,0:T(1,128)S(1)}, u32[]{:S(2)}, u32[]{:S(2)}) %all-to-all-start) | async-done | bytes 589856 | tf_op jit(solution)/shard_map/all_to_all | solution.py:368
  60.8 2.1 %collective-permute-start.8 = (f32[512,256]{1,0:T(8,128)S(1)}, f32[512,256]{1,0:T(8,128)S(1)}, u32[]{:S(2)}, u32[]{:S(2)}) collective-permute-start(f32[512,256]{1,0:T(8,128)S(1)} %unpack.1.s0), channel_id=1, source_target_pairs={{0,1},{1,2},{2,3},{3,0},{4,5},{5,6},{6,7},{7,4},{8,9},{9,10},{10,1... | collective-permute-start | bytes 1572872 | tf_op jit(solution)/shard_map/ppermute | solution.py:260
  62.9 4.5 %collective-permute-start.7 = (f32[512,256]{1,0:T(8,128)S(1)}, f32[512,256]{1,0:T(8,128)S(1)}, u32[]{:S(2)}, u32[]{:S(2)}) collective-permute-start(f32[512,256]{1,0:T(8,128)S(1)} %unpack.1.s0), channel_id=1, source_target_pairs={{0,2},{1,3},{2,0},{3,1},{4,6},{5,7},{6,4},{7,5},{8,10},{9,11},{10,... | collective-permute-start | bytes 1572872 | tf_op jit(solution)/shard_map/ppermute | solution.py:260
  67.4 1.9 %collective-permute-start.6 = (f32[512,256]{1,0:T(8,128)S(1)}, f32[512,256]{1,0:T(8,128)S(1)}, u32[]{:S(2)}, u32[]{:S(2)}) collective-permute-start(f32[512,256]{1,0:T(8,128)S(1)} %unpack.1.s0), channel_id=1, source_target_pairs={{0,3},{1,0},{2,1},{3,2},{4,7},{5,4},{6,5},{7,6},{8,11},{9,8},{10,9... | collective-permute-start | bytes 1572872 | tf_op jit(solution)/shard_map/ppermute | solution.py:260
  69.6 7.9 %collective-permute-done.8.s3 = f32[512,256]{1,0:T(8,128)S(1)} collective-permute-done((f32[512,256]{1,0:T(8,128)S(1)}, f32[512,256]{1,0:T(8,128)S(1)}, u32[]{:S(2)}, u32[]{:S(2)}) %collective-permute-start.8) | collective-permute-done | bytes 524320 | tf_op jit(solution)/shard_map/ppermute | solution.py:260
  77.5 3.7 %collective-permute-done.7.s2 = f32[512,256]{1,0:T(8,128)S(1)} collective-permute-done((f32[512,256]{1,0:T(8,128)S(1)}, f32[512,256]{1,0:T(8,128)S(1)}, u32[]{:S(2)}, u32[]{:S(2)}) %collective-permute-start.7) | collective-permute-done | bytes 524320 | tf_op jit(solution)/shard_map/ppermute | solution.py:260
  81.2 9.1 %collective-permute-done.6.s1 = f32[512,256]{1,0:T(8,128)S(1)} collective-permute-done((f32[512,256]{1,0:T(8,128)S(1)}, f32[512,256]{1,0:T(8,128)S(1)}, u32[]{:S(2)}, u32[]{:S(2)}) %collective-permute-start.6) | collective-permute-done | bytes 524320 | tf_op jit(solution)/shard_map/ppermute | solution.py:260
  90.4 1.2 columns_of_class.1
  91.6 2.1 %collective-permute-start.9 = (f32[512,256]{1,0:T(8,128)S(1)}, f32[512,256]{1,0:T(8,128)S(1)}, u32[]{:S(2)}, u32[]{:S(2)}) collective-permute-start(f32[512,256]{1,0:T(8,128)S(1)} %get-tuple-element.60), channel_id=1, source_target_pairs={{0,508},{4,8},{8,4},{12,16},{16,12},{20,24},{24,20},{28,32},{32,28... | collective-permute-start | bytes 1572872 | tf_op jit(solution)/shard_map/ppermute | solution.py:314
  93.7 3.2 %collective-permute-start.10 = (f32[512,256]{1,0:T(8,128)S(1)}, f32[512,256]{1,0:T(8,128)S(1)}, u32[]{:S(2)}, u32[]{:S(2)}) collective-permute-start(f32[512,256]{1,0:T(8,128)S(1)} %get-tuple-element.61), channel_id=1, source_target_pairs={{0,4},{4,0},{8,12},{12,8},{16,20},{20,16},{24,28},{28,24},{32,36},... | collective-permute-start | bytes 1572872 | tf_op jit(solution)/shard_map/ppermute | solution.py:314
  96.9 8.5 %collective-permute-done.9.cross = f32[512,256]{1,0:T(8,128)S(1)} collective-permute-done((f32[512,256]{1,0:T(8,128)S(1)}, f32[512,256]{1,0:T(8,128)S(1)}, u32[]{:S(2)}, u32[]{:S(2)}) %collective-permute-start.9) | collective-permute-done | bytes 524320 | tf_op jit(solution)/shard_map/ppermute | solution.py:314
  105.5 4.0 %square.1 = (f32[512,384]{1,0:T(8,128)S(1)}, f32[512,256]{1,0:T(8,128)S(1)}, f32[512,256]{1,0:T(8,128)S(1)}, f32[1024,128]{1,0:T(8,128)S(1)}, f32[512,128]{1,0:T...) custom-call(s32[417]{0:T(512)S(1)} %concatenate.11.table_ref, f32[512,256]{1,0:T(8,128)S(1)} %unpack.1.s0, ...), custom_call_target="tpu_custom_call" | custom-call | flops 1207959552 | bytes 8388608 | tf_op jit(solution)/shard_map/square/pallas_call | solution.py:265
  109.5 2.1 %collective-permute-start.14 = (f32[512,256]{1,0:T(8,128)S(1)}, f32[512,256]{1,0:T(8,128)S(1)}, u32[]{:S(2)}, u32[]{:S(2)}) collective-permute-start(f32[512,256]{1,0:T(8,128)S(1)} %get-tuple-element.67), channel_id=1, source_target_pairs={{0,508},{4,8},{8,4},{12,16},{16,12},{20,24},{24,20},{28,32},{32,28... | collective-permute-start | bytes 1572872 | tf_op jit(solution)/shard_map/ppermute | solution.py:314
  111.6 1.9 %collective-permute-start.15 = (f32[512,256]{1,0:T(8,128)S(1)}, f32[512,256]{1,0:T(8,128)S(1)}, u32[]{:S(2)}, u32[]{:S(2)}) collective-permute-start(f32[512,256]{1,0:T(8,128)S(1)} %get-tuple-element.68), channel_id=1, source_target_pairs={{0,4},{4,0},{8,12},{12,8},{16,20},{20,16},{24,28},{28,24},{32,36},... | collective-permute-start | bytes 1572872 | tf_op jit(solution)/shard_map/ppermute | solution.py:314
  113.5 2.3 %collective-permute-start.11 = (f32[512,128]{1,0:T(8,128)S(1)}, f32[512,128]{1,0:T(8,128)S(1)}, u32[]{:S(2)}, u32[]{:S(2)}) collective-permute-start(f32[512,128]{1,0:T(8,128)S(1)} %get-tuple-element.63), channel_id=1, source_target_pairs={{0,1},{1,2},{2,3},{3,0},{4,5},{5,6},{6,7},{7,4},{8,9},{9,10},{10,1... | collective-permute-start | bytes 786440 | tf_op jit(solution)/shard_map/ppermute | solution.py:260
  115.9 4.4 %collective-permute-start.12 = (f32[512,128]{1,0:T(8,128)S(1)}, f32[512,128]{1,0:T(8,128)S(1)}, u32[]{:S(2)}, u32[]{:S(2)}) collective-permute-start(f32[512,128]{1,0:T(8,128)S(1)} %get-tuple-element.64), channel_id=1, source_target_pairs={{0,2},{1,3},{2,0},{3,1},{4,6},{5,7},{6,4},{7,5},{8,10},{9,11},{10,... | collective-permute-start | bytes 786440 | tf_op jit(solution)/shard_map/ppermute | solution.py:260
  120.3 3.1 %collective-permute-start.13 = (f32[512,128]{1,0:T(8,128)S(1)}, f32[512,128]{1,0:T(8,128)S(1)}, u32[]{:S(2)}, u32[]{:S(2)}) collective-permute-start(f32[512,128]{1,0:T(8,128)S(1)} %get-tuple-element.65), channel_id=1, source_target_pairs={{0,3},{1,0},{2,1},{3,2},{4,7},{5,4},{6,5},{7,6},{8,11},{9,8},{10,9... | collective-permute-start | bytes 786440 | tf_op jit(solution)/shard_map/ppermute | solution.py:260
  123.4 4.0 %cubic.1 = (f32[512,384]{1,0:T(8,128)S(1)}, f32[1024,128]{1,0:T(8,128)S(1)}, f32[512,128]{1,0:T(8,128)S(1)}, f32[512,128]{1,0:T(8,128)S(1)}, f32[512,128]{1,0:T(8,128)S(1)}) custom-call(s32[417]{0:T(512)S(1)} %concatenate.11.table_ref, f32[512,256]{1,0:T(8,128)S(1)} %unpack.1.s0, f32[512,256]{1,0:T(8,128)S(1)} %collective-permute-done.6.s1, ...), custom_call_target="tpu_custom_call" | custom-call | flops 1207959552 | bytes 8388608 | tf_op jit(solution)/shard_map/cubic/pallas_call | solution.py:265
  127.4 4.1 %collective-permute-start.16 = (f32[512,128]{1,0:T(8,128)S(1)}, f32[512,128]{1,0:T(8,128)S(1)}, u32[]{:S(2)}, u32[]{:S(2)}) collective-permute-start(f32[512,128]{1,0:T(8,128)S(1)} %get-tuple-element.70), channel_id=1, source_target_pairs={{0,1},{1,2},{2,3},{3,0},{4,5},{5,6},{6,7},{7,4},{8,9},{9,10},{10,1... | collective-permute-start | bytes 786440 | tf_op jit(solution)/shard_map/ppermute | solution.py:260
  131.6 2.7 %collective-permute-start.17 = (f32[512,128]{1,0:T(8,128)S(1)}, f32[512,128]{1,0:T(8,128)S(1)}, u32[]{:S(2)}, u32[]{:S(2)}) collective-permute-start(f32[512,128]{1,0:T(8,128)S(1)} %get-tuple-element.71), channel_id=1, source_target_pairs={{0,2},{1,3},{2,0},{3,1},{4,6},{5,7},{6,4},{7,5},{8,10},{9,11},{10,... | collective-permute-start | bytes 786440 | tf_op jit(solution)/shard_map/ppermute | solution.py:260
  134.3 2.7 %collective-permute-start.18 = (f32[512,128]{1,0:T(8,128)S(1)}, f32[512,128]{1,0:T(8,128)S(1)}, u32[]{:S(2)}, u32[]{:S(2)}) collective-permute-start(f32[512,128]{1,0:T(8,128)S(1)} %get-tuple-element.72), channel_id=1, source_target_pairs={{0,3},{1,0},{2,1},{3,2},{4,7},{5,4},{6,5},{7,6},{8,11},{9,8},{10,9... | collective-permute-start | bytes 786440 | tf_op jit(solution)/shard_map/ppermute | solution.py:260
  137.0 1.0 place_blocks.2
  138.0 4.6 %collective-permute-done.16.p1 = f32[512,128]{1,0:T(8,128)S(1)} collective-permute-done((f32[512,128]{1,0:T(8,128)S(1)}, f32[512,128]{1,0:T(8,128)S(1)}, u32[]{:S(2)}, u32[]{:S(2)}) %collective-permute-start.16) | collective-permute-done | bytes 262176 | tf_op jit(solution)/shard_map/ppermute | solution.py:260
  142.6 1.7 %collective-permute-done.17.p2 = f32[512,128]{1,0:T(8,128)S(1)} collective-permute-done((f32[512,128]{1,0:T(8,128)S(1)}, f32[512,128]{1,0:T(8,128)S(1)}, u32[]{:S(2)}, u32[]{:S(2)}) %collective-permute-start.17) | collective-permute-done | bytes 262176 | tf_op jit(solution)/shard_map/ppermute | solution.py:260
  144.2 3.9 %collective-permute-done.18.p3 = f32[512,128]{1,0:T(8,128)S(1)} collective-permute-done((f32[512,128]{1,0:T(8,128)S(1)}, f32[512,128]{1,0:T(8,128)S(1)}, u32[]{:S(2)}, u32[]{:S(2)}) %collective-permute-start.18) | collective-permute-done | bytes 262176 | tf_op jit(solution)/shard_map/ppermute | solution.py:260
  148.2 1.8 %place_blocks.3 = f32[512,256]{1,0:T(8,128)} custom-call(s32[417]{0:T(512)S(1)} %concatenate.11.table_ref, f32[1024,128]{1,0:T(8,128)S(1)} %get-tuple-element.69.p0, f32[512,128]{1,0:T(8,128)S(1)} %collective-permute-done.16.p1, f32[512,128]{1,0:T(8,128)S(1)} %collective-permute-done.17.p2, f32[512,128]{1,0:T(8,128)S(1)} %collective-permute-done.18.p3), custom_call_target="tpu_custom_call" | custom-call | bytes 1048576 | tf_op jit(solution)/shard_map/place_blocks/pallas_call | solution.py:265
  150.0 0.8 copy-done.7
  (55 shorter events, 7.0 us)
Async XLA Ops:
  0.6 24.1 %copy-start = (s32[1024,16]{0,1:T(8,128)S(1)}, s32[1024,16]{0,1:T(8,128)}, u32[]{:S(2)}) copy-start(s32[1024,16]{0,1:T(8,128)} %param.8) | copy-start | bytes 196612
  0.6 1.1 copy-start.1
  1.7 0.7 copy-start.2
  4.1 19.9 %copy-start.8 = (s32[1024,16]{0,1:T(8,128)S(1)}, s32[1024,16]{0,1:T(8,128)}, u32[]{:S(2)}) copy-start(s32[1024,16]{0,1:T(8,128)} %param.9) | copy-start | bytes 196612
  4.1 56.0 %all-to-all-start = ((f32[128,9,1,128]{3,2,1,0:T(1,128)}), f32[128,9,1,128]{3,2,1,0:T(1,128)S(1)}, u32[]{:S(2)}, u32[]{:S(2)}) async-start(f32[128,9,1,128]{3,2,1,0:T(1,128)} %pack.1), calls=%async_computation | async-start | bytes 1179648 | tf_op jit(solution)/shard_map/all_to_all | solution.py:368
  60.8 16.8 %collective-permute-start.8 = (f32[512,256]{1,0:T(8,128)S(1)}, f32[512,256]{1,0:T(8,128)S(1)}, u32[]{:S(2)}, u32[]{:S(2)}) collective-permute-start(f32[512,256]{1,0:T(8,128)S(1)} %unpack.1.s0), channel_id=1, source_target_pairs={{0,1},{1,2},{2,3},{3,0},{4,5},{5,6},{6,7},{7,4},{8,9},{9,10},{10,1... | collective-permute-start | bytes 1572872 | tf_op jit(solution)/shard_map/ppermute | solution.py:260
  62.9 18.3 %collective-permute-start.7 = (f32[512,256]{1,0:T(8,128)S(1)}, f32[512,256]{1,0:T(8,128)S(1)}, u32[]{:S(2)}, u32[]{:S(2)}) collective-permute-start(f32[512,256]{1,0:T(8,128)S(1)} %unpack.1.s0), channel_id=1, source_target_pairs={{0,2},{1,3},{2,0},{3,1},{4,6},{5,7},{6,4},{7,5},{8,10},{9,11},{10,... | collective-permute-start | bytes 1572872 | tf_op jit(solution)/shard_map/ppermute | solution.py:260
  67.4 22.9 %collective-permute-start.6 = (f32[512,256]{1,0:T(8,128)S(1)}, f32[512,256]{1,0:T(8,128)S(1)}, u32[]{:S(2)}, u32[]{:S(2)}) collective-permute-start(f32[512,256]{1,0:T(8,128)S(1)} %unpack.1.s0), channel_id=1, source_target_pairs={{0,3},{1,0},{2,1},{3,2},{4,7},{5,4},{6,5},{7,6},{8,11},{9,8},{10,9... | collective-permute-start | bytes 1572872 | tf_op jit(solution)/shard_map/ppermute | solution.py:260
  91.6 13.8 %collective-permute-start.9 = (f32[512,256]{1,0:T(8,128)S(1)}, f32[512,256]{1,0:T(8,128)S(1)}, u32[]{:S(2)}, u32[]{:S(2)}) collective-permute-start(f32[512,256]{1,0:T(8,128)S(1)} %get-tuple-element.60), channel_id=1, source_target_pairs={{0,508},{4,8},{8,4},{12,16},{16,12},{20,24},{24,20},{28,32},{32,28... | collective-permute-start | bytes 1572872 | tf_op jit(solution)/shard_map/ppermute | solution.py:314
  93.7 11.7 %collective-permute-start.10 = (f32[512,256]{1,0:T(8,128)S(1)}, f32[512,256]{1,0:T(8,128)S(1)}, u32[]{:S(2)}, u32[]{:S(2)}) collective-permute-start(f32[512,256]{1,0:T(8,128)S(1)} %get-tuple-element.61), channel_id=1, source_target_pairs={{0,4},{4,0},{8,12},{12,8},{16,20},{20,16},{24,28},{28,24},{32,36},... | collective-permute-start | bytes 1572872 | tf_op jit(solution)/shard_map/ppermute | solution.py:314
  109.5 13.9 %collective-permute-start.14 = (f32[512,256]{1,0:T(8,128)S(1)}, f32[512,256]{1,0:T(8,128)S(1)}, u32[]{:S(2)}, u32[]{:S(2)}) collective-permute-start(f32[512,256]{1,0:T(8,128)S(1)} %get-tuple-element.67), channel_id=1, source_target_pairs={{0,508},{4,8},{8,4},{12,16},{16,12},{20,24},{24,20},{28,32},{32,28... | collective-permute-start | bytes 1572872 | tf_op jit(solution)/shard_map/ppermute | solution.py:314
  111.6 11.8 %collective-permute-start.15 = (f32[512,256]{1,0:T(8,128)S(1)}, f32[512,256]{1,0:T(8,128)S(1)}, u32[]{:S(2)}, u32[]{:S(2)}) collective-permute-start(f32[512,256]{1,0:T(8,128)S(1)} %get-tuple-element.68), channel_id=1, source_target_pairs={{0,4},{4,0},{8,12},{12,8},{16,20},{20,16},{24,28},{28,24},{32,36},... | collective-permute-start | bytes 1572872 | tf_op jit(solution)/shard_map/ppermute | solution.py:314
  113.5 20.7 %collective-permute-start.11 = (f32[512,128]{1,0:T(8,128)S(1)}, f32[512,128]{1,0:T(8,128)S(1)}, u32[]{:S(2)}, u32[]{:S(2)}) collective-permute-start(f32[512,128]{1,0:T(8,128)S(1)} %get-tuple-element.63), channel_id=1, source_target_pairs={{0,1},{1,2},{2,3},{3,0},{4,5},{5,6},{6,7},{7,4},{8,9},{9,10},{10,1... | collective-permute-start | bytes 786440 | tf_op jit(solution)/shard_map/ppermute | solution.py:260
  115.9 21.1 %collective-permute-start.12 = (f32[512,128]{1,0:T(8,128)S(1)}, f32[512,128]{1,0:T(8,128)S(1)}, u32[]{:S(2)}, u32[]{:S(2)}) collective-permute-start(f32[512,128]{1,0:T(8,128)S(1)} %get-tuple-element.64), channel_id=1, source_target_pairs={{0,2},{1,3},{2,0},{3,1},{4,6},{5,7},{6,4},{7,5},{8,10},{9,11},{10,... | collective-permute-start | bytes 786440 | tf_op jit(solution)/shard_map/ppermute | solution.py:260
  120.3 16.7 %collective-permute-start.13 = (f32[512,128]{1,0:T(8,128)S(1)}, f32[512,128]{1,0:T(8,128)S(1)}, u32[]{:S(2)}, u32[]{:S(2)}) collective-permute-start(f32[512,128]{1,0:T(8,128)S(1)} %get-tuple-element.65), channel_id=1, source_target_pairs={{0,3},{1,0},{2,1},{3,2},{4,7},{5,4},{6,5},{7,6},{8,11},{9,8},{10,9... | collective-permute-start | bytes 786440 | tf_op jit(solution)/shard_map/ppermute | solution.py:260
  127.4 15.2 %collective-permute-start.16 = (f32[512,128]{1,0:T(8,128)S(1)}, f32[512,128]{1,0:T(8,128)S(1)}, u32[]{:S(2)}, u32[]{:S(2)}) collective-permute-start(f32[512,128]{1,0:T(8,128)S(1)} %get-tuple-element.70), channel_id=1, source_target_pairs={{0,1},{1,2},{2,3},{3,0},{4,5},{5,6},{6,7},{7,4},{8,9},{9,10},{10,1... | collective-permute-start | bytes 786440 | tf_op jit(solution)/shard_map/ppermute | solution.py:260
  131.6 12.7 %collective-permute-start.17 = (f32[512,128]{1,0:T(8,128)S(1)}, f32[512,128]{1,0:T(8,128)S(1)}, u32[]{:S(2)}, u32[]{:S(2)}) collective-permute-start(f32[512,128]{1,0:T(8,128)S(1)} %get-tuple-element.71), channel_id=1, source_target_pairs={{0,2},{1,3},{2,0},{3,1},{4,6},{5,7},{6,4},{7,5},{8,10},{9,11},{10,... | collective-permute-start | bytes 786440 | tf_op jit(solution)/shard_map/ppermute | solution.py:260
  134.3 13.9 %collective-permute-start.18 = (f32[512,128]{1,0:T(8,128)S(1)}, f32[512,128]{1,0:T(8,128)S(1)}, u32[]{:S(2)}, u32[]{:S(2)}) collective-permute-start(f32[512,128]{1,0:T(8,128)S(1)} %get-tuple-element.72), channel_id=1, source_target_pairs={{0,3},{1,0},{2,1},{3,2},{4,7},{5,4},{6,5},{7,6},{8,11},{9,8},{10,9... | collective-permute-start | bytes 786440 | tf_op jit(solution)/shard_map/ppermute | solution.py:260
  149.9 0.8 copy-start.7

commit v6 on v4

--- a/solution.py
+++ b/solution.py
@@ -279,7 +279,9 @@
 
 
 def send_parts(parts):
-    return tuple(shift(part, "narrow", r + 1) for r, part in enumerate(parts))
+    near, far, back = parts
+    near, back = shift(near, "narrow", 1), shift(back, "narrow", 3)
+    return near, shift(far, "narrow", 2), back
 
 
 def place(table, own, parts):
@@ -353,7 +355,8 @@
     arrived = lax.all_to_all(packed, "wide", split_axis=0, concat_axis=0, tiled=True)
     scratch = (pltpu.VMEM((8 * N_WIDE, 128), jnp.float32), pltpu.VMEM((N_WIDE, 128), jnp.float32)) + (pltpu.VMEM((ROWS, 128), jnp.float32),) * 2
     mine = call(unpack_kernel, "unpack", f32(ROWS, WIDTH), arrived, scratch=scratch, scalars=0)
-    shards = (mine, shift(mine, "narrow", -1), shift(mine, "narrow", -2), shift(mine, "narrow", -3))
+    after, before = shift(mine, "narrow", -1), shift(mine, "narrow", -3)
+    shards = (mine, after, shift(mine, "narrow", -2), before)
 
     half = f32(ROWS, WIDTH)
     whole = f32(ROWS, CLASS_COLS)

time: 152 us -> 152 us (level)
  no operation moved by 1% of the time
where the time goes in v6:
time: 152 us; the launch traced here: 151 us
  waiting for transfers between devices  70.9 us (47%)
  starting transfers between devices  57.1 us (38%)
  Pallas kernels  15.3 us (10%)
  local copies, waits for them, and re-layouts  4.53 us (3%)
  other arithmetic  1.93 us (1%)
  between operations  1.58 us (1%)
    all_to_all x1, waiting for transfers between devices, local(): lax.all_to_all(packed, 'wide', split_axis=0, concat_axis=0, tiled=True)  32.2 us
    ppermute x9, waiting for transfers between devices, shift(): return lax.ppermute(x, axis, [(i, (i + by) % count) for i in range(count)])  30.1 us
    ppermute x9, starting transfers between devices, shift(): return lax.ppermute(x, axis, [(i, (i + by) % count) for i in range(count)])  28 us
    all_to_all x1, starting transfers between devices, local(): lax.all_to_all(packed, 'wide', split_axis=0, concat_axis=0, tiled=True)  19.9 us
    pallas_call x7, Pallas kernels, call(): pl.pallas_call(kernel, out_shape=outs, in_specs=[SMEM] * scalars + [VMEM]...  15.3 us
    ppermute x2, waiting for transfers between devices, halos(): lax.ppermute(cross, 'wide', over)  8.54 us
    ppermute x2, starting transfers between devices, halos(): lax.ppermute(inner, 'wide', [(i, i ^ 1) for i in range(count)])  5.09 us
    ppermute x2, starting transfers between devices, halos(): lax.ppermute(cross, 'wide', over)  4.18 us
  transfers between devices with their start and end apart: 14, of which 8 were waited for; matrix products, arithmetic and copies ran while one was open for 3% of the time, Pallas kernels for 4%

profile of v6, /device:TPU:24, one launch (start us, length us, event | category | flops | bytes accessed | tf_op | source)
XLA Modules:
  0.0 151.4 jit_solution(4111700071001802278)
XLA Ops:
  0.6 1.0 copy-done
  2.3 1.7 %pack.1 = f32[128,9,1,128]{3,2,1,0:T(1,128)} custom-call(s32[128]{0:T(128)S(1)} %copy-done.1, f32[512,256]{1,0:T(8,128)S(1)} %copy-done), custom_call_target="tpu_custom_call" | custom-call | bytes 1048576 | tf_op jit(solution)/shard_map/pack/pallas_call | solution.py:265
  4.1 19.9 %all-to-all-start = ((f32[128,9,1,128]{3,2,1,0:T(1,128)}), f32[128,9,1,128]{3,2,1,0:T(1,128)S(1)}, u32[]{:S(2)}, u32[]{:S(2)}) async-start(f32[128,9,1,128]{3,2,1,0:T(1,128)} %pack.1), calls=%async_computation | async-start | bytes 1179648 | tf_op jit(solution)/shard_map/all_to_all | solution.py:355
  24.0 0.8 constant_dynamic-slice_fusion.1
  27.9 32.2 %all-to-all-done.arrived_ref = f32[128,9,1,128]{3,2,1,0:T(1,128)S(1)} async-done(((f32[128,9,1,128]{3,2,1,0:T(1,128)}), f32[128,9,1,128]{3,2,1,0:T(1,128)S(1)}, u32[]{:S(2)}, u32[]{:S(2)}) %all-to-all-start) | async-done | bytes 589856 | tf_op jit(solution)/shard_map/all_to_all | solution.py:355
  60.1 0.7 unpack.1.s0
  60.7 2.1 %collective-permute-start.8 = (f32[512,256]{1,0:T(8,128)S(1)}, f32[512,256]{1,0:T(8,128)S(1)}, u32[]{:S(2)}, u32[]{:S(2)}) collective-permute-start(f32[512,256]{1,0:T(8,128)S(1)} %unpack.1.s0), channel_id=1, source_target_pairs={{0,1},{1,2},{2,3},{3,0},{4,5},{5,6},{6,7},{7,4},{8,9},{9,10},{10,1... | collective-permute-start | bytes 1572872 | tf_op jit(solution)/shard_map/ppermute | solution.py:260
  62.9 4.5 %collective-permute-start.7 = (f32[512,256]{1,0:T(8,128)S(1)}, f32[512,256]{1,0:T(8,128)S(1)}, u32[]{:S(2)}, u32[]{:S(2)}) collective-permute-start(f32[512,256]{1,0:T(8,128)S(1)} %unpack.1.s0), channel_id=1, source_target_pairs={{0,2},{1,3},{2,0},{3,1},{4,6},{5,7},{6,4},{7,5},{8,10},{9,11},{10,... | collective-permute-start | bytes 1572872 | tf_op jit(solution)/shard_map/ppermute | solution.py:260
  67.4 1.9 %collective-permute-start.6 = (f32[512,256]{1,0:T(8,128)S(1)}, f32[512,256]{1,0:T(8,128)S(1)}, u32[]{:S(2)}, u32[]{:S(2)}) collective-permute-start(f32[512,256]{1,0:T(8,128)S(1)} %unpack.1.s0), channel_id=1, source_target_pairs={{0,3},{1,0},{2,1},{3,2},{4,7},{5,4},{6,5},{7,6},{8,11},{9,8},{10,9... | collective-permute-start | bytes 1572872 | tf_op jit(solution)/shard_map/ppermute | solution.py:260
  69.3 0.7 select_reduce_fusion.2
  71.0 6.5 %collective-permute-done.8.s3 = f32[512,256]{1,0:T(8,128)S(1)} collective-permute-done((f32[512,256]{1,0:T(8,128)S(1)}, f32[512,256]{1,0:T(8,128)S(1)}, u32[]{:S(2)}, u32[]{:S(2)}) %collective-permute-start.8) | collective-permute-done | bytes 524320 | tf_op jit(solution)/shard_map/ppermute | solution.py:260
  77.5 3.7 %collective-permute-done.7.s2 = f32[512,256]{1,0:T(8,128)S(1)} collective-permute-done((f32[512,256]{1,0:T(8,128)S(1)}, f32[512,256]{1,0:T(8,128)S(1)}, u32[]{:S(2)}, u32[]{:S(2)}) %collective-permute-start.7) | collective-permute-done | bytes 524320 | tf_op jit(solution)/shard_map/ppermute | solution.py:260
  81.2 9.1 %collective-permute-done.6.s1 = f32[512,256]{1,0:T(8,128)S(1)} collective-permute-done((f32[512,256]{1,0:T(8,128)S(1)}, f32[512,256]{1,0:T(8,128)S(1)}, u32[]{:S(2)}, u32[]{:S(2)}) %collective-permute-start.6) | collective-permute-done | bytes 524320 | tf_op jit(solution)/shard_map/ppermute | solution.py:260
  90.3 1.2 columns_of_class.1
  91.6 2.1 %collective-permute-start.9 = (f32[512,256]{1,0:T(8,128)S(1)}, f32[512,256]{1,0:T(8,128)S(1)}, u32[]{:S(2)}, u32[]{:S(2)}) collective-permute-start(f32[512,256]{1,0:T(8,128)S(1)} %get-tuple-element.60), channel_id=1, source_target_pairs={{0,508},{4,8},{8,4},{12,16},{16,12},{20,24},{24,20},{28,32},{32,28... | collective-permute-start | bytes 1572872 | tf_op jit(solution)/shard_map/ppermute | solution.py:310
  93.7 3.2 %collective-permute-start.10 = (f32[512,256]{1,0:T(8,128)S(1)}, f32[512,256]{1,0:T(8,128)S(1)}, u32[]{:S(2)}, u32[]{:S(2)}) collective-permute-start(f32[512,256]{1,0:T(8,128)S(1)} %get-tuple-element.61), channel_id=1, source_target_pairs={{0,4},{4,0},{8,12},{12,8},{16,20},{20,16},{24,28},{28,24},{32,36},... | collective-permute-start | bytes 1572872 | tf_op jit(solution)/shard_map/ppermute | solution.py:310
  96.9 8.5 %collective-permute-done.9.cross = f32[512,256]{1,0:T(8,128)S(1)} collective-permute-done((f32[512,256]{1,0:T(8,128)S(1)}, f32[512,256]{1,0:T(8,128)S(1)}, u32[]{:S(2)}, u32[]{:S(2)}) %collective-permute-start.9) | collective-permute-done | bytes 524320 | tf_op jit(solution)/shard_map/ppermute | solution.py:310
  105.4 4.1 %square.1 = (f32[512,384]{1,0:T(8,128)S(1)}, f32[512,256]{1,0:T(8,128)S(1)}, f32[512,256]{1,0:T(8,128)S(1)}, f32[1024,128]{1,0:T(8,128)S(1)}, f32[576,128]{1,0:T...) custom-call(s32[417]{0:T(512)S(1)} %concatenate.11.table_ref, f32[512,256]{1,0:T(8,128)S(1)} %unpack.1.s0, ...), custom_call_target="tpu_custom_call" | custom-call | flops 1207959552 | bytes 8388608 | tf_op jit(solution)/shard_map/square/pallas_call | solution.py:265
  109.5 2.1 %collective-permute-start.14 = (f32[512,256]{1,0:T(8,128)S(1)}, f32[512,256]{1,0:T(8,128)S(1)}, u32[]{:S(2)}, u32[]{:S(2)}) collective-permute-start(f32[512,256]{1,0:T(8,128)S(1)} %get-tuple-element.67), channel_id=1, source_target_pairs={{0,508},{4,8},{8,4},{12,16},{16,12},{20,24},{24,20},{28,32},{32,28... | collective-permute-start | bytes 1572872 | tf_op jit(solution)/shard_map/ppermute | solution.py:310
  111.6 1.9 %collective-permute-start.15 = (f32[512,256]{1,0:T(8,128)S(1)}, f32[512,256]{1,0:T(8,128)S(1)}, u32[]{:S(2)}, u32[]{:S(2)}) collective-permute-start(f32[512,256]{1,0:T(8,128)S(1)} %get-tuple-element.68), channel_id=1, source_target_pairs={{0,4},{4,0},{8,12},{12,8},{16,20},{20,16},{24,28},{28,24},{32,36},... | collective-permute-start | bytes 1572872 | tf_op jit(solution)/shard_map/ppermute | solution.py:310
  113.5 2.3 %collective-permute-start.11 = (f32[576,128]{1,0:T(8,128)S(1)}, f32[576,128]{1,0:T(8,128)S(1)}, u32[]{:S(2)}, u32[]{:S(2)}) collective-permute-start(f32[576,128]{1,0:T(8,128)S(1)} %get-tuple-element.63), channel_id=1, source_target_pairs={{0,1},{1,2},{2,3},{3,0},{4,5},{5,6},{6,7},{7,4},{8,9},{9,10},{10,1... | collective-permute-start | bytes 884744 | tf_op jit(solution)/shard_map/ppermute | solution.py:260
  115.9 4.4 %collective-permute-start.12 = (f32[576,128]{1,0:T(8,128)S(1)}, f32[576,128]{1,0:T(8,128)S(1)}, u32[]{:S(2)}, u32[]{:S(2)}) collective-permute-start(f32[576,128]{1,0:T(8,128)S(1)} %get-tuple-element.64), channel_id=1, source_target_pairs={{0,2},{1,3},{2,0},{3,1},{4,6},{5,7},{6,4},{7,5},{8,10},{9,11},{10,... | collective-permute-start | bytes 884744 | tf_op jit(solution)/shard_map/ppermute | solution.py:260
  120.3 3.1 %collective-permute-start.13 = (f32[576,128]{1,0:T(8,128)S(1)}, f32[576,128]{1,0:T(8,128)S(1)}, u32[]{:S(2)}, u32[]{:S(2)}) collective-permute-start(f32[576,128]{1,0:T(8,128)S(1)} %get-tuple-element.65), channel_id=1, source_target_pairs={{0,3},{1,0},{2,1},{3,2},{4,7},{5,4},{6,5},{7,6},{8,11},{9,8},{10,9... | collective-permute-start | bytes 884744 | tf_op jit(solution)/shard_map/ppermute | solution.py:260
  123.4 4.0 %cubic.1 = (f32[512,384]{1,0:T(8,128)S(1)}, f32[1024,128]{1,0:T(8,128)S(1)}, f32[576,128]{1,0:T(8,128)S(1)}, f32[576,128]{1,0:T(8,128)S(1)}, f32[576,128]{1,0:T(8,128)S(1)}) custom-call(s32[417]{0:T(512)S(1)} %concatenate.11.table_ref, f32[512,256]{1,0:T(8,128)S(1)} %unpack.1.s0, f32[512,256]{1,0:T(8,128)S(1)} %collective-permute-done.6.s1, ...), custom_call_target="tpu_custom_call" | custom-call | flops 1207959552 | bytes 8388608 | tf_op jit(solution)/shard_map/cubic/pallas_call | solution.py:265
  127.5 4.1 %collective-permute-start.16 = (f32[576,128]{1,0:T(8,128)S(1)}, f32[576,128]{1,0:T(8,128)S(1)}, u32[]{:S(2)}, u32[]{:S(2)}) collective-permute-start(f32[576,128]{1,0:T(8,128)S(1)} %get-tuple-element.70), channel_id=1, source_target_pairs={{0,1},{1,2},{2,3},{3,0},{4,5},{5,6},{6,7},{7,4},{8,9},{9,10},{10,1... | collective-permute-start | bytes 884744 | tf_op jit(solution)/shard_map/ppermute | solution.py:260
  131.6 2.7 %collective-permute-start.17 = (f32[576,128]{1,0:T(8,128)S(1)}, f32[576,128]{1,0:T(8,128)S(1)}, u32[]{:S(2)}, u32[]{:S(2)}) collective-permute-start(f32[576,128]{1,0:T(8,128)S(1)} %get-tuple-element.71), channel_id=1, source_target_pairs={{0,2},{1,3},{2,0},{3,1},{4,6},{5,7},{6,4},{7,5},{8,10},{9,11},{10,... | collective-permute-start | bytes 884744 | tf_op jit(solution)/shard_map/ppermute | solution.py:260
  134.3 2.7 %collective-permute-start.18 = (f32[576,128]{1,0:T(8,128)S(1)}, f32[576,128]{1,0:T(8,128)S(1)}, u32[]{:S(2)}, u32[]{:S(2)}) collective-permute-start(f32[576,128]{1,0:T(8,128)S(1)} %get-tuple-element.72), channel_id=1, source_target_pairs={{0,3},{1,0},{2,1},{3,2},{4,7},{5,4},{6,5},{7,6},{8,11},{9,8},{10,9... | collective-permute-start | bytes 884744 | tf_op jit(solution)/shard_map/ppermute | solution.py:260
  137.1 1.8 %place_blocks.2 = f32[512,256]{1,0:T(8,128)} custom-call(s32[417]{0:T(512)S(1)} %concatenate.11.table_ref, f32[1024,128]{1,0:T(8,128)S(1)} %get-tuple-element.62.p0, f32[576,128]{1,0:T(8,128)S(1)} %collective-permute-done.11.p1, f32[576,128]{1,0:T(8,128)S(1)} %collective-permute-done.12.p2, f32[576,128]{1,0:T(8,128)S(1)} %collective-permute-done.13.p3), custom_call_target="tpu_custom_call" | custom-call | bytes 1048576 | tf_op jit(solution)/shard_map/place_blocks/pallas_call | solution.py:265
  138.9 5.2 %collective-permute-done.16.p1 = f32[576,128]{1,0:T(8,128)S(1)} collective-permute-done((f32[576,128]{1,0:T(8,128)S(1)}, f32[576,128]{1,0:T(8,128)S(1)}, u32[]{:S(2)}, u32[]{:S(2)}) %collective-permute-start.16) | collective-permute-done | bytes 294944 | tf_op jit(solution)/shard_map/ppermute | solution.py:260
  144.0 1.0 collective-permute-done.17.p2
  145.0 4.6 %collective-permute-done.18.p3 = f32[576,128]{1,0:T(8,128)S(1)} collective-permute-done((f32[576,128]{1,0:T(8,128)S(1)}, f32[576,128]{1,0:T(8,128)S(1)}, u32[]{:S(2)}, u32[]{:S(2)}) %collective-permute-start.18) | collective-permute-done | bytes 294944 | tf_op jit(solution)/shard_map/ppermute | solution.py:260
  149.6 1.8 %place_blocks.3 = f32[512,256]{1,0:T(8,128)} custom-call(s32[417]{0:T(512)S(1)} %concatenate.11.table_ref, f32[1024,128]{1,0:T(8,128)S(1)} %get-tuple-element.69.p0, f32[576,128]{1,0:T(8,128)S(1)} %collective-permute-done.16.p1, f32[576,128]{1,0:T(8,128)S(1)} %collective-permute-done.17.p2, f32[576,128]{1,0:T(8,128)S(1)} %collective-permute-done.18.p3), custom_call_target="tpu_custom_call" | custom-call | bytes 1048576 | tf_op jit(solution)/shard_map/place_blocks/pallas_call | solution.py:265
  (51 shorter events, 4.0 us)
Async XLA Ops:
  0.6 1.0 copy-start
  1.7 0.7 copy-start.1
  4.1 19.9 %copy-start.5 = (s32[1024,16]{0,1:T(8,128)S(1)}, s32[1024,16]{0,1:T(8,128)}, u32[]{:S(2)}) copy-start(s32[1024,16]{0,1:T(8,128)} %param.9) | copy-start | bytes 196612
  4.1 56.0 %all-to-all-start = ((f32[128,9,1,128]{3,2,1,0:T(1,128)}), f32[128,9,1,128]{3,2,1,0:T(1,128)S(1)}, u32[]{:S(2)}, u32[]{:S(2)}) async-start(f32[128,9,1,128]{3,2,1,0:T(1,128)} %pack.1), calls=%async_computation | async-start | bytes 1179648 | tf_op jit(solution)/shard_map/all_to_all | solution.py:355
  60.7 16.8 %collective-permute-start.8 = (f32[512,256]{1,0:T(8,128)S(1)}, f32[512,256]{1,0:T(8,128)S(1)}, u32[]{:S(2)}, u32[]{:S(2)}) collective-permute-start(f32[512,256]{1,0:T(8,128)S(1)} %unpack.1.s0), channel_id=1, source_target_pairs={{0,1},{1,2},{2,3},{3,0},{4,5},{5,6},{6,7},{7,4},{8,9},{9,10},{10,1... | collective-permute-start | bytes 1572872 | tf_op jit(solution)/shard_map/ppermute | solution.py:260
  62.9 18.3 %collective-permute-start.7 = (f32[512,256]{1,0:T(8,128)S(1)}, f32[512,256]{1,0:T(8,128)S(1)}, u32[]{:S(2)}, u32[]{:S(2)}) collective-permute-start(f32[512,256]{1,0:T(8,128)S(1)} %unpack.1.s0), channel_id=1, source_target_pairs={{0,2},{1,3},{2,0},{3,1},{4,6},{5,7},{6,4},{7,5},{8,10},{9,11},{10,... | collective-permute-start | bytes 1572872 | tf_op jit(solution)/shard_map/ppermute | solution.py:260
  67.4 23.0 %collective-permute-start.6 = (f32[512,256]{1,0:T(8,128)S(1)}, f32[512,256]{1,0:T(8,128)S(1)}, u32[]{:S(2)}, u32[]{:S(2)}) collective-permute-start(f32[512,256]{1,0:T(8,128)S(1)} %unpack.1.s0), channel_id=1, source_target_pairs={{0,3},{1,0},{2,1},{3,2},{4,7},{5,4},{6,5},{7,6},{8,11},{9,8},{10,9... | collective-permute-start | bytes 1572872 | tf_op jit(solution)/shard_map/ppermute | solution.py:260
  91.6 13.8 %collective-permute-start.9 = (f32[512,256]{1,0:T(8,128)S(1)}, f32[512,256]{1,0:T(8,128)S(1)}, u32[]{:S(2)}, u32[]{:S(2)}) collective-permute-start(f32[512,256]{1,0:T(8,128)S(1)} %get-tuple-element.60), channel_id=1, source_target_pairs={{0,508},{4,8},{8,4},{12,16},{16,12},{20,24},{24,20},{28,32},{32,28... | collective-permute-start | bytes 1572872 | tf_op jit(solution)/shard_map/ppermute | solution.py:310
  93.7 11.7 %collective-permute-start.10 = (f32[512,256]{1,0:T(8,128)S(1)}, f32[512,256]{1,0:T(8,128)S(1)}, u32[]{:S(2)}, u32[]{:S(2)}) collective-permute-start(f32[512,256]{1,0:T(8,128)S(1)} %get-tuple-element.61), channel_id=1, source_target_pairs={{0,4},{4,0},{8,12},{12,8},{16,20},{20,16},{24,28},{28,24},{32,36},... | collective-permute-start | bytes 1572872 | tf_op jit(solution)/shard_map/ppermute | solution.py:310
  109.5 13.9 %collective-permute-start.14 = (f32[512,256]{1,0:T(8,128)S(1)}, f32[512,256]{1,0:T(8,128)S(1)}, u32[]{:S(2)}, u32[]{:S(2)}) collective-permute-start(f32[512,256]{1,0:T(8,128)S(1)} %get-tuple-element.67), channel_id=1, source_target_pairs={{0,508},{4,8},{8,4},{12,16},{16,12},{20,24},{24,20},{28,32},{32,28... | collective-permute-start | bytes 1572872 | tf_op jit(solution)/shard_map/ppermute | solution.py:310
  111.6 11.8 %collective-permute-start.15 = (f32[512,256]{1,0:T(8,128)S(1)}, f32[512,256]{1,0:T(8,128)S(1)}, u32[]{:S(2)}, u32[]{:S(2)}) collective-permute-start(f32[512,256]{1,0:T(8,128)S(1)} %get-tuple-element.68), channel_id=1, source_target_pairs={{0,4},{4,0},{8,12},{12,8},{16,20},{20,16},{24,28},{28,24},{32,36},... | collective-permute-start | bytes 1572872 | tf_op jit(solution)/shard_map/ppermute | solution.py:310
  113.5 20.8 %collective-permute-start.11 = (f32[576,128]{1,0:T(8,128)S(1)}, f32[576,128]{1,0:T(8,128)S(1)}, u32[]{:S(2)}, u32[]{:S(2)}) collective-permute-start(f32[576,128]{1,0:T(8,128)S(1)} %get-tuple-element.63), channel_id=1, source_target_pairs={{0,1},{1,2},{2,3},{3,0},{4,5},{5,6},{6,7},{7,4},{8,9},{9,10},{10,1... | collective-permute-start | bytes 884744 | tf_op jit(solution)/shard_map/ppermute | solution.py:260
  115.9 21.2 %collective-permute-start.12 = (f32[576,128]{1,0:T(8,128)S(1)}, f32[576,128]{1,0:T(8,128)S(1)}, u32[]{:S(2)}, u32[]{:S(2)}) collective-permute-start(f32[576,128]{1,0:T(8,128)S(1)} %get-tuple-element.64), channel_id=1, source_target_pairs={{0,2},{1,3},{2,0},{3,1},{4,6},{5,7},{6,4},{7,5},{8,10},{9,11},{10,... | collective-permute-start | bytes 884744 | tf_op jit(solution)/shard_map/ppermute | solution.py:260
  120.3 16.8 %collective-permute-start.13 = (f32[576,128]{1,0:T(8,128)S(1)}, f32[576,128]{1,0:T(8,128)S(1)}, u32[]{:S(2)}, u32[]{:S(2)}) collective-permute-start(f32[576,128]{1,0:T(8,128)S(1)} %get-tuple-element.65), channel_id=1, source_target_pairs={{0,3},{1,0},{2,1},{3,2},{4,7},{5,4},{6,5},{7,6},{8,11},{9,8},{10,9... | collective-permute-start | bytes 884744 | tf_op jit(solution)/shard_map/ppermute | solution.py:260
  127.5 16.6 %collective-permute-start.16 = (f32[576,128]{1,0:T(8,128)S(1)}, f32[576,128]{1,0:T(8,128)S(1)}, u32[]{:S(2)}, u32[]{:S(2)}) collective-permute-start(f32[576,128]{1,0:T(8,128)S(1)} %get-tuple-element.70), channel_id=1, source_target_pairs={{0,1},{1,2},{2,3},{3,0},{4,5},{5,6},{6,7},{7,4},{8,9},{9,10},{10,1... | collective-permute-start | bytes 884744 | tf_op jit(solution)/shard_map/ppermute | solution.py:260
  131.6 13.4 %collective-permute-start.17 = (f32[576,128]{1,0:T(8,128)S(1)}, f32[576,128]{1,0:T(8,128)S(1)}, u32[]{:S(2)}, u32[]{:S(2)}) collective-permute-start(f32[576,128]{1,0:T(8,128)S(1)} %get-tuple-element.71), channel_id=1, source_target_pairs={{0,2},{1,3},{2,0},{3,1},{4,6},{5,7},{6,4},{7,5},{8,10},{9,11},{10,... | collective-permute-start | bytes 884744 | tf_op jit(solution)/shard_map/ppermute | solution.py:260
  134.3 15.3 %collective-permute-start.18 = (f32[576,128]{1,0:T(8,128)S(1)}, f32[576,128]{1,0:T(8,128)S(1)}, u32[]{:S(2)}, u32[]{:S(2)}) collective-permute-start(f32[576,128]{1,0:T(8,128)S(1)} %get-tuple-element.72), channel_id=1, source_target_pairs={{0,3},{1,0},{2,1},{3,2},{4,7},{5,4},{6,5},{7,6},{8,11},{9,8},{10,9... | collective-permute-start | bytes 884744 | tf_op jit(solution)/shard_map/ppermute | solution.py:260
